TPU v7x, 128 devices: a whole 4x4x4 slice. The times are simulated.
128 devices in a mesh: gx: 4 (over x_lo, core), gy: 4 (over y), gz: 8 (over x_hi, z).
Axes of the slice: x: 4 (x_hi: 2, x_lo: 2; x = x_hi * 2 + x_lo), y: 4, z: 4, core: 2. Of those that a mesh axis runs over, the one named last changes fastest.
Arguments:
- sources: bfloat16 [16, 4194304], P(None, ('gx', 'gy', 'gz')), may hold values from -6 to 6
- in_slot: int32 [16384], P(('gx', 'gy', 'gz')), may hold values from 0 to 127, as said below
- interp: bfloat16 [16384, 64, 256], P(('gx', 'gy', 'gz')), may hold values from -0.375 to 0.375
- translate: bfloat16 [7, 16384, 64, 128], P(None, ('gx', 'gy', 'gz')), may hold values from -0.5 to 0.5
- evaluate: bfloat16 [16384, 64, 256], P(('gx', 'gy', 'gz')), may hold values from -0.75 to 0.75
- owner_slot: int32 [16384], P(('gx', 'gy', 'gz')), may hold values from 0 to 127, as said below
Outputs:
- targets: bfloat16 [16, 4194304], P(None, ('gx', 'gy', 'gz'))
Inputs may be any that keep to these rules, and one draw needn't show every extreme that they name: `in_slot`: each aligned block of 128 entries is a permutation of 0 to 127. `owner_slot`: each aligned block of 128 entries is a permutation of 0 to 127.
All inputs are finite; a program needn't handle non-finite values.
Results may differ from a plain program's by a relative error of at most 0.015.
Values may be sent and summed in bfloat16 or wider, within the bound.
No kernel may reach another device: no remote copies, remote signals or barrier semaphores. Data moves between devices by JAX's collectives and lax.ppermute only.
A program may use at most 128 MiB of HBM per device.

v0:
```python
import jax
import jax.numpy as jnp
from jax import lax
from jax.sharding import PartitionSpec as P


def from_partner(value, axis, distance):
    mask = 2**distance
    pairs = [(source, source ^ mask) for source in range(lax.axis_size(axis))]
    return lax.ppermute(value, axis, pairs)


def level_step(coeffs, tables, partner):
    rank_k = coeffs.shape[1]
    own_part = jnp.einsum(
        "bkj,bjr->bkr", tables[:, :, :rank_k], coeffs, preferred_element_type=jnp.float32
    )
    far_part = jnp.einsum(
        "bkj,bjr->bkr", tables[:, :, rank_k:], partner, preferred_element_type=jnp.float32
    )
    return (own_part + far_part).astype(jnp.bfloat16)


def local(sources, in_slot, interp, translate, evaluate, owner_slot):
    box_count, rank_k, span_s = interp.shape
    rhs_count = sources.shape[0]
    spread = sources.reshape(rhs_count, box_count, span_s)
    chosen = jnp.take(spread, in_slot, axis=1)
    coeffs = jnp.einsum("bks,rbs->bkr", interp, chosen, preferred_element_type=jnp.float32).astype(
        jnp.bfloat16
    )
    level_no = 0
    for bit_pos in range(lax.axis_size("gz").bit_length() - 1):
        flat = coeffs.reshape(box_count, rank_k * rhs_count)
        partner = from_partner(flat, "gz", bit_pos).reshape(box_count, rank_k, rhs_count)
        coeffs = level_step(coeffs, translate[level_no], partner)
        level_no = level_no + 1
    for bit_pos in range(lax.axis_size("gy").bit_length() - 1):
        flat = coeffs.reshape(box_count, rank_k * rhs_count)
        partner = from_partner(flat, "gy", bit_pos).reshape(box_count, rank_k, rhs_count)
        coeffs = level_step(coeffs, translate[level_no], partner)
        level_no = level_no + 1
    for bit_pos in range(lax.axis_size("gx").bit_length() - 1):
        flat = coeffs.reshape(box_count, rank_k * rhs_count)
        partner = from_partner(flat, "gx", bit_pos).reshape(box_count, rank_k, rhs_count)
        coeffs = level_step(coeffs, translate[level_no], partner)
        level_no = level_no + 1
    values = jnp.einsum(
        "bks,bkr->rbs", evaluate, coeffs, preferred_element_type=jnp.float32
    ).astype(jnp.bfloat16)
    size_x = lax.axis_size("gx")
    size_yz = lax.axis_size("gy") * lax.axis_size("gz")
    blocks = size_x * size_yz
    per_peer = box_count // blocks
    shaped = values.reshape(rhs_count, per_peer, blocks, span_s)
    moved = lax.all_to_all(shaped, ("gx", "gy", "gz"), split_axis=2, concat_axis=2, tiled=True)
    arranged = jnp.transpose(moved, (0, 2, 1, 3)).reshape(rhs_count, box_count, span_s)
    placed = jnp.take(arranged, owner_slot, axis=1)
    return placed.reshape(rhs_count, box_count * span_s)


def solution(mesh):
    placed = (
        P(None, ("gx", "gy", "gz")),
        P(("gx", "gy", "gz")),
        P(("gx", "gy", "gz"), None, None),
        P(None, ("gx", "gy", "gz"), None, None),
        P(("gx", "gy", "gz"), None, None),
        P(("gx", "gy", "gz")),
    )
    return jax.shard_map(
        local, mesh=mesh, in_specs=placed, out_specs=P(None, ("gx", "gy", "gz")), check_vma=False
    )
```

profile of v0, /device:TPU:1, one launch (start us, length us, event | category | flops | bytes accessed | tf_op | source)
XLA Modules:
  0.0 127.8 jit_solution(49475900685241755)
XLA Ops:
  0.0 0.7 compare_select_fusion.1
  0.7 0.7 compare_and_fusion.1
  1.3 1.3 %copy.57 = bf16[2,128,8,256]{3,2,0,1:T(8,128)(2,1)S(1)} copy(bf16[2,128,8,256]{3,2,1,0:T(8,128)(2,1)} %bitcast.78) | data formatting | bytes 2097152 | tf_op jit(solution)/shard_map/reshape | solution.py:27
  2.6 0.6 gather_fusion
  3.3 3.4 %convolution_convert_fusion.1 = bf16[128,16,64]{2,1,0:T(8,128)(2,1)S(1)} fusion(bf16[128,64,256]{2,1,0:T(8,128)(2,1)} %param.10, bf16[128,16,256]{2,1,0:T(8,128)(2,1)S(1)} %gather_fusion, pred[128]{0:T(512)(128)(4,1)S(1)} %compare_and_fusion.1), kind=kOutput, calls=%fused_computation.46 | convolution fusion | flops 67764224 | bytes 5505152 | tf_op jit(solution)/shard_map/bks,rbs->bkr/dot_general | solution.py:29
  6.7 0.6 copy.38
  7.3 2.5 %collective-permute-start = (bf16[128,1024]{0,1:T(8,128)(2,1)S(1)}, bf16[128,1024]{0,1:T(8,128)(2,1)S(1)}, u32[]{:S(2)}, u32[]{:S(2)}) collective-permute-start(bf16[128,1024]{0,1:T(8,128)(2,1)S(1)} %bitcast.80), channel_id=1, source_target_pairs={{0,1},{1,0},{2,3},{3,2},{4,5},{5,4},{6,7},{7,6},{8,9},{9,8},{10,11... | collective-permute-start | bytes 786440 | tf_op jit(solution)/shard_map/ppermute | solution.py:10
  9.9 10.0 %slice_bitcast_fusion = (bf16[128,64,128]{2,1,0:T(8,128)(2,1)}, bf16[128,64,128]{2,1,0:T(8,128)(2,1)}, bf16[128,64,128]{2,1,0:T(8,128)(2,1)}, bf16[128,64,128]{2...) fusion(bf16[7,128,64,128]{3,2,1,0:T(8,128)(2,1)} %param.11), kind=kLoop, calls=%fused_computation.30 | loop fusion | bytes 29360128 | tf_op jit(solution)/shard_map/squeeze | solution.py:46
  19.9 2.2 %fusion.26 = f32[128,16,64]{2,1,0:T(8,128)} fusion(bf16[128,16,64]{2,1,0:T(8,128)(2,1)S(1)} %convolution_convert_fusion.1, bf16[128,64,128]{2,1,0:T(8,128)(2,1)S(1)} %get-tuple-element.11), kind=kOutput, calls=%fused_computation.28 | convolution fusion | flops 16777216 | bytes 2883584 | tf_op jit(solution)/shard_map/bkj,bjr->bkr/dot_general | solution.py:15
  22.1 0.5 copy.39
  22.7 3.1 %fusion.68 = bf16[128,16,64]{2,1,0:T(8,128)(2,1)S(1)} fusion(f32[128,16,64]{2,1,0:T(8,128)} %fusion.26, bf16[128,64,16]{1,2,0:T(8,128)(2,1)S(1)} %copy.39, bf16[128,64,128]{2,1,0:T(8,128)(2,1)} %copy-done.1), kind=kOutput, calls=%fused_computation.53 | convolution fusion | flops 17039360 | bytes 3145728 | tf_op jit(solution)/shard_map/bkj,bjr->bkr/dot_general | solution.py:18
  25.8 0.6 copy.40
  26.4 3.4 %collective-permute-start.1 = (bf16[128,1024]{0,1:T(8,128)(2,1)S(1)}, bf16[128,1024]{0,1:T(8,128)(2,1)S(1)}, u32[]{:S(2)}, u32[]{:S(2)}) collective-permute-start(bf16[128,1024]{0,1:T(8,128)(2,1)S(1)} %bitcast.88), channel_id=1, source_target_pairs={{0,2},{1,3},{2,0},{3,1},{4,6},{5,7},{6,4},{7,5},{8,10},{9,11},{10,... | collective-permute-start | bytes 786440 | tf_op jit(solution)/shard_map/ppermute | solution.py:10
  29.8 2.8 %fusion.22 = f32[128,16,64]{2,1,0:T(8,128)S(1)} fusion(bf16[128,16,64]{2,1,0:T(8,128)(2,1)S(1)} %fusion.68, bf16[128,64,128]{2,1,0:T(8,128)(2,1)} %get-tuple-element.10), kind=kOutput, calls=%fused_computation.24 | convolution fusion | flops 16777216 | bytes 2883584 | tf_op jit(solution)/shard_map/bkj,bjr->bkr/dot_general | solution.py:15
  32.5 2.9 %collective-permute-done.1 = bf16[128,1024]{0,1:T(8,128)(2,1)S(1)} collective-permute-done((bf16[128,1024]{0,1:T(8,128)(2,1)S(1)}, bf16[128,1024]{0,1:T(8,128)(2,1)S(1)}, u32[]{:S(2)}, u32[]{:S(2)}) %collective-permute-start.1) | collective-permute-done | bytes 262176 | tf_op jit(solution)/shard_map/ppermute | solution.py:10
  35.5 0.5 copy.41
  36.0 2.9 %fusion.65 = bf16[128,16,64]{2,1,0:T(8,128)(2,1)S(1)} fusion(f32[128,16,64]{2,1,0:T(8,128)S(1)} %fusion.22, bf16[128,64,16]{1,2,0:T(8,128)(2,1)S(1)} %copy.41, bf16[128,64,128]{2,1,0:T(8,128)(2,1)} %get-tuple-element.10), kind=kOutput, calls=%fused_computation.52 | convolution fusion | flops 17039360 | bytes 3145728 | tf_op jit(solution)/shard_map/bkj,bjr->bkr/dot_general | solution.py:18
  38.9 0.6 copy.42
  39.5 3.0 %collective-permute-start.2 = (bf16[128,1024]{0,1:T(8,128)(2,1)S(1)}, bf16[128,1024]{0,1:T(8,128)(2,1)S(1)}, u32[]{:S(2)}, u32[]{:S(2)}) collective-permute-start(bf16[128,1024]{0,1:T(8,128)(2,1)S(1)} %bitcast.89), channel_id=1, source_target_pairs={{0,4},{1,5},{2,6},{3,7},{4,0},{5,1},{6,2},{7,3},{8,12},{9,13},{10,... | collective-permute-start | bytes 786440 | tf_op jit(solution)/shard_map/ppermute | solution.py:10
  42.5 2.8 %fusion.18 = f32[128,16,64]{2,1,0:T(8,128)S(1)} fusion(bf16[128,16,64]{2,1,0:T(8,128)(2,1)S(1)} %fusion.65, bf16[128,64,128]{2,1,0:T(8,128)(2,1)} %get-tuple-element.9), kind=kOutput, calls=%fused_computation.20 | convolution fusion | flops 16777216 | bytes 2883584 | tf_op jit(solution)/shard_map/bkj,bjr->bkr/dot_general | solution.py:15
  45.2 2.2 %collective-permute-done.2 = bf16[128,1024]{0,1:T(8,128)(2,1)S(1)} collective-permute-done((bf16[128,1024]{0,1:T(8,128)(2,1)S(1)}, bf16[128,1024]{0,1:T(8,128)(2,1)S(1)}, u32[]{:S(2)}, u32[]{:S(2)}) %collective-permute-start.2) | collective-permute-done | bytes 262176 | tf_op jit(solution)/shard_map/ppermute | solution.py:10
  47.5 0.5 copy.43
  48.0 2.9 %fusion.62 = bf16[128,16,64]{2,1,0:T(8,128)(2,1)S(1)} fusion(f32[128,16,64]{2,1,0:T(8,128)S(1)} %fusion.18, bf16[128,64,16]{1,2,0:T(8,128)(2,1)S(1)} %copy.43, bf16[128,64,128]{2,1,0:T(8,128)(2,1)} %get-tuple-element.9), kind=kOutput, calls=%fused_computation.51 | convolution fusion | flops 17039360 | bytes 3145728 | tf_op jit(solution)/shard_map/bkj,bjr->bkr/dot_general | solution.py:18
  50.9 0.6 copy.44
  51.5 1.4 %collective-permute-start.3 = (bf16[128,1024]{0,1:T(8,128)(2,1)S(1)}, bf16[128,1024]{0,1:T(8,128)(2,1)S(1)}, u32[]{:S(2)}, u32[]{:S(2)}) collective-permute-start(bf16[128,1024]{0,1:T(8,128)(2,1)S(1)} %bitcast.90), channel_id=1, source_target_pairs={{0,8},{8,0},{16,24},{24,16},{1,9},{9,1},{17,25},{25,17},{2,10},{10... | collective-permute-start | bytes 786440 | tf_op jit(solution)/shard_map/ppermute | solution.py:10
  52.9 2.8 %fusion.14 = f32[128,16,64]{2,1,0:T(8,128)S(1)} fusion(bf16[128,16,64]{2,1,0:T(8,128)(2,1)S(1)} %fusion.62, bf16[128,64,128]{2,1,0:T(8,128)(2,1)} %get-tuple-element.8), kind=kOutput, calls=%fused_computation.16 | convolution fusion | flops 16777216 | bytes 2883584 | tf_op jit(solution)/shard_map/bkj,bjr->bkr/dot_general | solution.py:15
  55.6 1.2 collective-permute-done.3
  56.8 0.5 copy.45
  57.3 2.9 %fusion.59 = bf16[128,16,64]{2,1,0:T(8,128)(2,1)S(1)} fusion(f32[128,16,64]{2,1,0:T(8,128)S(1)} %fusion.14, bf16[128,64,16]{1,2,0:T(8,128)(2,1)S(1)} %copy.45, bf16[128,64,128]{2,1,0:T(8,128)(2,1)} %get-tuple-element.8), kind=kOutput, calls=%fused_computation.50 | convolution fusion | flops 17039360 | bytes 3145728 | tf_op jit(solution)/shard_map/bkj,bjr->bkr/dot_general | solution.py:18
  60.2 0.6 copy.46
  60.8 3.0 %collective-permute-start.4 = (bf16[128,1024]{0,1:T(8,128)(2,1)S(1)}, bf16[128,1024]{0,1:T(8,128)(2,1)S(1)}, u32[]{:S(2)}, u32[]{:S(2)}) collective-permute-start(bf16[128,1024]{0,1:T(8,128)(2,1)S(1)} %bitcast.91), channel_id=1, source_target_pairs={{0,16},{8,24},{16,0},{24,8},{1,17},{9,25},{17,1},{25,9},{2,18},{10... | collective-permute-start | bytes 786440 | tf_op jit(solution)/shard_map/ppermute | solution.py:10
  63.8 2.8 %fusion.10 = f32[128,16,64]{2,1,0:T(8,128)S(1)} fusion(bf16[128,16,64]{2,1,0:T(8,128)(2,1)S(1)} %fusion.59, bf16[128,64,128]{2,1,0:T(8,128)(2,1)} %get-tuple-element.7), kind=kOutput, calls=%fused_computation.12 | convolution fusion | flops 16777216 | bytes 2883584 | tf_op jit(solution)/shard_map/bkj,bjr->bkr/dot_general | solution.py:15
  66.6 1.0 collective-permute-done.4
  68.1 2.9 %fusion.56 = bf16[128,16,64]{2,1,0:T(8,128)(2,1)S(1)} fusion(f32[128,16,64]{2,1,0:T(8,128)S(1)} %fusion.10, bf16[128,64,16]{1,2,0:T(8,128)(2,1)S(1)} %copy.47, bf16[128,64,128]{2,1,0:T(8,128)(2,1)} %get-tuple-element.7), kind=kOutput, calls=%fused_computation.49 | convolution fusion | flops 17039360 | bytes 3145728 | tf_op jit(solution)/shard_map/bkj,bjr->bkr/dot_general | solution.py:18
  71.0 0.6 copy.48
  71.6 4.8 %collective-permute-start.5 = (bf16[128,1024]{0,1:T(8,128)(2,1)S(1)}, bf16[128,1024]{0,1:T(8,128)(2,1)S(1)}, u32[]{:S(2)}, u32[]{:S(2)}) collective-permute-start(bf16[128,1024]{0,1:T(8,128)(2,1)S(1)} %bitcast.92), channel_id=1, source_target_pairs={{0,32},{32,0},{64,96},{96,64},{1,33},{33,1},{65,97},{97,65},{2,34}... | collective-permute-start | bytes 786440 | tf_op jit(solution)/shard_map/ppermute | solution.py:10
  76.4 2.8 %fusion.6 = f32[128,16,64]{2,1,0:T(8,128)S(1)} fusion(bf16[128,16,64]{2,1,0:T(8,128)(2,1)S(1)} %fusion.56, bf16[128,64,128]{2,1,0:T(8,128)(2,1)} %get-tuple-element.12), kind=kOutput, calls=%fused_computation.8 | convolution fusion | flops 16777216 | bytes 2883584 | tf_op jit(solution)/shard_map/bkj,bjr->bkr/dot_general | solution.py:15
  79.2 0.6 copy.49
  79.8 2.9 %fusion.53 = bf16[128,16,64]{2,1,0:T(8,128)(2,1)S(1)} fusion(f32[128,16,64]{2,1,0:T(8,128)S(1)} %fusion.6, bf16[128,64,16]{1,2,0:T(8,128)(2,1)S(1)} %copy.49, bf16[128,64,128]{2,1,0:T(8,128)(2,1)} %get-tuple-element.12), kind=kOutput, calls=%fused_computation.48 | convolution fusion | flops 17039360 | bytes 3145728 | tf_op jit(solution)/shard_map/bkj,bjr->bkr/dot_general | solution.py:18
  82.6 0.6 copy.50
  83.2 1.5 %collective-permute-start.6 = (bf16[128,1024]{0,1:T(8,128)(2,1)S(1)}, bf16[128,1024]{0,1:T(8,128)(2,1)S(1)}, u32[]{:S(2)}, u32[]{:S(2)}) collective-permute-start(bf16[128,1024]{0,1:T(8,128)(2,1)S(1)} %bitcast.87), channel_id=1, source_target_pairs={{0,64},{32,96},{64,0},{96,32},{1,65},{33,97},{65,1},{97,33},{2,66}... | collective-permute-start | bytes 786440 | tf_op jit(solution)/shard_map/ppermute | solution.py:10
  84.7 3.9 %fusion.2 = f32[128,16,64]{2,1,0:T(8,128)} fusion(bf16[128,16,64]{2,1,0:T(8,128)(2,1)S(1)} %fusion.53, bf16[128,64,128]{2,1,0:T(8,128)(2,1)} %get-tuple-element.6), kind=kOutput, calls=%fused_computation.4 | convolution fusion | flops 16777216 | bytes 2883584 | tf_op jit(solution)/shard_map/bkj,bjr->bkr/dot_general | solution.py:15
  88.6 2.8 %collective-permute-done.6 = bf16[128,1024]{0,1:T(8,128)(2,1)S(1)} collective-permute-done((bf16[128,1024]{0,1:T(8,128)(2,1)S(1)}, bf16[128,1024]{0,1:T(8,128)(2,1)S(1)}, u32[]{:S(2)}, u32[]{:S(2)}) %collective-permute-start.6) | collective-permute-done | bytes 262176 | tf_op jit(solution)/shard_map/ppermute | solution.py:10
  92.0 5.3 %fusion.28 = bf16[16,1,128,256]{3,0,1,2:T(8,128)(2,1)} fusion(bf16[128,64,256]{2,1,0:T(8,128)(2,1)} %param.12, f32[128,16,64]{2,1,0:T(8,128)} %fusion.2, bf16[128,64,16]{1,2,0:T(8,128)(2,1)S(1)} %copy.51, bf16[128,64,128]{2,1,0:T(8,128)(2,1)S(1)} %copy-done), kind=kOutput, calls=%fused_computation.38 | convolution fusion | flops 84672512 | bytes 8126464 | tf_op jit(solution)/shard_map/bks,bkr->rbs/dot_general | solution.py:48
  97.3 9.7 %all-to-all-start = ((bf16[16,1,128,256]{3,0,1,2:T(8,128)(2,1)}), bf16[16,1,128,256]{3,0,1,2:T(8,128)(2,1)S(1)}, u32[]{:S(2)}, u32[]{:S(2)}) async-start(bf16[16,1,128,256]{3,0,1,2:T(8,128)(2,1)} %fusion.28), calls=%async_computation | async-start | bytes 2097152 | tf_op jit(solution)/shard_map/all_to_all | solution.py:56
  107.1 18.9 %all-to-all-done = bf16[16,1,128,256]{3,0,1,2:T(8,128)(2,1)S(1)} async-done(((bf16[16,1,128,256]{3,0,1,2:T(8,128)(2,1)}), bf16[16,1,128,256]{3,0,1,2:T(8,128)(2,1)S(1)}, u32[]{:S(2)}, u32[]{:S(2)}) %all-to-all-start) | async-done | bytes 1048608 | tf_op jit(solution)/shard_map/all_to_all | solution.py:56
  125.9 0.6 gather_fusion.1
  126.8 1.0 copy.55
  (15 shorter events, 1.3 us)
Async XLA Ops:
  7.3 14.8 %collective-permute-start = (bf16[128,1024]{0,1:T(8,128)(2,1)S(1)}, bf16[128,1024]{0,1:T(8,128)(2,1)S(1)}, u32[]{:S(2)}, u32[]{:S(2)}) collective-permute-start(bf16[128,1024]{0,1:T(8,128)(2,1)S(1)} %bitcast.80), channel_id=1, source_target_pairs={{0,1},{1,0},{2,3},{3,2},{4,5},{5,4},{6,7},{7,6},{8,9},{9,8},{10,11... | collective-permute-start | bytes 786440 | tf_op jit(solution)/shard_map/ppermute | solution.py:10
  19.9 2.7 %copy-start.1 = (bf16[128,64,128]{2,1,0:T(8,128)(2,1)}, bf16[128,64,128]{2,1,0:T(8,128)(2,1)S(1)}, u32[]{:S(2)}) copy-start(bf16[128,64,128]{2,1,0:T(8,128)(2,1)S(1)} %get-tuple-element.11) | copy-start | bytes 6291460
  26.4 9.1 %collective-permute-start.1 = (bf16[128,1024]{0,1:T(8,128)(2,1)S(1)}, bf16[128,1024]{0,1:T(8,128)(2,1)S(1)}, u32[]{:S(2)}, u32[]{:S(2)}) collective-permute-start(bf16[128,1024]{0,1:T(8,128)(2,1)S(1)} %bitcast.88), channel_id=1, source_target_pairs={{0,2},{1,3},{2,0},{3,1},{4,6},{5,7},{6,4},{7,5},{8,10},{9,11},{10,... | collective-permute-start | bytes 786440 | tf_op jit(solution)/shard_map/ppermute | solution.py:10
  39.5 8.0 %collective-permute-start.2 = (bf16[128,1024]{0,1:T(8,128)(2,1)S(1)}, bf16[128,1024]{0,1:T(8,128)(2,1)S(1)}, u32[]{:S(2)}, u32[]{:S(2)}) collective-permute-start(bf16[128,1024]{0,1:T(8,128)(2,1)S(1)} %bitcast.89), channel_id=1, source_target_pairs={{0,4},{1,5},{2,6},{3,7},{4,0},{5,1},{6,2},{7,3},{8,12},{9,13},{10,... | collective-permute-start | bytes 786440 | tf_op jit(solution)/shard_map/ppermute | solution.py:10
  51.5 5.3 %collective-permute-start.3 = (bf16[128,1024]{0,1:T(8,128)(2,1)S(1)}, bf16[128,1024]{0,1:T(8,128)(2,1)S(1)}, u32[]{:S(2)}, u32[]{:S(2)}) collective-permute-start(bf16[128,1024]{0,1:T(8,128)(2,1)S(1)} %bitcast.90), channel_id=1, source_target_pairs={{0,8},{8,0},{16,24},{24,16},{1,9},{9,1},{17,25},{25,17},{2,10},{10... | collective-permute-start | bytes 786440 | tf_op jit(solution)/shard_map/ppermute | solution.py:10
  60.8 6.8 %collective-permute-start.4 = (bf16[128,1024]{0,1:T(8,128)(2,1)S(1)}, bf16[128,1024]{0,1:T(8,128)(2,1)S(1)}, u32[]{:S(2)}, u32[]{:S(2)}) collective-permute-start(bf16[128,1024]{0,1:T(8,128)(2,1)S(1)} %bitcast.91), channel_id=1, source_target_pairs={{0,16},{8,24},{16,0},{24,8},{1,17},{9,25},{17,1},{25,9},{2,18},{10... | collective-permute-start | bytes 786440 | tf_op jit(solution)/shard_map/ppermute | solution.py:10
  71.6 7.6 %collective-permute-start.5 = (bf16[128,1024]{0,1:T(8,128)(2,1)S(1)}, bf16[128,1024]{0,1:T(8,128)(2,1)S(1)}, u32[]{:S(2)}, u32[]{:S(2)}) collective-permute-start(bf16[128,1024]{0,1:T(8,128)(2,1)S(1)} %bitcast.92), channel_id=1, source_target_pairs={{0,32},{32,0},{64,96},{96,64},{1,33},{33,1},{65,97},{97,65},{2,34}... | collective-permute-start | bytes 786440 | tf_op jit(solution)/shard_map/ppermute | solution.py:10
  83.2 8.2 %collective-permute-start.6 = (bf16[128,1024]{0,1:T(8,128)(2,1)S(1)}, bf16[128,1024]{0,1:T(8,128)(2,1)S(1)}, u32[]{:S(2)}, u32[]{:S(2)}) collective-permute-start(bf16[128,1024]{0,1:T(8,128)(2,1)S(1)} %bitcast.87), channel_id=1, source_target_pairs={{0,64},{32,96},{64,0},{96,32},{1,65},{33,97},{65,1},{97,33},{2,66}... | collective-permute-start | bytes 786440 | tf_op jit(solution)/shard_map/ppermute | solution.py:10
  84.7 7.3 %copy-start = (bf16[128,64,128]{2,1,0:T(8,128)(2,1)S(1)}, bf16[128,64,128]{2,1,0:T(8,128)(2,1)}, u32[]{:S(2)}) copy-start(bf16[128,64,128]{2,1,0:T(8,128)(2,1)} %get-tuple-element.6) | copy-start | bytes 6291460
  97.3 9.7 %copy-start.2 = (s32[128]{0:T(128)S(1)}, s32[128]{0:T(128)}, u32[]{:S(2)}) copy-start(s32[128]{0:T(128)} %param.13) | copy-start | bytes 1540
  97.3 28.6 %all-to-all-start = ((bf16[16,1,128,256]{3,0,1,2:T(8,128)(2,1)}), bf16[16,1,128,256]{3,0,1,2:T(8,128)(2,1)S(1)}, u32[]{:S(2)}, u32[]{:S(2)}) async-start(bf16[16,1,128,256]{3,0,1,2:T(8,128)(2,1)} %fusion.28), calls=%async_computation | async-start | bytes 2097152 | tf_op jit(solution)/shard_map/all_to_all | solution.py:56
where the time goes:
time: 128 us
  matrix products  46 us (36%)
  starting transfers between devices  29.3 us (23%)
  waiting for transfers between devices  29.1 us (23%)
  local copies, waits for them, and re-layouts  21.6 us (17%)
  other arithmetic  1.55 us (1%)
    dot_general x7, matrix products, level_step(): jnp.einsum('bkj,bjr->bkr', tables[:, :, :rank_k], coeffs, preferred_eleme...  19.9 us
    ppermute x7, starting transfers between devices, from_partner(): return lax.ppermute(value, axis, pairs)  19.7 us
    all_to_all x1, waiting for transfers between devices, local(): lax.all_to_all(shaped, ('gx', 'gy', 'gz'), split_axis=2, concat_axis=2, t...  18.9 us
    dot_general x6, matrix products, level_step(): jnp.einsum('bkj,bjr->bkr', tables[:, :, rank_k:], partner, preferred_elem...  17.4 us
    ppermute x7, waiting for transfers between devices, from_partner(): return lax.ppermute(value, axis, pairs)  10.2 us
    squeeze x1, local copies, waits for them, and re-layouts, local(): coeffs = level_step(coeffs, translate[level_no], partner)  10 us
    all_to_all x1, starting transfers between devices, local(): lax.all_to_all(shaped, ('gx', 'gy', 'gz'), split_axis=2, concat_axis=2, t...  9.68 us
    dot_general x1, matrix products, local(): jnp.einsum('bks,bkr->rbs', evaluate, coeffs, preferred_element_type=jnp.f...  5.31 us
  transfers between devices with their start and end apart: 8, of which 6 were waited for; matrix products, arithmetic and copies ran while one was open for 23% of the time, Pallas kernels for 0%

commit v1 on v0

v1 whole, which is shorter than its diff:
```python
import functools

import jax
import jax.numpy as jnp
from jax import lax
from jax.experimental import pallas as pl
from jax.experimental.pallas import tpu as pltpu
from jax.sharding import PartitionSpec as P

AXES = ("gx", "gy", "gz")
PACK = 8
CHUNKS = (8, 8)


def own_lanes(shape, cols):
    return lax.broadcasted_iota(jnp.int32, shape, 1) // cols


def pick(wide, rank, cols):
    lane_box = own_lanes((rank, PACK * cols), cols)
    out = wide[:rank]
    for box in range(1, PACK):
        out = jnp.where(lane_box == box, wide[box * rank : (box + 1) * rank], out)
    return out


def interp_body(first, per_step, slot_ref, src_ref, interp_ref, *rest):
    out_ref = rest[-1]
    _, rank, span = interp_ref.shape
    rhs = src_ref.shape[0]
    for grp in range(per_step):
        base = (first + pl.program_id(0) * per_step + grp) * PACK
        slabs = []
        for box in range(PACK):
            at = pl.multiple_of(slot_ref[base + box] * span, span)
            slabs.append(src_ref[:, pl.ds(at, span)])
        points = jnp.concatenate(slabs, axis=0)
        block = interp_ref[grp * PACK : (grp + 1) * PACK].reshape(PACK * rank, span)
        wide = lax.dot_general(
            block, points, (((1,), (1,)), ((), ())), preferred_element_type=jnp.float32
        )
        out_ref[grp] = pick(wide, rank, rhs).astype(jnp.bfloat16)


def interp_call(first, groups, slot, src, interp, *after):
    per_step = 2
    boxes, rank, span = interp.shape
    rhs = src.shape[0]
    lanes = PACK * rhs
    return pl.pallas_call(
        functools.partial(interp_body, first, per_step),
        grid_spec=pltpu.PrefetchScalarGridSpec(
            num_scalar_prefetch=1,
            grid=(groups // per_step,),
            in_specs=[
                pl.BlockSpec(src.shape, lambda i, s: (0, 0)),
                pl.BlockSpec(
                    (per_step * PACK, rank, span), lambda i, s: (first // per_step + i, 0, 0)
                ),
            ]
            + [pl.BlockSpec(memory_space=pl.ANY)] * len(after),
            out_specs=pl.BlockSpec((per_step, rank, lanes), lambda i, s: (i, 0, 0)),
        ),
        out_shape=jax.ShapeDtypeStruct((groups, rank, lanes), jnp.bfloat16),
        compiler_params=pltpu.CompilerParams(vmem_limit_bytes=24 * 2**20),
        cost_estimate=pl.CostEstimate(
            flops=2 * groups * lanes * rank * span,
            bytes_accessed=groups * PACK * rank * span * 2 + src.size * 2,
            transcendentals=0,
        ),
        name="interp",
    )(slot, src, interp, *after)


def level_body(per_step, table_ref, own_ref, far_ref, *rest):
    out_ref = rest[-1]
    _, _, rank, both = table_ref.shape
    lanes = own_ref.shape[2]
    for grp in range(per_step):
        block = table_ref[0, grp * PACK : (grp + 1) * PACK].reshape(PACK * rank, both)
        pair = jnp.concatenate([own_ref[grp], far_ref[grp]], axis=0)
        wide = jnp.dot(block, pair, preferred_element_type=jnp.float32)
        out_ref[grp] = pick(wide, rank, lanes // PACK).astype(jnp.bfloat16)


def level_call(level, first, tables, own, far, *after):
    per_step = 2
    groups, rank, lanes = own.shape
    both = tables.shape[3]
    return pl.pallas_call(
        functools.partial(level_body, per_step),
        grid=(groups // per_step,),
        in_specs=[
            pl.BlockSpec(
                (1, per_step * PACK, rank, both), lambda i: (level, first // per_step + i, 0, 0)
            ),
            pl.BlockSpec((per_step, rank, lanes), lambda i: (i, 0, 0)),
            pl.BlockSpec((per_step, rank, lanes), lambda i: (i, 0, 0)),
        ]
        + [pl.BlockSpec(memory_space=pl.ANY)] * len(after),
        out_specs=pl.BlockSpec((per_step, rank, lanes), lambda i: (i, 0, 0)),
        out_shape=jax.ShapeDtypeStruct(own.shape, jnp.bfloat16),
        compiler_params=pltpu.CompilerParams(vmem_limit_bytes=24 * 2**20),
        cost_estimate=pl.CostEstimate(
            flops=2 * groups * lanes * rank * both,
            bytes_accessed=groups * PACK * rank * both * 2,
            transcendentals=0,
        ),
        name="level",
    )(tables, own, far, *after)


def eval_body(per_step, coeffs_ref, eval_ref, *rest):
    out_ref = rest[-1]
    _, rank, span = eval_ref.shape
    lanes = coeffs_ref.shape[2]
    rhs = lanes // PACK
    for grp in range(per_step):
        mine = coeffs_ref[grp].astype(jnp.float32)
        twice = jnp.concatenate([mine, mine], axis=0).T.astype(jnp.bfloat16)
        left = jnp.concatenate([twice] * (PACK // 2), axis=1)
        row_box = lax.broadcasted_iota(jnp.int32, left.shape, 0) // rhs
        col_box = lax.broadcasted_iota(jnp.int32, left.shape, 1) // rank
        left = jnp.where(row_box == col_box, left, jnp.zeros_like(left))
        block = eval_ref[grp * PACK : (grp + 1) * PACK].reshape(PACK * rank, span)
        vals = jnp.dot(left, block, preferred_element_type=jnp.float32)
        out_ref[grp * PACK : (grp + 1) * PACK] = vals.astype(jnp.bfloat16).reshape(
            PACK, rhs, span
        )


def eval_call(first, coeffs, evaluate, *before):
    per_step = 2
    groups, rank, lanes = coeffs.shape
    boxes, _, span = evaluate.shape
    rhs = lanes // PACK
    return pl.pallas_call(
        functools.partial(eval_body, per_step),
        grid=(groups // per_step,),
        in_specs=[
            pl.BlockSpec((per_step, rank, lanes), lambda i: (i, 0, 0)),
            pl.BlockSpec((per_step * PACK, rank, span), lambda i: (first // per_step + i, 0, 0)),
        ]
        + [pl.BlockSpec(memory_space=pl.ANY)] * len(before),
        out_specs=pl.BlockSpec(
            (per_step * PACK, rhs, span), lambda i: (first // per_step + i, 0, 0)
        ),
        out_shape=jax.ShapeDtypeStruct((boxes, rhs, span), jnp.bfloat16),
        input_output_aliases={2: 0} if before else {},
        compiler_params=pltpu.CompilerParams(vmem_limit_bytes=24 * 2**20),
        cost_estimate=pl.CostEstimate(
            flops=2 * groups * lanes * rank * span,
            bytes_accessed=groups * PACK * (rank + rhs) * span * 2,
            transcendentals=0,
        ),
        name="evaluate",
    )(coeffs, evaluate, *before)


def place_body(per_step, slot_ref, got_ref, out_ref):
    span = got_ref.shape[2]
    base = pl.program_id(0) * per_step
    for box in range(per_step):
        out_ref[:, box * span : (box + 1) * span] = got_ref[slot_ref[base + box]]


def place_call(slot, got):
    per_step = 32
    boxes, rhs, span = got.shape
    return pl.pallas_call(
        functools.partial(place_body, per_step),
        grid_spec=pltpu.PrefetchScalarGridSpec(
            num_scalar_prefetch=1,
            grid=(boxes // per_step,),
            in_specs=[pl.BlockSpec(got.shape, lambda i, s: (0, 0, 0))],
            out_specs=pl.BlockSpec((rhs, per_step * span), lambda i, s: (0, i)),
        ),
        out_shape=jax.ShapeDtypeStruct((rhs, boxes * span), got.dtype),
        compiler_params=pltpu.CompilerParams(vmem_limit_bytes=24 * 2**20),
        cost_estimate=pl.CostEstimate(
            flops=0, bytes_accessed=4 * got.size, transcendentals=0
        ),
        name="place",
    )(slot, got)


def from_partner(value, axis, distance):
    mask = 2**distance
    pairs = [(source, source ^ mask) for source in range(lax.axis_size(axis))]
    return lax.ppermute(value, axis, pairs)


def local(sources, in_slot, interp, translate, evaluate, owner_slot):
    firsts = [sum(CHUNKS[:i]) for i in range(len(CHUNKS))]
    coeffs = []
    for first, groups in zip(firsts, CHUNKS):
        coeffs.append(interp_call(first, groups, in_slot, sources, interp, *coeffs[-1:]))
    steps = [
        (axis, bit_pos)
        for axis in ("gz", "gy", "gx")
        for bit_pos in range(lax.axis_size(axis).bit_length() - 1)
    ]
    for level, (axis, bit_pos) in enumerate(steps):
        last = coeffs[-1]
        for i, first in enumerate(firsts):
            far = from_partner(coeffs[i], axis, bit_pos)
            after = () if len(firsts) == 1 else (last,)
            last = coeffs[i] = level_call(level, first, translate, coeffs[i], far, *after)
    values = ()
    for i, first in enumerate(firsts):
        values = (eval_call(first, coeffs[i], evaluate, *values),)
    moved = lax.all_to_all(values[0], AXES, split_axis=0, concat_axis=0, tiled=True)
    return place_call(owner_slot, moved)


def solution(mesh):
    placed = (
        P(None, AXES),
        P(AXES),
        P(AXES, None, None),
        P(None, AXES, None, None),
        P(AXES, None, None),
        P(AXES),
    )
    return jax.shard_map(
        local, mesh=mesh, in_specs=placed, out_specs=P(None, AXES), check_vma=False
    )
```

time: 128 us -> 96.8 us (0.76)
  matrix products: 46 us -> 0 us
  blocking collectives: 0 us -> 27.7 us
  waiting for transfers between devices: 29.1 us -> 7.03 us
  Pallas kernels: 0 us -> 20.4 us
  local copies, waits for them, and re-layouts: 21.6 us -> 10.3 us
  starting transfers between devices: 29.3 us -> 31 us
  other arithmetic: 1.55 us -> 0 us
    dot_general x15 -> x0, matrix products: 46 us -> none  [the longest x7 19.9 us: level_step(): jnp.einsum('bkj,bjr->bkr', tables[:, :, :rank_k], coeffs, preferred_eleme...]
    all_to_all x0 -> x1, blocking collectives: none -> 27.7 us  [local(): lax.all_to_all(values[0], AXES, split_axis=0, concat_axis=0, tiled=True)]
    pallas_call x0 -> x19, Pallas kernels: none -> 20.4 us  [the longest x14 12.3 us: level_call(): pl.pallas_call(functools.partial(level_body, per_step), grid=(groups // p...]
    all_to_all x1 -> x0, waiting for transfers between devices: 18.9 us -> none  [local(): lax.all_to_all(shaped, ('gx', 'gy', 'gz'), split_axis=2, concat_axis=2, t...]
    ppermute x7 -> x14, starting transfers between devices: 19.7 us -> 31 us  [from_partner(): return lax.ppermute(value, axis, pairs)]
    unnamed x6 -> x14, local copies, waits for them, and re-layouts: 0.01 us -> 10.3 us
    squeeze x1 -> x0, local copies, waits for them, and re-layouts: 10 us -> none  [local(): coeffs = level_step(coeffs, translate[level_no], partner)]
    all_to_all x1 -> x0, starting transfers between devices: 9.68 us -> none  [local(): lax.all_to_all(shaped, ('gx', 'gy', 'gz'), split_axis=2, concat_axis=2, t...]
  transfers between devices with their start and end apart: 8 -> 14, of which waited for: 6 -> 7; matrix products, arithmetic and copies ran while one was open for 23% -> 0% of each run, Pallas kernels for 0% -> 15%
where the time goes in v1:
time: 96.8 us; the launch traced here: 96.5 us
  starting transfers between devices  31 us (32%)
  blocking collectives  27.7 us (29%)
  Pallas kernels  20.4 us (21%)
  local copies, waits for them, and re-layouts  10.3 us (11%)
  waiting for transfers between devices  7.03 us (7%)
    ppermute x14, starting transfers between devices, from_partner(): return lax.ppermute(value, axis, pairs)  31 us
    all_to_all x1, blocking collectives, local(): lax.all_to_all(values[0], AXES, split_axis=0, concat_axis=0, tiled=True)  27.7 us
    pallas_call x14, Pallas kernels, level_call(): pl.pallas_call(functools.partial(level_body, per_step), grid=(groups // p...  12.3 us
    unnamed x14, local copies, waits for them, and re-layouts  10.3 us
    ppermute x14, waiting for transfers between devices, from_partner(): return lax.ppermute(value, axis, pairs)  7.03 us
    pallas_call x2, Pallas kernels, interp_call(): pl.pallas_call(functools.partial(interp_body, first, per_step), grid_spec...  3.64 us
    pallas_call x2, Pallas kernels, eval_call(): pl.pallas_call(functools.partial(eval_body, per_step), grid=(groups // pe...  2.29 us
    pallas_call x1, Pallas kernels, place_call(): pl.pallas_call(functools.partial(place_body, per_step), grid_spec=pltpu.P...  2.11 us
  transfers between devices with their start and end apart: 14, of which 7 were waited for; matrix products, arithmetic and copies ran while one was open for 0% of the time, Pallas kernels for 15%

profile of v1, /device:TPU:1, one launch (start us, length us, event | category | flops | bytes accessed | tf_op | source)
XLA Modules:
  0.0 96.5 jit_solution(14694967150168084706)
XLA Ops:
  0.0 2.2 %copy-done.2 = bf16[128,64,256]{2,1,0:T(8,128)(2,1)S(1)} copy-done((bf16[128,64,256]{2,1,0:T(8,128)(2,1)S(1)}, bf16[128,64,256]{2,1,0:T(8,128)(2,1)}, u32[]{:S(2)}) %copy-start.2) | copy-done | bytes 4194328
  2.2 1.2 %copy-done.4 = bf16[16,32768]{1,0:T(8,128)(2,1)S(1)} copy-done((bf16[16,32768]{1,0:T(8,128)(2,1)S(1)}, bf16[16,32768]{1,0:T(8,128)(2,1)}, u32[]{:S(2)}) %copy-start.4) | copy-done | bytes 1048600
  3.4 0.7 copy-done.5
  4.1 1.8 %interp.2.rest_0_.own_ref = bf16[8,64,128]{2,1,0:T(8,128)(2,1)S(1)} custom-call(s32[128]{0:T(128)S(1)} %copy-done.5, bf16[16,32768]{1,0:T(8,128)(2,1)S(1)} %copy-done.4, bf16[128,64,256]{2,1,0:T(8,128)(2,1)S(1)} %copy-done.2), custom_call_target="tpu_custom_call" | custom-call | flops 33554432 | bytes 3145728 | tf_op jit(solution)/shard_map/interp/pallas_call | solution.py:50
  5.9 2.5 %collective-permute-start.1 = (bf16[8,64,128]{2,1,0:T(8,128)(2,1)S(1)}, bf16[8,64,128]{2,1,0:T(8,128)(2,1)S(1)}, u32[]{:S(2)}, u32[]{:S(2)}) collective-permute-start(bf16[8,64,128]{2,1,0:T(8,128)(2,1)S(1)} %interp.2.rest_0_.own_ref), channel_id=1, source_target_pairs={{0,1},{1,0},{2,3},{3,2},{4,5},{5,4},{6,7},{7,6},{8,9},{9,8},{10,11... | collective-permute-start | bytes 393224 | tf_op jit(solution)/shard_map/ppermute | solution.py:190
  8.4 1.8 %interp.3.rest_0_.own_ref = bf16[8,64,128]{2,1,0:T(8,128)(2,1)S(1)} custom-call(s32[128]{0:T(128)S(1)} %copy-done.5, bf16[16,32768]{1,0:T(8,128)(2,1)S(1)} %copy-done.4, bf16[128,64,256]{2,1,0:T(8,128)(2,1)S(1)} %copy-done.2, bf16[8,64,128]{2,1,0:T(8,128)(2,1)S(1)} %interp.2.rest_0_.own_ref), custom_call_target="tpu_custom_call" | custom-call | flops 33554432 | bytes 3145728 | tf_op jit(solution)/shard_map/interp/pallas_call | solution.py:50
  10.3 0.1 collective-permute-start
  10.4 1.3 %collective-permute-done.1.far_ref = bf16[8,64,128]{2,1,0:T(8,128)(2,1)S(1)} collective-permute-done((bf16[8,64,128]{2,1,0:T(8,128)(2,1)S(1)}, bf16[8,64,128]{2,1,0:T(8,128)(2,1)S(1)}, u32[]{:S(2)}, u32[]{:S(2)}) %collective-permute-start.1) | collective-permute-done | bytes 131104 | tf_op jit(solution)/shard_map/ppermute | solution.py:190
  11.7 5.2 %copy-done = bf16[7,128,64,128]{3,2,1,0:T(8,128)(2,1)S(1)} copy-done((bf16[7,128,64,128]{3,2,1,0:T(8,128)(2,1)S(1)}, bf16[7,128,64,128]{3,2,1,0:T(8,128)(2,1)}, u32[]{:S(2)}) %copy-start) | copy-done | bytes 14680088
  16.8 0.9 level.14.rest_0_.own_ref
  17.7 3.2 %collective-permute-start.3 = (bf16[8,64,128]{2,1,0:T(8,128)(2,1)S(1)}, bf16[8,64,128]{2,1,0:T(8,128)(2,1)S(1)}, u32[]{:S(2)}, u32[]{:S(2)}) collective-permute-start(bf16[8,64,128]{2,1,0:T(8,128)(2,1)S(1)} %level.14.rest_0_.own_ref), channel_id=1, source_target_pairs={{0,2},{1,3},{2,0},{3,1},{4,6},{5,7},{6,4},{7,5},{8,10},{9,11},{10,... | collective-permute-start | bytes 393224 | tf_op jit(solution)/shard_map/ppermute | solution.py:190
  20.9 1.1 %copy-done.1 = bf16[7,128,64,128]{3,2,1,0:T(8,128)(2,1)S(1)} copy-done((bf16[7,128,64,128]{3,2,1,0:T(8,128)(2,1)S(1)}, bf16[7,128,64,128]{3,2,1,0:T(8,128)(2,1)}, u32[]{:S(2)}) %copy-start.1) | copy-done | bytes 14680088
  22.0 0.9 level.15.rest_0_.own_ref
  22.9 3.2 %collective-permute-start.2 = (bf16[8,64,128]{2,1,0:T(8,128)(2,1)S(1)}, bf16[8,64,128]{2,1,0:T(8,128)(2,1)S(1)}, u32[]{:S(2)}, u32[]{:S(2)}) collective-permute-start(bf16[8,64,128]{2,1,0:T(8,128)(2,1)S(1)} %level.15.rest_0_.own_ref), channel_id=1, source_target_pairs={{0,2},{1,3},{2,0},{3,1},{4,6},{5,7},{6,4},{7,5},{8,10},{9,11},{10,... | collective-permute-start | bytes 393224 | tf_op jit(solution)/shard_map/ppermute | solution.py:190
  26.1 0.9 level.16.rest_0_.own_ref
  27.0 2.8 %collective-permute-start.5 = (bf16[8,64,128]{2,1,0:T(8,128)(2,1)S(1)}, bf16[8,64,128]{2,1,0:T(8,128)(2,1)S(1)}, u32[]{:S(2)}, u32[]{:S(2)}) collective-permute-start(bf16[8,64,128]{2,1,0:T(8,128)(2,1)S(1)} %level.16.rest_0_.own_ref), channel_id=1, source_target_pairs={{0,4},{1,5},{2,6},{3,7},{4,0},{5,1},{6,2},{7,3},{8,12},{9,13},{10,... | collective-permute-start | bytes 393224 | tf_op jit(solution)/shard_map/ppermute | solution.py:190
  29.8 0.9 level.17.rest_0_.own_ref
  30.7 1.5 %collective-permute-start.4 = (bf16[8,64,128]{2,1,0:T(8,128)(2,1)S(1)}, bf16[8,64,128]{2,1,0:T(8,128)(2,1)S(1)}, u32[]{:S(2)}, u32[]{:S(2)}) collective-permute-start(bf16[8,64,128]{2,1,0:T(8,128)(2,1)S(1)} %level.17.rest_0_.own_ref), channel_id=1, source_target_pairs={{0,4},{1,5},{2,6},{3,7},{4,0},{5,1},{6,2},{7,3},{8,12},{9,13},{10,... | collective-permute-start | bytes 393224 | tf_op jit(solution)/shard_map/ppermute | solution.py:190
  32.2 0.2 collective-permute-done.5.far_ref
  32.4 0.9 level.18.rest_0_.own_ref
  33.3 1.4 %collective-permute-start.7 = (bf16[8,64,128]{2,1,0:T(8,128)(2,1)S(1)}, bf16[8,64,128]{2,1,0:T(8,128)(2,1)S(1)}, u32[]{:S(2)}, u32[]{:S(2)}) collective-permute-start(bf16[8,64,128]{2,1,0:T(8,128)(2,1)S(1)} %level.18.rest_0_.own_ref), channel_id=1, source_target_pairs={{0,8},{8,0},{16,24},{24,16},{1,9},{9,1},{17,25},{25,17},{2,10},{10... | collective-permute-start | bytes 393224 | tf_op jit(solution)/shard_map/ppermute | solution.py:190
  34.6 1.5 %collective-permute-done.4.far_ref = bf16[8,64,128]{2,1,0:T(8,128)(2,1)S(1)} collective-permute-done((bf16[8,64,128]{2,1,0:T(8,128)(2,1)S(1)}, bf16[8,64,128]{2,1,0:T(8,128)(2,1)S(1)}, u32[]{:S(2)}, u32[]{:S(2)}) %collective-permute-start.4) | collective-permute-done | bytes 131104 | tf_op jit(solution)/shard_map/ppermute | solution.py:190
  36.1 0.9 level.19.rest_0_.own_ref
  37.0 1.4 %collective-permute-start.6 = (bf16[8,64,128]{2,1,0:T(8,128)(2,1)S(1)}, bf16[8,64,128]{2,1,0:T(8,128)(2,1)S(1)}, u32[]{:S(2)}, u32[]{:S(2)}) collective-permute-start(bf16[8,64,128]{2,1,0:T(8,128)(2,1)S(1)} %level.19.rest_0_.own_ref), channel_id=1, source_target_pairs={{0,8},{8,0},{16,24},{24,16},{1,9},{9,1},{17,25},{25,17},{2,10},{10... | collective-permute-start | bytes 393224 | tf_op jit(solution)/shard_map/ppermute | solution.py:190
  38.4 0.9 level.20.rest_0_.own_ref
  39.3 2.7 %collective-permute-start.9 = (bf16[8,64,128]{2,1,0:T(8,128)(2,1)S(1)}, bf16[8,64,128]{2,1,0:T(8,128)(2,1)S(1)}, u32[]{:S(2)}, u32[]{:S(2)}) collective-permute-start(bf16[8,64,128]{2,1,0:T(8,128)(2,1)S(1)} %level.20.rest_0_.own_ref), channel_id=1, source_target_pairs={{0,16},{8,24},{16,0},{24,8},{1,17},{9,25},{17,1},{25,9},{2,18},{10... | collective-permute-start | bytes 393224 | tf_op jit(solution)/shard_map/ppermute | solution.py:190
  42.0 0.6 collective-permute-done.6.far_ref
  42.5 0.9 level.21.rest_0_.own_ref
  43.4 3.0 %collective-permute-start.8 = (bf16[8,64,128]{2,1,0:T(8,128)(2,1)S(1)}, bf16[8,64,128]{2,1,0:T(8,128)(2,1)S(1)}, u32[]{:S(2)}, u32[]{:S(2)}) collective-permute-start(bf16[8,64,128]{2,1,0:T(8,128)(2,1)S(1)} %level.21.rest_0_.own_ref), channel_id=1, source_target_pairs={{0,16},{8,24},{16,0},{24,8},{1,17},{9,25},{17,1},{25,9},{2,18},{10... | collective-permute-start | bytes 393224 | tf_op jit(solution)/shard_map/ppermute | solution.py:190
  46.4 0.2 collective-permute-done.9.far_ref
  46.6 0.9 level.22.rest_0_.own_ref
  47.5 4.5 %collective-permute-start.11 = (bf16[8,64,128]{2,1,0:T(8,128)(2,1)S(1)}, bf16[8,64,128]{2,1,0:T(8,128)(2,1)S(1)}, u32[]{:S(2)}, u32[]{:S(2)}) collective-permute-start(bf16[8,64,128]{2,1,0:T(8,128)(2,1)S(1)} %level.22.rest_0_.own_ref), channel_id=1, source_target_pairs={{0,32},{32,0},{64,96},{96,64},{1,33},{33,1},{65,97},{97,65},{2,34}... | collective-permute-start | bytes 393224 | tf_op jit(solution)/shard_map/ppermute | solution.py:190
  52.0 0.9 level.23.rest_0_.own_ref
  52.9 2.7 %collective-permute-start.10 = (bf16[8,64,128]{2,1,0:T(8,128)(2,1)S(1)}, bf16[8,64,128]{2,1,0:T(8,128)(2,1)S(1)}, u32[]{:S(2)}, u32[]{:S(2)}) collective-permute-start(bf16[8,64,128]{2,1,0:T(8,128)(2,1)S(1)} %level.23.rest_0_.own_ref), channel_id=1, source_target_pairs={{0,32},{32,0},{64,96},{96,64},{1,33},{33,1},{65,97},{97,65},{2,34}... | collective-permute-start | bytes 393224 | tf_op jit(solution)/shard_map/ppermute | solution.py:190
  55.6 0.9 level.24.rest_0_.own_ref
  56.5 1.8 %collective-permute-start.13 = (bf16[8,64,128]{2,1,0:T(8,128)(2,1)S(1)}, bf16[8,64,128]{2,1,0:T(8,128)(2,1)S(1)}, u32[]{:S(2)}, u32[]{:S(2)}) collective-permute-start(bf16[8,64,128]{2,1,0:T(8,128)(2,1)S(1)} %level.24.rest_0_.own_ref), channel_id=1, source_target_pairs={{0,64},{32,96},{64,0},{96,32},{1,65},{33,97},{65,1},{97,33},{2,66}... | collective-permute-start | bytes 393224 | tf_op jit(solution)/shard_map/ppermute | solution.py:190
  58.4 0.9 level.25.rest_0_.own_ref
  59.2 0.0 copy-start.3
  59.3 0.1 collective-permute-start.12
  59.4 2.8 %collective-permute-done.13.far_ref = bf16[8,64,128]{2,1,0:T(8,128)(2,1)S(1)} collective-permute-done((bf16[8,64,128]{2,1,0:T(8,128)(2,1)S(1)}, bf16[8,64,128]{2,1,0:T(8,128)(2,1)S(1)}, u32[]{:S(2)}, u32[]{:S(2)}) %collective-permute-start.13) | collective-permute-done | bytes 131104 | tf_op jit(solution)/shard_map/ppermute | solution.py:190
  62.2 0.9 level.26.rest_0_.coeffs_ref
  63.1 1.1 %evaluate.2.rest_0_ = bf16[128,16,256]{2,1,0:T(8,128)(2,1)S(1)} custom-call(bf16[8,64,128]{2,1,0:T(8,128)(2,1)S(1)} %level.26.rest_0_.coeffs_ref, bf16[128,64,256]{2,1,0:T(8,128)(2,1)S(1)} %copy-done.3), custom_call_target="tpu_custom_call" | custom-call | flops 33554432 | bytes 2621440 | tf_op jit(solution)/shard_map/evaluate/pallas_call | solution.py:137
  64.2 0.5 collective-permute-done.12.far_ref
  64.7 0.9 level.27.coeffs_ref
  65.6 0.0 copy-start.6
  65.6 1.1 %evaluate.3 = bf16[128,16,256]{2,1,0:T(8,128)(2,1)S(1)} custom-call(bf16[8,64,128]{2,1,0:T(8,128)(2,1)S(1)} %level.27.coeffs_ref, bf16[128,64,256]{2,1,0:T(8,128)(2,1)S(1)} %copy-done.3, bf16[128,16,256]{2,1,0:T(8,128)(2,1)S(1)} %evaluate.2.rest_0_), custom_call_target="tpu_custom_call", output_to_operand_aliasing={{}: (2, {})} | custom-call | flops 33554432 | bytes 2621440 | tf_op jit(solution)/shard_map/evaluate/pallas_call | solution.py:137
  66.8 27.7 %all_to_all.5.got_ref = bf16[128,16,256]{2,1,0:T(8,128)(2,1)S(1)} all-to-all(bf16[128,16,256]{2,1,0:T(8,128)(2,1)S(1)} %evaluate.3), channel_id=1, replica_groups=mesh['gx'=4,'gy'=4,'gz'=8] {'gx','gy','gz'}, dimensions={0} | all-to-all | bytes 2097152 | tf_op jit(solution)/shard_map/all_to_all | solution.py:212
  94.4 2.1 %place.1 = bf16[16,32768]{1,0:T(8,128)(2,1)} custom-call(s32[128]{0:T(128)S(1)} %copy-done.6, bf16[128,16,256]{2,1,0:T(8,128)(2,1)S(1)} %all_to_all.5.got_ref), custom_call_target="tpu_custom_call" | custom-call | bytes 2097152 | tf_op jit(solution)/shard_map/place/pallas_call | solution.py:170
  (14 shorter events, 0.0 us)
Async XLA Ops:
  0.0 2.2 %copy-start.2 = (bf16[128,64,256]{2,1,0:T(8,128)(2,1)S(1)}, bf16[128,64,256]{2,1,0:T(8,128)(2,1)}, u32[]{:S(2)}) copy-start(bf16[128,64,256]{2,1,0:T(8,128)(2,1)} %interp_ref.3) | copy-start | bytes 12582916
  2.2 1.2 %copy-start.4 = (bf16[16,32768]{1,0:T(8,128)(2,1)S(1)}, bf16[16,32768]{1,0:T(8,128)(2,1)}, u32[]{:S(2)}) copy-start(bf16[16,32768]{1,0:T(8,128)(2,1)} %src_ref.3) | copy-start | bytes 3145732
  3.4 0.7 copy-start.5
  5.9 5.7 %collective-permute-start.1 = (bf16[8,64,128]{2,1,0:T(8,128)(2,1)S(1)}, bf16[8,64,128]{2,1,0:T(8,128)(2,1)S(1)}, u32[]{:S(2)}, u32[]{:S(2)}) collective-permute-start(bf16[8,64,128]{2,1,0:T(8,128)(2,1)S(1)} %interp.2.rest_0_.own_ref), channel_id=1, source_target_pairs={{0,1},{1,0},{2,3},{3,2},{4,5},{5,4},{6,7},{7,6},{8,9},{9,8},{10,11... | collective-permute-start | bytes 393224 | tf_op jit(solution)/shard_map/ppermute | solution.py:190
  10.3 10.7 %collective-permute-start = (bf16[8,64,128]{2,1,0:T(8,128)(2,1)S(1)}, bf16[8,64,128]{2,1,0:T(8,128)(2,1)S(1)}, u32[]{:S(2)}, u32[]{:S(2)}) collective-permute-start(bf16[8,64,128]{2,1,0:T(8,128)(2,1)S(1)} %interp.3.rest_0_.own_ref), channel_id=1, source_target_pairs={{0,1},{1,0},{2,3},{3,2},{4,5},{5,4},{6,7},{7,6},{8,9},{9,8},{10,11... | collective-permute-start | bytes 393224 | tf_op jit(solution)/shard_map/ppermute | solution.py:190
  11.7 5.2 %copy-start = (bf16[7,128,64,128]{3,2,1,0:T(8,128)(2,1)S(1)}, bf16[7,128,64,128]{3,2,1,0:T(8,128)(2,1)}, u32[]{:S(2)}) copy-start(bf16[7,128,64,128]{3,2,1,0:T(8,128)(2,1)} %table_ref.27) | copy-start | bytes 44040196
  16.8 5.2 %copy-start.1 = (bf16[7,128,64,128]{3,2,1,0:T(8,128)(2,1)S(1)}, bf16[7,128,64,128]{3,2,1,0:T(8,128)(2,1)}, u32[]{:S(2)}) copy-start(bf16[7,128,64,128]{3,2,1,0:T(8,128)(2,1)} %table_ref.27) | copy-start | bytes 44040196
  17.7 8.4 %collective-permute-start.3 = (bf16[8,64,128]{2,1,0:T(8,128)(2,1)S(1)}, bf16[8,64,128]{2,1,0:T(8,128)(2,1)S(1)}, u32[]{:S(2)}, u32[]{:S(2)}) collective-permute-start(bf16[8,64,128]{2,1,0:T(8,128)(2,1)S(1)} %level.14.rest_0_.own_ref), channel_id=1, source_target_pairs={{0,2},{1,3},{2,0},{3,1},{4,6},{5,7},{6,4},{7,5},{8,10},{9,11},{10,... | collective-permute-start | bytes 393224 | tf_op jit(solution)/shard_map/ppermute | solution.py:190
  22.9 6.9 %collective-permute-start.2 = (bf16[8,64,128]{2,1,0:T(8,128)(2,1)S(1)}, bf16[8,64,128]{2,1,0:T(8,128)(2,1)S(1)}, u32[]{:S(2)}, u32[]{:S(2)}) collective-permute-start(bf16[8,64,128]{2,1,0:T(8,128)(2,1)S(1)} %level.15.rest_0_.own_ref), channel_id=1, source_target_pairs={{0,2},{1,3},{2,0},{3,1},{4,6},{5,7},{6,4},{7,5},{8,10},{9,11},{10,... | collective-permute-start | bytes 393224 | tf_op jit(solution)/shard_map/ppermute | solution.py:190
  27.0 5.4 %collective-permute-start.5 = (bf16[8,64,128]{2,1,0:T(8,128)(2,1)S(1)}, bf16[8,64,128]{2,1,0:T(8,128)(2,1)S(1)}, u32[]{:S(2)}, u32[]{:S(2)}) collective-permute-start(bf16[8,64,128]{2,1,0:T(8,128)(2,1)S(1)} %level.16.rest_0_.own_ref), channel_id=1, source_target_pairs={{0,4},{1,5},{2,6},{3,7},{4,0},{5,1},{6,2},{7,3},{8,12},{9,13},{10,... | collective-permute-start | bytes 393224 | tf_op jit(solution)/shard_map/ppermute | solution.py:190
  30.7 5.4 %collective-permute-start.4 = (bf16[8,64,128]{2,1,0:T(8,128)(2,1)S(1)}, bf16[8,64,128]{2,1,0:T(8,128)(2,1)S(1)}, u32[]{:S(2)}, u32[]{:S(2)}) collective-permute-start(bf16[8,64,128]{2,1,0:T(8,128)(2,1)S(1)} %level.17.rest_0_.own_ref), channel_id=1, source_target_pairs={{0,4},{1,5},{2,6},{3,7},{4,0},{5,1},{6,2},{7,3},{8,12},{9,13},{10,... | collective-permute-start | bytes 393224 | tf_op jit(solution)/shard_map/ppermute | solution.py:190
  33.3 5.1 %collective-permute-start.7 = (bf16[8,64,128]{2,1,0:T(8,128)(2,1)S(1)}, bf16[8,64,128]{2,1,0:T(8,128)(2,1)S(1)}, u32[]{:S(2)}, u32[]{:S(2)}) collective-permute-start(bf16[8,64,128]{2,1,0:T(8,128)(2,1)S(1)} %level.18.rest_0_.own_ref), channel_id=1, source_target_pairs={{0,8},{8,0},{16,24},{24,16},{1,9},{9,1},{17,25},{25,17},{2,10},{10... | collective-permute-start | bytes 393224 | tf_op jit(solution)/shard_map/ppermute | solution.py:190
  37.0 5.5 %collective-permute-start.6 = (bf16[8,64,128]{2,1,0:T(8,128)(2,1)S(1)}, bf16[8,64,128]{2,1,0:T(8,128)(2,1)S(1)}, u32[]{:S(2)}, u32[]{:S(2)}) collective-permute-start(bf16[8,64,128]{2,1,0:T(8,128)(2,1)S(1)} %level.19.rest_0_.own_ref), channel_id=1, source_target_pairs={{0,8},{8,0},{16,24},{24,16},{1,9},{9,1},{17,25},{25,17},{2,10},{10... | collective-permute-start | bytes 393224 | tf_op jit(solution)/shard_map/ppermute | solution.py:190
  39.3 7.3 %collective-permute-start.9 = (bf16[8,64,128]{2,1,0:T(8,128)(2,1)S(1)}, bf16[8,64,128]{2,1,0:T(8,128)(2,1)S(1)}, u32[]{:S(2)}, u32[]{:S(2)}) collective-permute-start(bf16[8,64,128]{2,1,0:T(8,128)(2,1)S(1)} %level.20.rest_0_.own_ref), channel_id=1, source_target_pairs={{0,16},{8,24},{16,0},{24,8},{1,17},{9,25},{17,1},{25,9},{2,18},{10... | collective-permute-start | bytes 393224 | tf_op jit(solution)/shard_map/ppermute | solution.py:190
  43.4 8.6 %collective-permute-start.8 = (bf16[8,64,128]{2,1,0:T(8,128)(2,1)S(1)}, bf16[8,64,128]{2,1,0:T(8,128)(2,1)S(1)}, u32[]{:S(2)}, u32[]{:S(2)}) collective-permute-start(bf16[8,64,128]{2,1,0:T(8,128)(2,1)S(1)} %level.21.rest_0_.own_ref), channel_id=1, source_target_pairs={{0,16},{8,24},{16,0},{24,8},{1,17},{9,25},{17,1},{25,9},{2,18},{10... | collective-permute-start | bytes 393224 | tf_op jit(solution)/shard_map/ppermute | solution.py:190
  47.5 8.2 %collective-permute-start.11 = (bf16[8,64,128]{2,1,0:T(8,128)(2,1)S(1)}, bf16[8,64,128]{2,1,0:T(8,128)(2,1)S(1)}, u32[]{:S(2)}, u32[]{:S(2)}) collective-permute-start(bf16[8,64,128]{2,1,0:T(8,128)(2,1)S(1)} %level.22.rest_0_.own_ref), channel_id=1, source_target_pairs={{0,32},{32,0},{64,96},{96,64},{1,33},{33,1},{65,97},{97,65},{2,34}... | collective-permute-start | bytes 393224 | tf_op jit(solution)/shard_map/ppermute | solution.py:190
  52.9 5.4 %collective-permute-start.10 = (bf16[8,64,128]{2,1,0:T(8,128)(2,1)S(1)}, bf16[8,64,128]{2,1,0:T(8,128)(2,1)S(1)}, u32[]{:S(2)}, u32[]{:S(2)}) collective-permute-start(bf16[8,64,128]{2,1,0:T(8,128)(2,1)S(1)} %level.23.rest_0_.own_ref), channel_id=1, source_target_pairs={{0,32},{32,0},{64,96},{96,64},{1,33},{33,1},{65,97},{97,65},{2,34}... | collective-permute-start | bytes 393224 | tf_op jit(solution)/shard_map/ppermute | solution.py:190
  56.5 5.6 %collective-permute-start.13 = (bf16[8,64,128]{2,1,0:T(8,128)(2,1)S(1)}, bf16[8,64,128]{2,1,0:T(8,128)(2,1)S(1)}, u32[]{:S(2)}, u32[]{:S(2)}) collective-permute-start(bf16[8,64,128]{2,1,0:T(8,128)(2,1)S(1)} %level.24.rest_0_.own_ref), channel_id=1, source_target_pairs={{0,64},{32,96},{64,0},{96,32},{1,65},{33,97},{65,1},{97,33},{2,66}... | collective-permute-start | bytes 393224 | tf_op jit(solution)/shard_map/ppermute | solution.py:190
  59.2 3.8 %copy-start.3 = (bf16[128,64,256]{2,1,0:T(8,128)(2,1)S(1)}, bf16[128,64,256]{2,1,0:T(8,128)(2,1)}, u32[]{:S(2)}) copy-start(bf16[128,64,256]{2,1,0:T(8,128)(2,1)} %eval_ref.3) | copy-start | bytes 12582916
  59.3 5.5 %collective-permute-start.12 = (bf16[8,64,128]{2,1,0:T(8,128)(2,1)S(1)}, bf16[8,64,128]{2,1,0:T(8,128)(2,1)S(1)}, u32[]{:S(2)}, u32[]{:S(2)}) collective-permute-start(bf16[8,64,128]{2,1,0:T(8,128)(2,1)S(1)} %level.25.rest_0_.own_ref), channel_id=1, source_target_pairs={{0,64},{32,96},{64,0},{96,32},{1,65},{33,97},{65,1},{97,33},{2,66}... | collective-permute-start | bytes 393224 | tf_op jit(solution)/shard_map/ppermute | solution.py:190
  65.6 28.8 %copy-start.6 = (s32[128]{0:T(128)S(1)}, s32[128]{0:T(128)}, u32[]{:S(2)}) copy-start(s32[128]{0:T(128)} %slot_ref.5) | copy-start | bytes 1540

commit v2 on v1

v2 whole, which is shorter than its diff:
```python
import functools

import jax
import jax.numpy as jnp
from jax import lax
from jax.experimental import pallas as pl
from jax.experimental.pallas import tpu as pltpu
from jax.sharding import PartitionSpec as P

AXES = ("gx", "gy", "gz")
PACK = 8
CHUNKS = (8, 8)
KEEP = True
LOADS = (2, 2, 3)
VMEM_LIMIT = 16 * 2**20
INTERP_LIMITS = (53.25, 53.25)
LOAD_LIMITS = (40, 38, 36)
MIB = 2**20


def own_lanes(shape, cols):
    return lax.broadcasted_iota(jnp.int32, shape, 1) // cols


def pick(wide, rank, cols):
    lane_box = own_lanes((rank, PACK * cols), cols)
    out = wide[:rank]
    for box in range(1, PACK):
        out = jnp.where(lane_box == box, wide[box * rank : (box + 1) * rank], out)
    return out


def interp_body(first, groups, pieces, slot_hbm, src_hbm, interp_hbm, *rest):
    out_ref, slot_ref, src_ref, interp_ref, sems = rest[-5:]
    _, rank, span = interp_ref.shape
    rhs = src_ref.shape[0]
    per = groups // pieces
    slot_load = pltpu.make_async_copy(slot_hbm, slot_ref, sems.at[pieces + 1])
    slot_load.start()
    load = pltpu.make_async_copy(src_hbm, src_ref, sems.at[pieces])
    load.start()
    loads = []
    for piece in range(pieces):
        at = pl.ds(piece * per * PACK, per * PACK)
        loads.append(
            pltpu.make_async_copy(
                interp_hbm.at[pl.ds(first * PACK + piece * per * PACK, per * PACK)],
                interp_ref.at[at],
                sems.at[piece],
            )
        )
        loads[-1].start()
    slot_load.wait()
    load.wait()
    for grp in range(groups):
        if grp % per == 0:
            loads[grp // per].wait()
        slabs = []
        for box in range(PACK):
            at = pl.multiple_of(slot_ref[(first + grp) * PACK + box] * span, span)
            slabs.append(src_ref[:, pl.ds(at, span)])
        points = jnp.concatenate(slabs, axis=0)
        block = interp_ref[grp * PACK : (grp + 1) * PACK].reshape(PACK * rank, span)
        wide = lax.dot_general(
            block, points, (((1,), (1,)), ((), ())), preferred_element_type=jnp.float32
        )
        out_ref[grp] = pick(wide, rank, rhs).astype(jnp.bfloat16)


def interp_call(limit, first, groups, slot, src, interp, *after):
    pieces = 4
    _, rank, span = interp.shape
    lanes = PACK * src.shape[0]
    return pl.pallas_call(
        functools.partial(interp_body, first, groups, pieces),
        in_specs=[pl.BlockSpec(memory_space=pl.ANY)] * (3 + len(after)),
        out_specs=pl.BlockSpec(memory_space=pltpu.VMEM),
        out_shape=jax.ShapeDtypeStruct((groups, rank, lanes), jnp.bfloat16),
        scratch_shapes=[
            pltpu.SMEM(slot.shape, slot.dtype),
            pltpu.VMEM(src.shape, src.dtype),
            pltpu.VMEM((groups * PACK, rank, span), interp.dtype),
            pltpu.SemaphoreType.DMA((pieces + 2,)),
        ],
        compiler_params=pltpu.CompilerParams(vmem_limit_bytes=int(limit * MIB)),
        cost_estimate=pl.CostEstimate(
            flops=2 * groups * lanes * rank * span,
            bytes_accessed=groups * PACK * rank * span * 2 + src.size * 2,
            transcendentals=0,
        ),
        name="interp",
    )(slot, src, interp, *after)


def load_body(levels, table_hbm, *rest):
    sems = rest[-1]
    loads = []
    for i, level in enumerate(levels):
        loads.append(pltpu.make_async_copy(table_hbm.at[level], rest[-1 - len(levels) + i], sems.at[i]))
        loads[-1].start()
    for load in loads:
        load.wait()


def load_call(limit, levels, tables, *after):
    shape = tables.shape[1:]
    return pl.pallas_call(
        functools.partial(load_body, levels),
        in_specs=[pl.BlockSpec(memory_space=pl.ANY)] * (1 + len(after)),
        out_specs=[pl.BlockSpec(memory_space=pltpu.VMEM)] * len(levels),
        out_shape=[jax.ShapeDtypeStruct(shape, tables.dtype)] * len(levels),
        scratch_shapes=[pltpu.SemaphoreType.DMA((len(levels),))],
        compiler_params=pltpu.CompilerParams(vmem_limit_bytes=int(limit * MIB)),
        cost_estimate=pl.CostEstimate(
            flops=0,
            bytes_accessed=len(levels) * shape[0] * shape[1] * shape[2] * 2,
            transcendentals=0,
        ),
        name="load",
    )(tables, *after)


def level_body(first, table_ref, own_ref, far_ref, *rest):
    out_ref = rest[-1]
    _, rank, both = table_ref.shape
    groups, _, lanes = own_ref.shape
    for grp in range(groups):
        at = (first + grp) * PACK
        block = table_ref[at : at + PACK].reshape(PACK * rank, both)
        pair = jnp.concatenate([own_ref[grp], far_ref[grp]], axis=0)
        wide = jnp.dot(block, pair, preferred_element_type=jnp.float32)
        out_ref[grp] = pick(wide, rank, lanes // PACK).astype(jnp.bfloat16)


def level_call(first, table, own, far, *after):
    groups, rank, lanes = own.shape
    both = table.shape[2]
    return pl.pallas_call(
        functools.partial(level_body, first),
        in_specs=[pl.BlockSpec(memory_space=pltpu.VMEM)] * 3
        + [pl.BlockSpec(memory_space=pl.ANY)] * len(after),
        out_specs=pl.BlockSpec(memory_space=pltpu.VMEM),
        out_shape=jax.ShapeDtypeStruct(own.shape, jnp.bfloat16),
        compiler_params=pltpu.CompilerParams(vmem_limit_bytes=VMEM_LIMIT),
        cost_estimate=pl.CostEstimate(
            flops=2 * groups * lanes * rank * both,
            bytes_accessed=groups * PACK * rank * both * 2,
            transcendentals=0,
        ),
        name="level",
    )(table, own, far, *after)


def eval_body(first, coeffs_ref, eval_ref, *rest):
    out_ref = rest[-1]
    _, rank, span = eval_ref.shape
    groups, _, lanes = coeffs_ref.shape
    rhs = lanes // PACK
    for grp in range(groups):
        mine = coeffs_ref[grp].astype(jnp.float32)
        twice = jnp.concatenate([mine, mine], axis=0).T.astype(jnp.bfloat16)
        left = jnp.concatenate([twice] * (PACK // 2), axis=1)
        row_box = lax.broadcasted_iota(jnp.int32, left.shape, 0) // rhs
        col_box = lax.broadcasted_iota(jnp.int32, left.shape, 1) // rank
        left = jnp.where(row_box == col_box, left, jnp.zeros_like(left))
        at = (first + grp) * PACK
        block = eval_ref[at : at + PACK].reshape(PACK * rank, span)
        vals = jnp.dot(left, block, preferred_element_type=jnp.float32)
        out_ref[at : at + PACK] = vals.astype(jnp.bfloat16).reshape(PACK, rhs, span)


def eval_call(first, coeffs, evaluate, *before):
    groups, rank, lanes = coeffs.shape
    boxes, _, span = evaluate.shape
    rhs = lanes // PACK
    return pl.pallas_call(
        functools.partial(eval_body, first),
        in_specs=[pl.BlockSpec(memory_space=pltpu.VMEM)] * (2 + len(before)),
        out_specs=pl.BlockSpec(memory_space=pltpu.VMEM),
        out_shape=jax.ShapeDtypeStruct((boxes, rhs, span), jnp.bfloat16),
        input_output_aliases={2: 0} if before else {},
        compiler_params=pltpu.CompilerParams(vmem_limit_bytes=VMEM_LIMIT),
        cost_estimate=pl.CostEstimate(
            flops=2 * groups * lanes * rank * span,
            bytes_accessed=groups * PACK * (rank + rhs) * span * 2,
            transcendentals=0,
        ),
        name="evaluate",
    )(coeffs, evaluate, *before)


def place_body(pieces, slot_ref, got_ref, *rest):
    out_hbm, out_ref, sems = rest[-3:]
    boxes, _, span = got_ref.shape
    per = boxes // pieces
    stores = []
    for piece in range(pieces):
        for box in range(piece * per, (piece + 1) * per):
            out_ref[:, box * span : (box + 1) * span] = got_ref[slot_ref[box]]
        at = pl.ds(piece * per * span, per * span)
        stores.append(
            pltpu.make_async_copy(out_ref.at[:, at], out_hbm.at[:, at], sems.at[piece])
        )
        stores[-1].start()
    for store in stores:
        store.wait()


def place_call(slot, got, *kept):
    pieces = 4
    boxes, rhs, span = got.shape
    shape = (rhs, boxes * span)
    return pl.pallas_call(
        functools.partial(place_body, pieces),
        in_specs=[
            pl.BlockSpec(memory_space=pltpu.SMEM),
            pl.BlockSpec(memory_space=pltpu.VMEM),
        ]
        + [pl.BlockSpec(memory_space=pl.ANY)] * len(kept),
        out_specs=pl.BlockSpec(memory_space=pl.ANY),
        out_shape=jax.ShapeDtypeStruct(shape, got.dtype),
        scratch_shapes=[
            pltpu.VMEM(shape, got.dtype),
            pltpu.SemaphoreType.DMA((pieces,)),
        ],
        compiler_params=pltpu.CompilerParams(vmem_limit_bytes=VMEM_LIMIT),
        cost_estimate=pl.CostEstimate(
            flops=0, bytes_accessed=4 * got.size, transcendentals=0
        ),
        name="place",
    )(slot, got, *kept)


def from_partner(value, axis, distance):
    mask = 2**distance
    pairs = [(source, source ^ mask) for source in range(lax.axis_size(axis))]
    return lax.ppermute(value, axis, pairs)


def local(sources, in_slot, interp, translate, evaluate, owner_slot):
    firsts = [sum(CHUNKS[:i]) for i in range(len(CHUNKS))]
    coeffs = []
    for limit, first, groups in zip(INTERP_LIMITS, firsts, CHUNKS):
        coeffs.append(interp_call(limit, first, groups, in_slot, sources, interp, *coeffs[-1:]))
    steps = [
        (axis, bit_pos)
        for axis in ("gz", "gy", "gx")
        for bit_pos in range(lax.axis_size(axis).bit_length() - 1)
    ]
    kept, held = [], []
    for level, (axis, bit_pos) in enumerate(steps):
        last = coeffs[-1]
        if level < len(LOADS):
            levels = range(len(held), len(held) + LOADS[level])
            held += load_call(LOAD_LIMITS[level], levels, translate, last)
        for i, first in enumerate(firsts):
            far = from_partner(coeffs[i], axis, bit_pos)
            kept += [coeffs[i], far]
            after = () if len(firsts) == 1 else (last,)
            last = coeffs[i] = level_call(first, held[level], coeffs[i], far, *after)
    values = ()
    for i, first in enumerate(firsts):
        values = (eval_call(first, coeffs[i], evaluate, *values),)
    moved = lax.all_to_all(values[0], AXES, split_axis=0, concat_axis=0, tiled=True)
    return place_call(owner_slot, moved, *(kept if KEEP else ()))


def solution(mesh):
    placed = (
        P(None, AXES),
        P(AXES),
        P(AXES, None, None),
        P(None, AXES, None, None),
        P(AXES, None, None),
        P(AXES),
    )
    return jax.shard_map(
        local, mesh=mesh, in_specs=placed, out_specs=P(None, AXES), check_vma=False
    )
```

time: 96.8 us -> 84.9 us (0.88)
  local copies, waits for them, and re-layouts: 10.3 us -> 0.67 us
  starting transfers between devices: 31 us -> 27.8 us
    unnamed x14 -> x6, local copies, waits for them, and re-layouts: 10.3 us -> 0.67 us
    ppermute x14, starting transfers between devices: 31 us -> 27.8 us  [from_partner(): return lax.ppermute(value, axis, pairs)]
    pallas_call x19 -> x22, Pallas kernels: 20.4 us -> 21 us  [the longest x3 7.36 us: load_call(): pl.pallas_call(functools.partial(load_body, levels), in_specs=[pl.BlockSp...]
  transfers between devices with their start and end apart: 14 -> 14, of which waited for: 7 -> 5; matrix products, arithmetic and copies ran while one was open for 0% -> 0% of each run, Pallas kernels for 15% -> 19%
where the time goes in v2:
time: 84.9 us; the launch traced here: 84.7 us
  blocking collectives  27.9 us (33%)
  starting transfers between devices  27.8 us (33%)
  Pallas kernels  21 us (25%)
  waiting for transfers between devices  7.08 us (8%)
    all_to_all x1, blocking collectives, local(): lax.all_to_all(values[0], AXES, split_axis=0, concat_axis=0, tiled=True)  27.9 us
    ppermute x14, starting transfers between devices, from_partner(): return lax.ppermute(value, axis, pairs)  27.8 us
    pallas_call x3, Pallas kernels, load_call(): pl.pallas_call(functools.partial(load_body, levels), in_specs=[pl.BlockSp...  7.36 us
    ppermute x14, waiting for transfers between devices, from_partner(): return lax.ppermute(value, axis, pairs)  7.08 us
    pallas_call x14, Pallas kernels, level_call(): pl.pallas_call(functools.partial(level_body, first), in_specs=[pl.BlockSp...  5.85 us
    pallas_call x2, Pallas kernels, interp_call(): pl.pallas_call(functools.partial(interp_body, first, groups, pieces), in_...  5.28 us
  transfers between devices with their start and end apart: 14, of which 5 were waited for; matrix products, arithmetic and copies ran while one was open for 0% of the time, Pallas kernels for 19%

profile of v2, /device:TPU:1, one launch (start us, length us, event | category | flops | bytes accessed | tf_op | source)
XLA Modules:
  0.0 84.7 jit_solution(3765384122904964285)
XLA Ops:
  0.0 0.7 copy-done.1
  0.7 2.6 %interp.2.rest_0_.own_ref = bf16[8,64,128]{2,1,0:T(8,128)(2,1)S(1)} custom-call(s32[128]{0:T(128)S(1)} %copy-done.1, bf16[16,32768]{1,0:T(8,128)(2,1)} %src_hbm.3, bf16[128,64,256]{2,1,0:T(8,128)(2,1)} %interp_hbm.3), custom_call_target="tpu_custom_call" | custom-call | flops 33554432 | bytes 3145728 | tf_op jit(solution)/shard_map/interp/pallas_call | solution.py:74
  3.3 2.5 %collective-permute-start.1 = (bf16[8,64,128]{2,1,0:T(8,128)(2,1)S(1)}, bf16[8,64,128]{2,1,0:T(8,128)(2,1)S(1)}, u32[]{:S(2)}, u32[]{:S(2)}) collective-permute-start(bf16[8,64,128]{2,1,0:T(8,128)(2,1)S(1)} %interp.2.rest_0_.own_ref), channel_id=1, source_target_pairs={{0,1},{1,0},{2,3},{3,2},{4,5},{5,4},{6,7},{7,6},{8,9},{9,8},{10,11... | collective-permute-start | bytes 393224 | tf_op jit(solution)/shard_map/ppermute | solution.py:237
  5.8 2.6 %interp.3.rest_0_.own_ref.rest_2_ = bf16[8,64,128]{2,1,0:T(8,128)(2,1)S(1)} custom-call(s32[128]{0:T(128)S(1)} %copy-done.1, bf16[16,32768]{1,0:T(8,128)(2,1)} %src_hbm.3, bf16[128,64,256]{2,1,0:T(8,128)(2,1)} %interp_hbm.3, bf16[8,64,128]{2,1,0:T(8,128)(2,1)S(1)} %interp.2.rest_0_.own_ref), custom_call_target="tpu_custom_call" | custom-call | flops 33554432 | bytes 3145728 | tf_op jit(solution)/shard_map/interp/pallas_call | solution.py:74
  8.5 0.1 collective-permute-start
  8.6 2.2 %load.3 = (bf16[128,64,128]{2,1,0:T(8,128)(2,1)S(1)}, bf16[128,64,128]{2,1,0:T(8,128)(2,1)S(1)}) custom-call(bf16[7,128,64,128]{3,2,1,0:T(8,128)(2,1)} %table_hbm.5, bf16[8,64,128]{2,1,0:T(8,128)(2,1)S(1)} %interp.3.rest_0_.own_ref.rest_2_), custom_call_target="tpu_custom_call" | custom-call | bytes 4194304 | tf_op jit(solution)/shard_map/load/pallas_call | solution.py:107
  10.8 0.0 collective-permute-done.1.far_ref.rest_1_
  10.9 0.4 level.14.rest_0_.own_ref.rest_4_
  11.3 3.5 %collective-permute-start.3 = (bf16[8,64,128]{2,1,0:T(8,128)(2,1)S(1)}, bf16[8,64,128]{2,1,0:T(8,128)(2,1)S(1)}, u32[]{:S(2)}, u32[]{:S(2)}) collective-permute-start(bf16[8,64,128]{2,1,0:T(8,128)(2,1)S(1)} %level.14.rest_0_.own_ref.rest_4_), channel_id=1, source_target_pairs={{0,2},{1,3},{2,0},{3,1},{4,6},{5,7},{6,4},{7,5},{8,10},{9,11},{10,... | collective-permute-start | bytes 393224 | tf_op jit(solution)/shard_map/ppermute | solution.py:237
  14.8 0.0 collective-permute-done.far_ref.rest_3_
  14.8 0.4 level.15.rest_0_.own_ref.rest_6_
  15.2 1.0 %collective-permute-start.2 = (bf16[8,64,128]{2,1,0:T(8,128)(2,1)S(1)}, bf16[8,64,128]{2,1,0:T(8,128)(2,1)S(1)}, u32[]{:S(2)}, u32[]{:S(2)}) collective-permute-start(bf16[8,64,128]{2,1,0:T(8,128)(2,1)S(1)} %level.15.rest_0_.own_ref.rest_6_), channel_id=1, source_target_pairs={{0,2},{1,3},{2,0},{3,1},{4,6},{5,7},{6,4},{7,5},{8,10},{9,11},{10,... | collective-permute-start | bytes 393224 | tf_op jit(solution)/shard_map/ppermute | solution.py:237
  16.2 1.0 %collective-permute-done.3.far_ref.rest_5_ = bf16[8,64,128]{2,1,0:T(8,128)(2,1)S(1)} collective-permute-done((bf16[8,64,128]{2,1,0:T(8,128)(2,1)S(1)}, bf16[8,64,128]{2,1,0:T(8,128)(2,1)S(1)}, u32[]{:S(2)}, u32[]{:S(2)}) %collective-permute-start.3) | collective-permute-done | bytes 131104 | tf_op jit(solution)/shard_map/ppermute | solution.py:237
  17.2 0.4 level.16.rest_0_.own_ref.rest_8_
  17.6 2.8 %collective-permute-start.5 = (bf16[8,64,128]{2,1,0:T(8,128)(2,1)S(1)}, bf16[8,64,128]{2,1,0:T(8,128)(2,1)S(1)}, u32[]{:S(2)}, u32[]{:S(2)}) collective-permute-start(bf16[8,64,128]{2,1,0:T(8,128)(2,1)S(1)} %level.16.rest_0_.own_ref.rest_8_), channel_id=1, source_target_pairs={{0,4},{1,5},{2,6},{3,7},{4,0},{5,1},{6,2},{7,3},{8,12},{9,13},{10,... | collective-permute-start | bytes 393224 | tf_op jit(solution)/shard_map/ppermute | solution.py:237
  20.4 0.2 collective-permute-done.2.far_ref.rest_7_
  20.6 0.4 level.17.rest_0_.own_ref.rest_10_
  21.0 2.8 %collective-permute-start.4 = (bf16[8,64,128]{2,1,0:T(8,128)(2,1)S(1)}, bf16[8,64,128]{2,1,0:T(8,128)(2,1)S(1)}, u32[]{:S(2)}, u32[]{:S(2)}) collective-permute-start(bf16[8,64,128]{2,1,0:T(8,128)(2,1)S(1)} %level.17.rest_0_.own_ref.rest_10_), channel_id=1, source_target_pairs={{0,4},{1,5},{2,6},{3,7},{4,0},{5,1},{6,2},{7,3},{8,12},{9,13},{10,... | collective-permute-start | bytes 393224 | tf_op jit(solution)/shard_map/ppermute | solution.py:237
  23.9 2.2 %load.5 = (bf16[128,64,128]{2,1,0:T(8,128)(2,1)S(1)}, bf16[128,64,128]{2,1,0:T(8,128)(2,1)S(1)}) custom-call(bf16[7,128,64,128]{3,2,1,0:T(8,128)(2,1)} %table_hbm.5, bf16[8,64,128]{2,1,0:T(8,128)(2,1)S(1)} %level.15.rest_0_.own_ref.rest_6_), custom_call_target="tpu_custom_call" | custom-call | bytes 4194304 | tf_op jit(solution)/shard_map/load/pallas_call | solution.py:107
  26.1 0.4 level.18.rest_0_.own_ref.rest_12_
  26.5 1.4 %collective-permute-start.7 = (bf16[8,64,128]{2,1,0:T(8,128)(2,1)S(1)}, bf16[8,64,128]{2,1,0:T(8,128)(2,1)S(1)}, u32[]{:S(2)}, u32[]{:S(2)}) collective-permute-start(bf16[8,64,128]{2,1,0:T(8,128)(2,1)S(1)} %level.18.rest_0_.own_ref.rest_12_), channel_id=1, source_target_pairs={{0,8},{8,0},{16,24},{24,16},{1,9},{9,1},{17,25},{25,17},{2,10},{10... | collective-permute-start | bytes 393224 | tf_op jit(solution)/shard_map/ppermute | solution.py:237
  27.9 0.0 collective-permute-done.4.far_ref.rest_11_
  27.9 0.4 level.19.rest_0_.own_ref.rest_14_
  28.3 1.1 %collective-permute-start.6 = (bf16[8,64,128]{2,1,0:T(8,128)(2,1)S(1)}, bf16[8,64,128]{2,1,0:T(8,128)(2,1)S(1)}, u32[]{:S(2)}, u32[]{:S(2)}) collective-permute-start(bf16[8,64,128]{2,1,0:T(8,128)(2,1)S(1)} %level.19.rest_0_.own_ref.rest_14_), channel_id=1, source_target_pairs={{0,8},{8,0},{16,24},{24,16},{1,9},{9,1},{17,25},{25,17},{2,10},{10... | collective-permute-start | bytes 393224 | tf_op jit(solution)/shard_map/ppermute | solution.py:237
  29.5 1.0 %collective-permute-done.7.far_ref.rest_13_ = bf16[8,64,128]{2,1,0:T(8,128)(2,1)S(1)} collective-permute-done((bf16[8,64,128]{2,1,0:T(8,128)(2,1)S(1)}, bf16[8,64,128]{2,1,0:T(8,128)(2,1)S(1)}, u32[]{:S(2)}, u32[]{:S(2)}) %collective-permute-start.7) | collective-permute-done | bytes 131104 | tf_op jit(solution)/shard_map/ppermute | solution.py:237
  30.4 0.4 level.20.rest_0_.own_ref.rest_16_
  30.9 3.0 %collective-permute-start.9 = (bf16[8,64,128]{2,1,0:T(8,128)(2,1)S(1)}, bf16[8,64,128]{2,1,0:T(8,128)(2,1)S(1)}, u32[]{:S(2)}, u32[]{:S(2)}) collective-permute-start(bf16[8,64,128]{2,1,0:T(8,128)(2,1)S(1)} %level.20.rest_0_.own_ref.rest_16_), channel_id=1, source_target_pairs={{0,16},{8,24},{16,0},{24,8},{1,17},{9,25},{17,1},{25,9},{2,18},{10... | collective-permute-start | bytes 393224 | tf_op jit(solution)/shard_map/ppermute | solution.py:237
  33.9 0.4 level.21.rest_0_.own_ref.rest_18_
  34.3 1.1 %collective-permute-start.8 = (bf16[8,64,128]{2,1,0:T(8,128)(2,1)S(1)}, bf16[8,64,128]{2,1,0:T(8,128)(2,1)S(1)}, u32[]{:S(2)}, u32[]{:S(2)}) collective-permute-start(bf16[8,64,128]{2,1,0:T(8,128)(2,1)S(1)} %level.21.rest_0_.own_ref.rest_18_), channel_id=1, source_target_pairs={{0,16},{8,24},{16,0},{24,8},{1,17},{9,25},{17,1},{25,9},{2,18},{10... | collective-permute-start | bytes 393224 | tf_op jit(solution)/shard_map/ppermute | solution.py:237
  35.4 2.9 %load.4 = (bf16[128,64,128]{2,1,0:T(8,128)(2,1)S(1)}, bf16[128,64,128]{2,1,0:T(8,128)(2,1)S(1)}, bf16[128,64,128]{2,1,0:T(8,128)(2,1)S(1)}) custom-call(bf16[7,128,64,128]{3,2,1,0:T(8,128)(2,1)} %table_hbm.5, bf16[8,64,128]{2,1,0:T(8,128)(2,1)S(1)} %level.17.rest_0_.own_ref.rest_10_), custom_call_target="tpu_custom_call" | custom-call | bytes 6291456 | tf_op jit(solution)/shard_map/load/pallas_call | solution.py:107
  38.3 0.4 level.22.rest_0_.own_ref.rest_20_
  38.8 5.9 %collective-permute-start.11 = (bf16[8,64,128]{2,1,0:T(8,128)(2,1)S(1)}, bf16[8,64,128]{2,1,0:T(8,128)(2,1)S(1)}, u32[]{:S(2)}, u32[]{:S(2)}) collective-permute-start(bf16[8,64,128]{2,1,0:T(8,128)(2,1)S(1)} %level.22.rest_0_.own_ref.rest_20_), channel_id=1, source_target_pairs={{0,32},{32,0},{64,96},{96,64},{1,33},{33,1},{65,97},{97,65},{2,34}... | collective-permute-start | bytes 393224 | tf_op jit(solution)/shard_map/ppermute | solution.py:237
  44.7 0.4 level.23.rest_0_.own_ref.rest_22_
  45.1 0.8 collective-permute-start.10
  45.9 0.4 level.24.rest_0_.own_ref.rest_24_
  46.3 0.0 copy-start
  46.3 0.8 collective-permute-start.13
  47.2 0.4 level.25.rest_0_.own_ref.rest_26_
  47.6 0.8 collective-permute-start.12
  48.4 3.1 %collective-permute-done.13.far_ref.rest_25_ = bf16[8,64,128]{2,1,0:T(8,128)(2,1)S(1)} collective-permute-done((bf16[8,64,128]{2,1,0:T(8,128)(2,1)S(1)}, bf16[8,64,128]{2,1,0:T(8,128)(2,1)S(1)}, u32[]{:S(2)}, u32[]{:S(2)}) %collective-permute-start.13) | collective-permute-done | bytes 131104 | tf_op jit(solution)/shard_map/ppermute | solution.py:237
  51.5 0.4 level.26.rest_0_.coeffs_ref
  51.9 0.5 evaluate.2.rest_0_
  52.4 1.9 %collective-permute-done.12.far_ref.rest_27_ = bf16[8,64,128]{2,1,0:T(8,128)(2,1)S(1)} collective-permute-done((bf16[8,64,128]{2,1,0:T(8,128)(2,1)S(1)}, bf16[8,64,128]{2,1,0:T(8,128)(2,1)S(1)}, u32[]{:S(2)}, u32[]{:S(2)}) %collective-permute-start.12) | collective-permute-done | bytes 131104 | tf_op jit(solution)/shard_map/ppermute | solution.py:237
  54.3 0.4 level.27.coeffs_ref
  54.7 0.5 evaluate.3
  55.2 0.0 copy-start.2
  55.2 27.9 %all_to_all.5.got_ref = bf16[128,16,256]{2,1,0:T(8,128)(2,1)S(1)} all-to-all(bf16[128,16,256]{2,1,0:T(8,128)(2,1)S(1)} %evaluate.3), channel_id=1, replica_groups=mesh['gx'=4,'gy'=4,'gz'=8] {'gx','gy','gz'}, dimensions={0} | all-to-all | bytes 2097152 | tf_op jit(solution)/shard_map/all_to_all | solution.py:264
  83.1 1.6 %place.1 = bf16[16,32768]{1,0:T(8,128)(2,1)} custom-call(s32[128]{0:T(128)S(1)} %copy-done.2, bf16[128,16,256]{2,1,0:T(8,128)(2,1)S(1)} %all_to_all.5.got_ref, bf16[8,64,128]{2,1,0:T(8,128)(2,1)S(1)} %interp.2.rest_0_.own_ref, bf16[8,64,128]{2,1,0:T(8,128)(2,1)S(1)} %collective-permute-done.1.far_ref.rest_1_, ...), custom_call_target="tpu_custom_call" | custom-call | bytes 2097152 | tf_op jit(solution)/shard_map/place/pallas_call | solution.py:213
  (9 shorter events, 0.0 us)
Async XLA Ops:
  0.0 0.7 copy-start.1
  3.3 7.5 %collective-permute-start.1 = (bf16[8,64,128]{2,1,0:T(8,128)(2,1)S(1)}, bf16[8,64,128]{2,1,0:T(8,128)(2,1)S(1)}, u32[]{:S(2)}, u32[]{:S(2)}) collective-permute-start(bf16[8,64,128]{2,1,0:T(8,128)(2,1)S(1)} %interp.2.rest_0_.own_ref), channel_id=1, source_target_pairs={{0,1},{1,0},{2,3},{3,2},{4,5},{5,4},{6,7},{7,6},{8,9},{9,8},{10,11... | collective-permute-start | bytes 393224 | tf_op jit(solution)/shard_map/ppermute | solution.py:237
  8.5 6.3 %collective-permute-start = (bf16[8,64,128]{2,1,0:T(8,128)(2,1)S(1)}, bf16[8,64,128]{2,1,0:T(8,128)(2,1)S(1)}, u32[]{:S(2)}, u32[]{:S(2)}) collective-permute-start(bf16[8,64,128]{2,1,0:T(8,128)(2,1)S(1)} %interp.3.rest_0_.own_ref.rest_2_), channel_id=1, source_target_pairs={{0,1},{1,0},{2,3},{3,2},{4,5},{5,4},{6,7},{7,6},{8,9},{9,8},{10,11... | collective-permute-start | bytes 393224 | tf_op jit(solution)/shard_map/ppermute | solution.py:237
  11.3 5.9 %collective-permute-start.3 = (bf16[8,64,128]{2,1,0:T(8,128)(2,1)S(1)}, bf16[8,64,128]{2,1,0:T(8,128)(2,1)S(1)}, u32[]{:S(2)}, u32[]{:S(2)}) collective-permute-start(bf16[8,64,128]{2,1,0:T(8,128)(2,1)S(1)} %level.14.rest_0_.own_ref.rest_4_), channel_id=1, source_target_pairs={{0,2},{1,3},{2,0},{3,1},{4,6},{5,7},{6,4},{7,5},{8,10},{9,11},{10,... | collective-permute-start | bytes 393224 | tf_op jit(solution)/shard_map/ppermute | solution.py:237
  15.2 5.4 %collective-permute-start.2 = (bf16[8,64,128]{2,1,0:T(8,128)(2,1)S(1)}, bf16[8,64,128]{2,1,0:T(8,128)(2,1)S(1)}, u32[]{:S(2)}, u32[]{:S(2)}) collective-permute-start(bf16[8,64,128]{2,1,0:T(8,128)(2,1)S(1)} %level.15.rest_0_.own_ref.rest_6_), channel_id=1, source_target_pairs={{0,2},{1,3},{2,0},{3,1},{4,6},{5,7},{6,4},{7,5},{8,10},{9,11},{10,... | collective-permute-start | bytes 393224 | tf_op jit(solution)/shard_map/ppermute | solution.py:237
  17.6 8.5 %collective-permute-start.5 = (bf16[8,64,128]{2,1,0:T(8,128)(2,1)S(1)}, bf16[8,64,128]{2,1,0:T(8,128)(2,1)S(1)}, u32[]{:S(2)}, u32[]{:S(2)}) collective-permute-start(bf16[8,64,128]{2,1,0:T(8,128)(2,1)S(1)} %level.16.rest_0_.own_ref.rest_8_), channel_id=1, source_target_pairs={{0,4},{1,5},{2,6},{3,7},{4,0},{5,1},{6,2},{7,3},{8,12},{9,13},{10,... | collective-permute-start | bytes 393224 | tf_op jit(solution)/shard_map/ppermute | solution.py:237
  21.0 6.9 %collective-permute-start.4 = (bf16[8,64,128]{2,1,0:T(8,128)(2,1)S(1)}, bf16[8,64,128]{2,1,0:T(8,128)(2,1)S(1)}, u32[]{:S(2)}, u32[]{:S(2)}) collective-permute-start(bf16[8,64,128]{2,1,0:T(8,128)(2,1)S(1)} %level.17.rest_0_.own_ref.rest_10_), channel_id=1, source_target_pairs={{0,4},{1,5},{2,6},{3,7},{4,0},{5,1},{6,2},{7,3},{8,12},{9,13},{10,... | collective-permute-start | bytes 393224 | tf_op jit(solution)/shard_map/ppermute | solution.py:237
  26.5 3.9 %collective-permute-start.7 = (bf16[8,64,128]{2,1,0:T(8,128)(2,1)S(1)}, bf16[8,64,128]{2,1,0:T(8,128)(2,1)S(1)}, u32[]{:S(2)}, u32[]{:S(2)}) collective-permute-start(bf16[8,64,128]{2,1,0:T(8,128)(2,1)S(1)} %level.18.rest_0_.own_ref.rest_12_), channel_id=1, source_target_pairs={{0,8},{8,0},{16,24},{24,16},{1,9},{9,1},{17,25},{25,17},{2,10},{10... | collective-permute-start | bytes 393224 | tf_op jit(solution)/shard_map/ppermute | solution.py:237
  28.3 5.5 %collective-permute-start.6 = (bf16[8,64,128]{2,1,0:T(8,128)(2,1)S(1)}, bf16[8,64,128]{2,1,0:T(8,128)(2,1)S(1)}, u32[]{:S(2)}, u32[]{:S(2)}) collective-permute-start(bf16[8,64,128]{2,1,0:T(8,128)(2,1)S(1)} %level.19.rest_0_.own_ref.rest_14_), channel_id=1, source_target_pairs={{0,8},{8,0},{16,24},{24,16},{1,9},{9,1},{17,25},{25,17},{2,10},{10... | collective-permute-start | bytes 393224 | tf_op jit(solution)/shard_map/ppermute | solution.py:237
  30.9 7.5 %collective-permute-start.9 = (bf16[8,64,128]{2,1,0:T(8,128)(2,1)S(1)}, bf16[8,64,128]{2,1,0:T(8,128)(2,1)S(1)}, u32[]{:S(2)}, u32[]{:S(2)}) collective-permute-start(bf16[8,64,128]{2,1,0:T(8,128)(2,1)S(1)} %level.20.rest_0_.own_ref.rest_16_), channel_id=1, source_target_pairs={{0,16},{8,24},{16,0},{24,8},{1,17},{9,25},{17,1},{25,9},{2,18},{10... | collective-permute-start | bytes 393224 | tf_op jit(solution)/shard_map/ppermute | solution.py:237
  34.3 10.4 %collective-permute-start.8 = (bf16[8,64,128]{2,1,0:T(8,128)(2,1)S(1)}, bf16[8,64,128]{2,1,0:T(8,128)(2,1)S(1)}, u32[]{:S(2)}, u32[]{:S(2)}) collective-permute-start(bf16[8,64,128]{2,1,0:T(8,128)(2,1)S(1)} %level.21.rest_0_.own_ref.rest_18_), channel_id=1, source_target_pairs={{0,16},{8,24},{16,0},{24,8},{1,17},{9,25},{17,1},{25,9},{2,18},{10... | collective-permute-start | bytes 393224 | tf_op jit(solution)/shard_map/ppermute | solution.py:237
  38.8 7.2 %collective-permute-start.11 = (bf16[8,64,128]{2,1,0:T(8,128)(2,1)S(1)}, bf16[8,64,128]{2,1,0:T(8,128)(2,1)S(1)}, u32[]{:S(2)}, u32[]{:S(2)}) collective-permute-start(bf16[8,64,128]{2,1,0:T(8,128)(2,1)S(1)} %level.22.rest_0_.own_ref.rest_20_), channel_id=1, source_target_pairs={{0,32},{32,0},{64,96},{96,64},{1,33},{33,1},{65,97},{97,65},{2,34}... | collective-permute-start | bytes 393224 | tf_op jit(solution)/shard_map/ppermute | solution.py:237
  45.1 2.1 %collective-permute-start.10 = (bf16[8,64,128]{2,1,0:T(8,128)(2,1)S(1)}, bf16[8,64,128]{2,1,0:T(8,128)(2,1)S(1)}, u32[]{:S(2)}, u32[]{:S(2)}) collective-permute-start(bf16[8,64,128]{2,1,0:T(8,128)(2,1)S(1)} %level.23.rest_0_.own_ref.rest_22_), channel_id=1, source_target_pairs={{0,32},{32,0},{64,96},{96,64},{1,33},{33,1},{65,97},{97,65},{2,34}... | collective-permute-start | bytes 393224 | tf_op jit(solution)/shard_map/ppermute | solution.py:237
  46.3 5.6 %copy-start = (bf16[128,64,256]{2,1,0:T(8,128)(2,1)S(1)}, bf16[128,64,256]{2,1,0:T(8,128)(2,1)}, u32[]{:S(2)}) copy-start(bf16[128,64,256]{2,1,0:T(8,128)(2,1)} %eval_ref.3) | copy-start | bytes 12582916
  46.3 5.1 %collective-permute-start.13 = (bf16[8,64,128]{2,1,0:T(8,128)(2,1)S(1)}, bf16[8,64,128]{2,1,0:T(8,128)(2,1)S(1)}, u32[]{:S(2)}, u32[]{:S(2)}) collective-permute-start(bf16[8,64,128]{2,1,0:T(8,128)(2,1)S(1)} %level.24.rest_0_.own_ref.rest_24_), channel_id=1, source_target_pairs={{0,64},{32,96},{64,0},{96,32},{1,65},{33,97},{65,1},{97,33},{2,66}... | collective-permute-start | bytes 393224 | tf_op jit(solution)/shard_map/ppermute | solution.py:237
  47.6 6.7 %collective-permute-start.12 = (bf16[8,64,128]{2,1,0:T(8,128)(2,1)S(1)}, bf16[8,64,128]{2,1,0:T(8,128)(2,1)S(1)}, u32[]{:S(2)}, u32[]{:S(2)}) collective-permute-start(bf16[8,64,128]{2,1,0:T(8,128)(2,1)S(1)} %level.25.rest_0_.own_ref.rest_26_), channel_id=1, source_target_pairs={{0,64},{32,96},{64,0},{96,32},{1,65},{33,97},{65,1},{97,33},{2,66}... | collective-permute-start | bytes 393224 | tf_op jit(solution)/shard_map/ppermute | solution.py:237
  55.2 27.9 %copy-start.2 = (s32[128]{0:T(128)S(1)}, s32[128]{0:T(128)}, u32[]{:S(2)}) copy-start(s32[128]{0:T(128)} %slot_ref.1) | copy-start | bytes 1540

commit v3 on v2

v3 whole, which is shorter than its diff:
```python
import functools
import itertools

import jax
import jax.numpy as jnp
import numpy as np
from jax import lax
from jax.experimental import pallas as pl
from jax.experimental.pallas import tpu as pltpu
from jax.sharding import PartitionSpec as P

AXES = ("gx", "gy", "gz")
PACK = 8
CHUNKS = (8, 8)
LOADS = {0: 2, 1: 1, 2: 1, 3: 2, 6: 1}
PIECES = 4
ORDER = (1, 2, 3, 0, 4)
SPLIT = (2, 2, 4, 2, 4)
MIB = 2**20
FREE = pl.CostEstimate(flops=0, bytes_accessed=0, transcendentals=0)
VMEM_LIMIT = 16 * MIB
INTERP_LIMIT = int(53.25 * MIB)
LOAD_LIMIT = 38 * MIB


def own_lanes(shape, cols):
    return lax.broadcasted_iota(jnp.int32, shape, 1) // cols


def pick(wide, rank, cols):
    lane_box = own_lanes((rank, PACK * cols), cols)
    out = wide[:rank]
    for box in range(1, PACK):
        out = jnp.where(lane_box == box, wide[box * rank : (box + 1) * rank], out)
    return out


def interp_body(firsts, slot_hbm, src_hbm, interp_hbm, *rest):
    *out_refs, slot_ref, src_ref, interp_ref, sems = rest
    boxes, rank, span = interp_ref.shape
    rhs = src_ref.shape[0]
    per = boxes // PIECES
    ready = [
        pltpu.make_async_copy(slot_hbm, slot_ref, sems.at[0]),
        pltpu.make_async_copy(src_hbm, src_ref, sems.at[1]),
    ]
    loads = []
    for piece in range(PIECES):
        at = pl.ds(piece * per, per)
        loads.append(
            pltpu.make_async_copy(interp_hbm.at[at], interp_ref.at[at], sems.at[2 + piece])
        )
    for copy in ready + loads:
        copy.start()
    for copy in ready:
        copy.wait()
    for first, out_ref in zip(firsts, out_refs):
        for grp in range(out_ref.shape[0]):
            base = (first + grp) * PACK
            slabs = []
            for box in range(PACK):
                at = pl.multiple_of(slot_ref[base + box] * span, span)
                slabs.append(src_ref[:, pl.ds(at, span)])
            inputs = jnp.concatenate(slabs, axis=0)
            if base % per == 0:
                loads[base // per].wait()
            block = interp_ref[base : base + PACK].reshape(PACK * rank, span)
            wide = lax.dot_general(
                block, inputs, (((1,), (1,)), ((), ())), preferred_element_type=jnp.float32
            )
            out_ref[grp] = pick(wide, rank, rhs).astype(jnp.bfloat16)


def interp_call(firsts, slot, src, interp):
    _, rank, span = interp.shape
    lanes = PACK * src.shape[0]
    return pl.pallas_call(
        functools.partial(interp_body, firsts),
        in_specs=[pl.BlockSpec(memory_space=pl.ANY)] * 3,
        out_specs=[pl.BlockSpec(memory_space=pltpu.VMEM)] * len(firsts),
        out_shape=[
            jax.ShapeDtypeStruct((groups, rank, lanes), jnp.bfloat16) for groups in CHUNKS
        ],
        scratch_shapes=[
            pltpu.SMEM(slot.shape, slot.dtype),
            pltpu.VMEM(src.shape, src.dtype),
            pltpu.VMEM(interp.shape, interp.dtype),
            pltpu.SemaphoreType.DMA((2 + PIECES,)),
        ],
        compiler_params=pltpu.CompilerParams(vmem_limit_bytes=INTERP_LIMIT),
        cost_estimate=FREE,
        name="interp",
    )(slot, src, interp)


def load_body(levels, whole, table_hbm, *rest):
    sems = rest[-1]
    loaded = rest[whole + 1 : -1]
    sources = [table_hbm.at[level] for level in levels] + list(rest[:whole])
    loads = [
        pltpu.make_async_copy(source, target, sems.at[i])
        for i, (source, target) in enumerate(zip(sources, loaded))
    ]
    for copy in loads:
        copy.start()
    for copy in loads:
        copy.wait()


def load_call(levels, tables, whole, after):
    outs = [jax.ShapeDtypeStruct(tables.shape[1:], tables.dtype)] * len(levels)
    outs += [jax.ShapeDtypeStruct(array.shape, array.dtype) for array in whole]
    return pl.pallas_call(
        functools.partial(load_body, levels, len(whole)),
        in_specs=[pl.BlockSpec(memory_space=pl.ANY)] * (2 + len(whole)),
        out_specs=[pl.BlockSpec(memory_space=pltpu.VMEM)] * len(outs),
        out_shape=outs,
        scratch_shapes=[pltpu.SemaphoreType.DMA((len(outs),))],
        compiler_params=pltpu.CompilerParams(vmem_limit_bytes=LOAD_LIMIT),
        cost_estimate=FREE,
        name="load",
    )(tables, *whole, after)


def level_body(first, table_ref, own_ref, far_ref, *rest):
    out_ref = rest[-1]
    _, rank, both = table_ref.shape
    groups, _, lanes = own_ref.shape
    for grp in range(groups):
        at = (first + grp) * PACK
        block = table_ref[at : at + PACK].reshape(PACK * rank, both)
        pair = jnp.concatenate([own_ref[grp], far_ref[grp]], axis=0)
        wide = jnp.dot(block, pair, preferred_element_type=jnp.float32)
        out_ref[grp] = pick(wide, rank, lanes // PACK).astype(jnp.bfloat16)


def level_call(first, table, own, far, *after):
    groups, rank, lanes = own.shape
    both = table.shape[2]
    return pl.pallas_call(
        functools.partial(level_body, first),
        in_specs=[pl.BlockSpec(memory_space=pltpu.VMEM)] * 3
        + [pl.BlockSpec(memory_space=pl.ANY)] * len(after),
        out_specs=pl.BlockSpec(memory_space=pltpu.VMEM),
        out_shape=jax.ShapeDtypeStruct(own.shape, jnp.bfloat16),
        compiler_params=pltpu.CompilerParams(vmem_limit_bytes=VMEM_LIMIT),
        cost_estimate=FREE,
        name="level",
    )(table, own, far, *after)


def eval_body(first, place_of, coeffs_ref, eval_ref, *rest):
    out_ref = rest[-1]
    _, rank, span = eval_ref.shape
    groups, _, lanes = coeffs_ref.shape
    rhs = lanes // PACK
    for grp in range(groups):
        mine = coeffs_ref[grp].astype(jnp.float32)
        twice = jnp.concatenate([mine, mine], axis=0).T.astype(jnp.bfloat16)
        left = jnp.concatenate([twice] * (PACK // 2), axis=1)
        row_box = lax.broadcasted_iota(jnp.int32, left.shape, 0) // rhs
        col_box = lax.broadcasted_iota(jnp.int32, left.shape, 1) // rank
        left = jnp.where(row_box == col_box, left, jnp.zeros_like(left))
        at = (first + grp) * PACK
        block = eval_ref[at : at + PACK].reshape(PACK * rank, span)
        vals = jnp.dot(left, block, preferred_element_type=jnp.float32)
        for box in range(PACK):
            mine = vals[box * rhs : (box + 1) * rhs]
            out_ref[place_of[at + box]] = mine.astype(jnp.bfloat16)


def eval_call(first, place_of, coeffs, evaluate, *before):
    groups, rank, lanes = coeffs.shape
    boxes, _, span = evaluate.shape
    rhs = lanes // PACK
    return pl.pallas_call(
        functools.partial(eval_body, first, place_of),
        in_specs=[pl.BlockSpec(memory_space=pltpu.VMEM)] * (2 + len(before)),
        out_specs=pl.BlockSpec(memory_space=pltpu.VMEM),
        out_shape=jax.ShapeDtypeStruct((boxes, rhs, span), jnp.bfloat16),
        input_output_aliases={2: 0} if before else {},
        compiler_params=pltpu.CompilerParams(vmem_limit_bytes=VMEM_LIMIT),
        cost_estimate=FREE,
        name="evaluate",
    )(coeffs, evaluate, *before)


def bits_by_shift():
    widths = [size.bit_length() - 1 for size in SPLIT]
    old = {axis: sum(widths[axis + 1 :]) for axis in range(len(SPLIT))}
    masks = {}
    for at, axis in enumerate(ORDER):
        new = sum(widths[later] for later in ORDER[at + 1 :])
        shift = new - old[axis]
        masks[shift] = masks.get(shift, 0) | (SPLIT[axis] - 1) << new
    return sorted(masks.items())


def place_of_device(device):
    place = 0
    for shift, mask in bits_by_shift():
        moved = device << shift if shift >= 0 else device >> -shift
        place = place | (moved & mask)
    return place


def place_body(pieces, slot_ref, got_ref, *rest):
    out_hbm, out_ref, sems = rest[-3:]
    boxes, _, span = got_ref.shape
    per = boxes // pieces
    stores = []
    for piece in range(pieces):
        for box in range(piece * per, (piece + 1) * per):
            out_ref[:, box * span : (box + 1) * span] = got_ref[place_of_device(slot_ref[box])]
        at = pl.ds(piece * per * span, per * span)
        stores.append(
            pltpu.make_async_copy(out_ref.at[:, at], out_hbm.at[:, at], sems.at[piece])
        )
        stores[-1].start()
    for store in stores:
        store.wait()


def place_call(slot, got):
    pieces = 4
    boxes, rhs, span = got.shape
    shape = (rhs, boxes * span)
    return pl.pallas_call(
        functools.partial(place_body, pieces),
        in_specs=[
            pl.BlockSpec(memory_space=pltpu.SMEM),
            pl.BlockSpec(memory_space=pltpu.VMEM),
        ],
        out_specs=pl.BlockSpec(memory_space=pl.ANY),
        out_shape=jax.ShapeDtypeStruct(shape, got.dtype),
        scratch_shapes=[
            pltpu.VMEM(shape, got.dtype),
            pltpu.SemaphoreType.DMA((pieces,)),
        ],
        compiler_params=pltpu.CompilerParams(vmem_limit_bytes=VMEM_LIMIT),
        cost_estimate=FREE,
        name="place",
    )(slot, got)


def from_partner(value, axis, distance):
    mask = 2**distance
    pairs = [(source, source ^ mask) for source in range(lax.axis_size(axis))]
    return lax.ppermute(value, axis, pairs)


def local(sources, in_slot, interp, translate, evaluate, owner_slot):
    firsts = [sum(CHUNKS[:i]) for i in range(len(CHUNKS))]
    coeffs = list(interp_call(firsts, in_slot, sources, interp))
    held = []
    steps = [
        (axis, bit_pos)
        for axis in ("gz", "gy", "gx")
        for bit_pos in range(lax.axis_size(axis).bit_length() - 1)
    ]
    tables = {}
    last = coeffs[-1]
    for level, i in itertools.product(range(len(steps)), range(len(firsts))):
        axis, bit_pos = steps[level]
        if i == 0:
            more = ()
            if level in LOADS:
                levels = range(len(held), len(held) + LOADS[level])
                final = level == len(steps) - 1
                more = load_call(levels, translate, [evaluate] * final, coeffs[-1])
                held += more[: len(levels)]
                if final:
                    evaluate = more[-1]
            tables[level] = more[:1]
        far = from_partner(coeffs[i], axis, bit_pos)
        last = coeffs[i] = level_call(
            firsts[i], held[level], coeffs[i], far, last, *tables[level]
        )
    devices = np.arange(int(np.prod(SPLIT))).reshape(SPLIT).transpose(ORDER).reshape(-1)
    group = [int(device) for device in devices]
    place_of = [int(at) for at in np.argsort(devices)]
    values = ()
    for i, first in enumerate(firsts):
        values = (eval_call(first, place_of, coeffs[i], evaluate, *values),)
    moved = lax.all_to_all(
        values[0], AXES, split_axis=0, concat_axis=0, axis_index_groups=[group], tiled=True
    )
    return place_call(owner_slot, moved)


def solution(mesh):
    placed = (
        P(None, AXES),
        P(AXES),
        P(AXES, None, None),
        P(None, AXES, None, None),
        P(AXES, None, None),
        P(AXES),
    )
    return jax.shard_map(
        local, mesh=mesh, in_specs=placed, out_specs=P(None, AXES), check_vma=False
    )
```

time: 84.9 us -> 82.5 us (0.972)
  blocking collectives: 27.9 us -> 24.4 us
  waiting for transfers between devices: 7.08 us -> 9.28 us
  starting transfers between devices: 27.8 us -> 26.6 us
    all_to_all x1, blocking collectives: 27.9 us -> 24.4 us  [local(): lax.all_to_all(values[0], AXES, split_axis=0, concat_axis=0, axis_index_g...]
    ppermute x14, waiting for transfers between devices: 7.08 us -> 9.28 us  [from_partner(): return lax.ppermute(value, axis, pairs)]
    ppermute x14, starting transfers between devices: 27.8 us -> 26.6 us  [from_partner(): return lax.ppermute(value, axis, pairs)]
    pallas_call x7 -> x8, Pallas kernels: 13.6 us -> 13.6 us  [the longest x5 9.28 us: load_call(): pl.pallas_call(functools.partial(load_body, levels, len(whole)), in_specs...]
  transfers between devices with their start and end apart: 14 -> 14, of which waited for: 5 -> 7; matrix products, arithmetic and copies ran while one was open for 0% -> 0% of each run, Pallas kernels for 19% -> 18%
where the time goes in v3:
time: 82.5 us; the launch traced here: 82.2 us
  starting transfers between devices  26.6 us (32%)
  blocking collectives  24.4 us (30%)
  Pallas kernels  21.1 us (26%)
  waiting for transfers between devices  9.28 us (11%)
    ppermute x14, starting transfers between devices, from_partner(): return lax.ppermute(value, axis, pairs)  26.6 us
    all_to_all x1, blocking collectives, local(): lax.all_to_all(values[0], AXES, split_axis=0, concat_axis=0, axis_index_g...  24.4 us
    pallas_call x5, Pallas kernels, load_call(): pl.pallas_call(functools.partial(load_body, levels, len(whole)), in_specs...  9.28 us
    ppermute x14, waiting for transfers between devices, from_partner(): return lax.ppermute(value, axis, pairs)  9.28 us
    pallas_call x14, Pallas kernels, level_call(): pl.pallas_call(functools.partial(level_body, first), in_specs=[pl.BlockSp...  5.84 us
    pallas_call x1, Pallas kernels, interp_call(): pl.pallas_call(functools.partial(interp_body, firsts), in_specs=[pl.Block...  3.37 us
  transfers between devices with their start and end apart: 14, of which 7 were waited for; matrix products, arithmetic and copies ran while one was open for 0% of the time, Pallas kernels for 18%

profile of v3, /device:TPU:1, one launch (start us, length us, event | category | flops | bytes accessed | tf_op | source)
XLA Modules:
  0.0 82.2 jit_solution(9292172598270748012)
XLA Ops:
  0.0 0.7 copy-done.2
  0.7 3.4 %interp.1 = (bf16[8,64,128]{2,1,0:T(8,128)(2,1)S(1)}, bf16[8,64,128]{2,1,0:T(8,128)(2,1)S(1)}) custom-call(s32[128]{0:T(128)S(1)} %copy-done.2, bf16[16,32768]{1,0:T(8,128)(2,1)} %src_hbm.1, bf16[128,64,256]{2,1,0:T(8,128)(2,1)} %interp_hbm.1), custom_call_target="tpu_custom_call" | custom-call | tf_op jit(solution)/shard_map/interp/pallas_call | solution.py:77
  4.0 2.5 %collective-permute-start.1 = (bf16[8,64,128]{2,1,0:T(8,128)(2,1)S(1)}, bf16[8,64,128]{2,1,0:T(8,128)(2,1)S(1)}, u32[]{:S(2)}, u32[]{:S(2)}) collective-permute-start(bf16[8,64,128]{2,1,0:T(8,128)(2,1)S(1)} %get-tuple-element.15.own_ref), channel_id=1, source_target_pairs={{0,1},{1,0},{2,3},{3,2},{4,5},{5,4},{6,7},{7,6},{8,9},{9,8},{10,11... | collective-permute-start | bytes 393224 | tf_op jit(solution)/shard_map/ppermute | solution.py:249
  6.6 0.1 collective-permute-start
  6.7 2.2 %load.5 = (bf16[128,64,128]{2,1,0:T(8,128)(2,1)S(1)}, bf16[128,64,128]{2,1,0:T(8,128)(2,1)S(1)}) custom-call(bf16[7,128,64,128]{3,2,1,0:T(8,128)(2,1)} %table_hbm.9, bf16[8,64,128]{2,1,0:T(8,128)(2,1)S(1)} %get-tuple-element.13.rest_0_.own_ref), custom_call_target="tpu_custom_call" | custom-call | tf_op jit(solution)/shard_map/load/pallas_call | solution.py:113
  8.9 0.9 %collective-permute-done.1.far_ref = bf16[8,64,128]{2,1,0:T(8,128)(2,1)S(1)} collective-permute-done((bf16[8,64,128]{2,1,0:T(8,128)(2,1)S(1)}, bf16[8,64,128]{2,1,0:T(8,128)(2,1)S(1)}, u32[]{:S(2)}, u32[]{:S(2)}) %collective-permute-start.1) | collective-permute-done | bytes 131104 | tf_op jit(solution)/shard_map/ppermute | solution.py:249
  9.8 0.4 level.14.rest_0_.own_ref
  10.2 3.2 %collective-permute-start.3 = (bf16[8,64,128]{2,1,0:T(8,128)(2,1)S(1)}, bf16[8,64,128]{2,1,0:T(8,128)(2,1)S(1)}, u32[]{:S(2)}, u32[]{:S(2)}) collective-permute-start(bf16[8,64,128]{2,1,0:T(8,128)(2,1)S(1)} %level.14.rest_0_.own_ref), channel_id=1, source_target_pairs={{0,2},{1,3},{2,0},{3,1},{4,6},{5,7},{6,4},{7,5},{8,10},{9,11},{10,... | collective-permute-start | bytes 393224 | tf_op jit(solution)/shard_map/ppermute | solution.py:249
  13.4 0.4 level.15.rest_0_.own_ref
  13.8 2.4 %collective-permute-start.2 = (bf16[8,64,128]{2,1,0:T(8,128)(2,1)S(1)}, bf16[8,64,128]{2,1,0:T(8,128)(2,1)S(1)}, u32[]{:S(2)}, u32[]{:S(2)}) collective-permute-start(bf16[8,64,128]{2,1,0:T(8,128)(2,1)S(1)} %level.15.rest_0_.own_ref), channel_id=1, source_target_pairs={{0,2},{1,3},{2,0},{3,1},{4,6},{5,7},{6,4},{7,5},{8,10},{9,11},{10,... | collective-permute-start | bytes 393224 | tf_op jit(solution)/shard_map/ppermute | solution.py:249
  16.2 1.6 %load.6.rest_1_.table_ref = bf16[128,64,128]{2,1,0:T(8,128)(2,1)S(1)} custom-call(bf16[7,128,64,128]{3,2,1,0:T(8,128)(2,1)} %table_hbm.9, bf16[8,64,128]{2,1,0:T(8,128)(2,1)S(1)} %level.15.rest_0_.own_ref), custom_call_target="tpu_custom_call" | custom-call | tf_op jit(solution)/shard_map/load/pallas_call | solution.py:113
  17.8 0.6 collective-permute-done.3.far_ref
  18.4 0.4 level.16.rest_0_.own_ref
  18.8 2.8 %collective-permute-start.5 = (bf16[8,64,128]{2,1,0:T(8,128)(2,1)S(1)}, bf16[8,64,128]{2,1,0:T(8,128)(2,1)S(1)}, u32[]{:S(2)}, u32[]{:S(2)}) collective-permute-start(bf16[8,64,128]{2,1,0:T(8,128)(2,1)S(1)} %level.16.rest_0_.own_ref), channel_id=1, source_target_pairs={{0,4},{1,5},{2,6},{3,7},{4,0},{5,1},{6,2},{7,3},{8,12},{9,13},{10,... | collective-permute-start | bytes 393224 | tf_op jit(solution)/shard_map/ppermute | solution.py:249
  21.7 0.4 level.17.rest_0_.own_ref
  22.1 1.9 %collective-permute-start.4 = (bf16[8,64,128]{2,1,0:T(8,128)(2,1)S(1)}, bf16[8,64,128]{2,1,0:T(8,128)(2,1)S(1)}, u32[]{:S(2)}, u32[]{:S(2)}) collective-permute-start(bf16[8,64,128]{2,1,0:T(8,128)(2,1)S(1)} %level.17.rest_0_.own_ref), channel_id=1, source_target_pairs={{0,4},{1,5},{2,6},{3,7},{4,0},{5,1},{6,2},{7,3},{8,12},{9,13},{10,... | collective-permute-start | bytes 393224 | tf_op jit(solution)/shard_map/ppermute | solution.py:249
  24.0 1.6 %load.7.rest_1_.table_ref = bf16[128,64,128]{2,1,0:T(8,128)(2,1)S(1)} custom-call(bf16[7,128,64,128]{3,2,1,0:T(8,128)(2,1)} %table_hbm.9, bf16[8,64,128]{2,1,0:T(8,128)(2,1)S(1)} %level.17.rest_0_.own_ref), custom_call_target="tpu_custom_call" | custom-call | tf_op jit(solution)/shard_map/load/pallas_call | solution.py:113
  25.6 0.4 level.18.rest_0_.own_ref
  26.0 1.4 %collective-permute-start.7 = (bf16[8,64,128]{2,1,0:T(8,128)(2,1)S(1)}, bf16[8,64,128]{2,1,0:T(8,128)(2,1)S(1)}, u32[]{:S(2)}, u32[]{:S(2)}) collective-permute-start(bf16[8,64,128]{2,1,0:T(8,128)(2,1)S(1)} %level.18.rest_0_.own_ref), channel_id=1, source_target_pairs={{0,8},{8,0},{16,24},{24,16},{1,9},{9,1},{17,25},{25,17},{2,10},{10... | collective-permute-start | bytes 393224 | tf_op jit(solution)/shard_map/ppermute | solution.py:249
  27.4 1.6 %collective-permute-done.4.far_ref = bf16[8,64,128]{2,1,0:T(8,128)(2,1)S(1)} collective-permute-done((bf16[8,64,128]{2,1,0:T(8,128)(2,1)S(1)}, bf16[8,64,128]{2,1,0:T(8,128)(2,1)S(1)}, u32[]{:S(2)}, u32[]{:S(2)}) %collective-permute-start.4) | collective-permute-done | bytes 131104 | tf_op jit(solution)/shard_map/ppermute | solution.py:249
  29.0 0.4 level.19.rest_0_.own_ref
  29.4 1.4 %collective-permute-start.6 = (bf16[8,64,128]{2,1,0:T(8,128)(2,1)S(1)}, bf16[8,64,128]{2,1,0:T(8,128)(2,1)S(1)}, u32[]{:S(2)}, u32[]{:S(2)}) collective-permute-start(bf16[8,64,128]{2,1,0:T(8,128)(2,1)S(1)} %level.19.rest_0_.own_ref), channel_id=1, source_target_pairs={{0,8},{8,0},{16,24},{24,16},{1,9},{9,1},{17,25},{25,17},{2,10},{10... | collective-permute-start | bytes 393224 | tf_op jit(solution)/shard_map/ppermute | solution.py:249
  30.8 2.2 %load.8 = (bf16[128,64,128]{2,1,0:T(8,128)(2,1)S(1)}, bf16[128,64,128]{2,1,0:T(8,128)(2,1)S(1)}) custom-call(bf16[7,128,64,128]{3,2,1,0:T(8,128)(2,1)} %table_hbm.9, bf16[8,64,128]{2,1,0:T(8,128)(2,1)S(1)} %level.19.rest_0_.own_ref), custom_call_target="tpu_custom_call" | custom-call | tf_op jit(solution)/shard_map/load/pallas_call | solution.py:113
  33.1 0.4 level.20.rest_0_.own_ref
  33.5 2.7 %collective-permute-start.9 = (bf16[8,64,128]{2,1,0:T(8,128)(2,1)S(1)}, bf16[8,64,128]{2,1,0:T(8,128)(2,1)S(1)}, u32[]{:S(2)}, u32[]{:S(2)}) collective-permute-start(bf16[8,64,128]{2,1,0:T(8,128)(2,1)S(1)} %level.20.rest_0_.own_ref), channel_id=1, source_target_pairs={{0,16},{8,24},{16,0},{24,8},{1,17},{9,25},{17,1},{25,9},{2,18},{10... | collective-permute-start | bytes 393224 | tf_op jit(solution)/shard_map/ppermute | solution.py:249
  36.2 0.0 collective-permute-done.6.far_ref
  36.2 0.4 level.21.rest_0_.own_ref
  36.6 1.0 %collective-permute-start.8 = (bf16[8,64,128]{2,1,0:T(8,128)(2,1)S(1)}, bf16[8,64,128]{2,1,0:T(8,128)(2,1)S(1)}, u32[]{:S(2)}, u32[]{:S(2)}) collective-permute-start(bf16[8,64,128]{2,1,0:T(8,128)(2,1)S(1)} %level.21.rest_0_.own_ref), channel_id=1, source_target_pairs={{0,16},{8,24},{16,0},{24,8},{1,17},{9,25},{17,1},{25,9},{2,18},{10... | collective-permute-start | bytes 393224 | tf_op jit(solution)/shard_map/ppermute | solution.py:249
  37.6 2.7 %collective-permute-done.9.far_ref = bf16[8,64,128]{2,1,0:T(8,128)(2,1)S(1)} collective-permute-done((bf16[8,64,128]{2,1,0:T(8,128)(2,1)S(1)}, bf16[8,64,128]{2,1,0:T(8,128)(2,1)S(1)}, u32[]{:S(2)}, u32[]{:S(2)}) %collective-permute-start.9) | collective-permute-done | bytes 131104 | tf_op jit(solution)/shard_map/ppermute | solution.py:249
  40.2 0.4 level.22.rest_0_.own_ref
  40.7 3.9 %collective-permute-start.11 = (bf16[8,64,128]{2,1,0:T(8,128)(2,1)S(1)}, bf16[8,64,128]{2,1,0:T(8,128)(2,1)S(1)}, u32[]{:S(2)}, u32[]{:S(2)}) collective-permute-start(bf16[8,64,128]{2,1,0:T(8,128)(2,1)S(1)} %level.22.rest_0_.own_ref), channel_id=1, source_target_pairs={{0,32},{32,0},{64,96},{96,64},{1,33},{33,1},{65,97},{97,65},{2,34}... | collective-permute-start | bytes 393224 | tf_op jit(solution)/shard_map/ppermute | solution.py:249
  44.6 0.4 level.23.rest_0_.own_ref
  45.0 1.8 %collective-permute-start.10 = (bf16[8,64,128]{2,1,0:T(8,128)(2,1)S(1)}, bf16[8,64,128]{2,1,0:T(8,128)(2,1)S(1)}, u32[]{:S(2)}, u32[]{:S(2)}) collective-permute-start(bf16[8,64,128]{2,1,0:T(8,128)(2,1)S(1)} %level.23.rest_0_.own_ref), channel_id=1, source_target_pairs={{0,32},{32,0},{64,96},{96,64},{1,33},{33,1},{65,97},{97,65},{2,34}... | collective-permute-start | bytes 393224 | tf_op jit(solution)/shard_map/ppermute | solution.py:249
  46.8 0.4 level.24.rest_0_.own_ref
  47.3 0.4 collective-permute-start.13
  47.7 0.2 collective-permute-done.10.far_ref
  47.8 0.4 level.25.rest_1_.rest_0_.own_ref
  48.2 1.1 %collective-permute-start.12 = (bf16[8,64,128]{2,1,0:T(8,128)(2,1)S(1)}, bf16[8,64,128]{2,1,0:T(8,128)(2,1)S(1)}, u32[]{:S(2)}, u32[]{:S(2)}) collective-permute-start(bf16[8,64,128]{2,1,0:T(8,128)(2,1)S(1)} %level.25.rest_1_.rest_0_.own_ref), channel_id=1, source_target_pairs={{0,64},{32,96},{64,0},{96,32},{1,65},{33,97},{65,1},{97,33},{2,66}... | collective-permute-start | bytes 393224 | tf_op jit(solution)/shard_map/ppermute | solution.py:249
  49.3 1.6 %load.9 = (bf16[128,64,128]{2,1,0:T(8,128)(2,1)S(1)}, bf16[128,64,256]{2,1,0:T(8,128)(2,1)S(1)}) custom-call(bf16[7,128,64,128]{3,2,1,0:T(8,128)(2,1)} %table_hbm.9, bf16[128,64,256]{2,1,0:T(8,128)(2,1)S(1)} %copy-done, bf16[8,64,128]{2,1,0:T(8,128)(2,1)S(1)} %level.25.rest_1_.rest_0_.own_ref), custom_call_target="tpu_custom_call" | custom-call | tf_op jit(solution)/shard_map/load/pallas_call | solution.py:113
  50.9 1.5 %collective-permute-done.13.far_ref = bf16[8,64,128]{2,1,0:T(8,128)(2,1)S(1)} collective-permute-done((bf16[8,64,128]{2,1,0:T(8,128)(2,1)S(1)}, bf16[8,64,128]{2,1,0:T(8,128)(2,1)S(1)}, u32[]{:S(2)}, u32[]{:S(2)}) %collective-permute-start.13) | collective-permute-done | bytes 131104 | tf_op jit(solution)/shard_map/ppermute | solution.py:249
  52.4 0.4 level.26.rest_0_.coeffs_ref
  52.9 0.5 evaluate.2.rest_0_
  53.4 1.9 %collective-permute-done.12.far_ref = bf16[8,64,128]{2,1,0:T(8,128)(2,1)S(1)} collective-permute-done((bf16[8,64,128]{2,1,0:T(8,128)(2,1)S(1)}, bf16[8,64,128]{2,1,0:T(8,128)(2,1)S(1)}, u32[]{:S(2)}, u32[]{:S(2)}) %collective-permute-start.12) | collective-permute-done | bytes 131104 | tf_op jit(solution)/shard_map/ppermute | solution.py:249
  55.2 0.4 level.27.coeffs_ref
  55.7 0.5 evaluate.3
  56.2 0.0 copy-start.1
  56.2 24.4 %all_to_all.5.got_ref = bf16[128,16,256]{2,1,0:T(8,128)(2,1)S(1)} all-to-all(bf16[128,16,256]{2,1,0:T(8,128)(2,1)S(1)} %evaluate.3), channel_id=1, replica_groups={{0,1,2,3,64,65,66,67,4,5,6,7,68,69,70,71,8,9,10,11,72,73,74,75,12,13,14..., dimensions={0} | all-to-all | bytes 2097152 | tf_op jit(solution)/shard_map/all_to_all | solution.py:285
  80.6 1.6 %place.1 = bf16[16,32768]{1,0:T(8,128)(2,1)} custom-call(s32[128]{0:T(128)S(1)} %copy-done.1, bf16[128,16,256]{2,1,0:T(8,128)(2,1)S(1)} %all_to_all.5.got_ref), custom_call_target="tpu_custom_call" | custom-call | tf_op jit(solution)/shard_map/place/pallas_call | solution.py:228
  (10 shorter events, 0.0 us)
Async XLA Ops:
  0.0 0.7 copy-start.2
  4.0 5.8 %collective-permute-start.1 = (bf16[8,64,128]{2,1,0:T(8,128)(2,1)S(1)}, bf16[8,64,128]{2,1,0:T(8,128)(2,1)S(1)}, u32[]{:S(2)}, u32[]{:S(2)}) collective-permute-start(bf16[8,64,128]{2,1,0:T(8,128)(2,1)S(1)} %get-tuple-element.15.own_ref), channel_id=1, source_target_pairs={{0,1},{1,0},{2,3},{3,2},{4,5},{5,4},{6,7},{7,6},{8,9},{9,8},{10,11... | collective-permute-start | bytes 393224 | tf_op jit(solution)/shard_map/ppermute | solution.py:249
  6.6 6.8 %collective-permute-start = (bf16[8,64,128]{2,1,0:T(8,128)(2,1)S(1)}, bf16[8,64,128]{2,1,0:T(8,128)(2,1)S(1)}, u32[]{:S(2)}, u32[]{:S(2)}) collective-permute-start(bf16[8,64,128]{2,1,0:T(8,128)(2,1)S(1)} %get-tuple-element.13.rest_0_.own_ref), channel_id=1, source_target_pairs={{0,1},{1,0},{2,3},{3,2},{4,5},{5,4},{6,7},{7,6},{8,9},{9,8},{10,11... | collective-permute-start | bytes 393224 | tf_op jit(solution)/shard_map/ppermute | solution.py:249
  10.2 8.2 %collective-permute-start.3 = (bf16[8,64,128]{2,1,0:T(8,128)(2,1)S(1)}, bf16[8,64,128]{2,1,0:T(8,128)(2,1)S(1)}, u32[]{:S(2)}, u32[]{:S(2)}) collective-permute-start(bf16[8,64,128]{2,1,0:T(8,128)(2,1)S(1)} %level.14.rest_0_.own_ref), channel_id=1, source_target_pairs={{0,2},{1,3},{2,0},{3,1},{4,6},{5,7},{6,4},{7,5},{8,10},{9,11},{10,... | collective-permute-start | bytes 393224 | tf_op jit(solution)/shard_map/ppermute | solution.py:249
  13.8 7.8 %collective-permute-start.2 = (bf16[8,64,128]{2,1,0:T(8,128)(2,1)S(1)}, bf16[8,64,128]{2,1,0:T(8,128)(2,1)S(1)}, u32[]{:S(2)}, u32[]{:S(2)}) collective-permute-start(bf16[8,64,128]{2,1,0:T(8,128)(2,1)S(1)} %level.15.rest_0_.own_ref), channel_id=1, source_target_pairs={{0,2},{1,3},{2,0},{3,1},{4,6},{5,7},{6,4},{7,5},{8,10},{9,11},{10,... | collective-permute-start | bytes 393224 | tf_op jit(solution)/shard_map/ppermute | solution.py:249
  18.8 6.7 %collective-permute-start.5 = (bf16[8,64,128]{2,1,0:T(8,128)(2,1)S(1)}, bf16[8,64,128]{2,1,0:T(8,128)(2,1)S(1)}, u32[]{:S(2)}, u32[]{:S(2)}) collective-permute-start(bf16[8,64,128]{2,1,0:T(8,128)(2,1)S(1)} %level.16.rest_0_.own_ref), channel_id=1, source_target_pairs={{0,4},{1,5},{2,6},{3,7},{4,0},{5,1},{6,2},{7,3},{8,12},{9,13},{10,... | collective-permute-start | bytes 393224 | tf_op jit(solution)/shard_map/ppermute | solution.py:249
  22.1 6.9 %collective-permute-start.4 = (bf16[8,64,128]{2,1,0:T(8,128)(2,1)S(1)}, bf16[8,64,128]{2,1,0:T(8,128)(2,1)S(1)}, u32[]{:S(2)}, u32[]{:S(2)}) collective-permute-start(bf16[8,64,128]{2,1,0:T(8,128)(2,1)S(1)} %level.17.rest_0_.own_ref), channel_id=1, source_target_pairs={{0,4},{1,5},{2,6},{3,7},{4,0},{5,1},{6,2},{7,3},{8,12},{9,13},{10,... | collective-permute-start | bytes 393224 | tf_op jit(solution)/shard_map/ppermute | solution.py:249
  26.0 7.1 %collective-permute-start.7 = (bf16[8,64,128]{2,1,0:T(8,128)(2,1)S(1)}, bf16[8,64,128]{2,1,0:T(8,128)(2,1)S(1)}, u32[]{:S(2)}, u32[]{:S(2)}) collective-permute-start(bf16[8,64,128]{2,1,0:T(8,128)(2,1)S(1)} %level.18.rest_0_.own_ref), channel_id=1, source_target_pairs={{0,8},{8,0},{16,24},{24,16},{1,9},{9,1},{17,25},{25,17},{2,10},{10... | collective-permute-start | bytes 393224 | tf_op jit(solution)/shard_map/ppermute | solution.py:249
  29.4 6.8 %collective-permute-start.6 = (bf16[8,64,128]{2,1,0:T(8,128)(2,1)S(1)}, bf16[8,64,128]{2,1,0:T(8,128)(2,1)S(1)}, u32[]{:S(2)}, u32[]{:S(2)}) collective-permute-start(bf16[8,64,128]{2,1,0:T(8,128)(2,1)S(1)} %level.19.rest_0_.own_ref), channel_id=1, source_target_pairs={{0,8},{8,0},{16,24},{24,16},{1,9},{9,1},{17,25},{25,17},{2,10},{10... | collective-permute-start | bytes 393224 | tf_op jit(solution)/shard_map/ppermute | solution.py:249
  33.5 6.7 %collective-permute-start.9 = (bf16[8,64,128]{2,1,0:T(8,128)(2,1)S(1)}, bf16[8,64,128]{2,1,0:T(8,128)(2,1)S(1)}, u32[]{:S(2)}, u32[]{:S(2)}) collective-permute-start(bf16[8,64,128]{2,1,0:T(8,128)(2,1)S(1)} %level.20.rest_0_.own_ref), channel_id=1, source_target_pairs={{0,16},{8,24},{16,0},{24,8},{1,17},{9,25},{17,1},{25,9},{2,18},{10... | collective-permute-start | bytes 393224 | tf_op jit(solution)/shard_map/ppermute | solution.py:249
  36.6 8.0 %collective-permute-start.8 = (bf16[8,64,128]{2,1,0:T(8,128)(2,1)S(1)}, bf16[8,64,128]{2,1,0:T(8,128)(2,1)S(1)}, u32[]{:S(2)}, u32[]{:S(2)}) collective-permute-start(bf16[8,64,128]{2,1,0:T(8,128)(2,1)S(1)} %level.21.rest_0_.own_ref), channel_id=1, source_target_pairs={{0,16},{8,24},{16,0},{24,8},{1,17},{9,25},{17,1},{25,9},{2,18},{10... | collective-permute-start | bytes 393224 | tf_op jit(solution)/shard_map/ppermute | solution.py:249
  40.7 6.2 %collective-permute-start.11 = (bf16[8,64,128]{2,1,0:T(8,128)(2,1)S(1)}, bf16[8,64,128]{2,1,0:T(8,128)(2,1)S(1)}, u32[]{:S(2)}, u32[]{:S(2)}) collective-permute-start(bf16[8,64,128]{2,1,0:T(8,128)(2,1)S(1)} %level.22.rest_0_.own_ref), channel_id=1, source_target_pairs={{0,32},{32,0},{64,96},{96,64},{1,33},{33,1},{65,97},{97,65},{2,34}... | collective-permute-start | bytes 393224 | tf_op jit(solution)/shard_map/ppermute | solution.py:249
  45.0 2.8 %collective-permute-start.10 = (bf16[8,64,128]{2,1,0:T(8,128)(2,1)S(1)}, bf16[8,64,128]{2,1,0:T(8,128)(2,1)S(1)}, u32[]{:S(2)}, u32[]{:S(2)}) collective-permute-start(bf16[8,64,128]{2,1,0:T(8,128)(2,1)S(1)} %level.23.rest_0_.own_ref), channel_id=1, source_target_pairs={{0,32},{32,0},{64,96},{96,64},{1,33},{33,1},{65,97},{97,65},{2,34}... | collective-permute-start | bytes 393224 | tf_op jit(solution)/shard_map/ppermute | solution.py:249
  46.8 2.5 %copy-start = (bf16[128,64,256]{2,1,0:T(8,128)(2,1)S(1)}, bf16[128,64,256]{2,1,0:T(8,128)(2,1)}, u32[]{:S(2)}) copy-start(bf16[128,64,256]{2,1,0:T(8,128)(2,1)} %rest_0_.1) | copy-start | bytes 12582916
  47.3 5.2 %collective-permute-start.13 = (bf16[8,64,128]{2,1,0:T(8,128)(2,1)S(1)}, bf16[8,64,128]{2,1,0:T(8,128)(2,1)S(1)}, u32[]{:S(2)}, u32[]{:S(2)}) collective-permute-start(bf16[8,64,128]{2,1,0:T(8,128)(2,1)S(1)} %level.24.rest_0_.own_ref), channel_id=1, source_target_pairs={{0,64},{32,96},{64,0},{96,32},{1,65},{33,97},{65,1},{97,33},{2,66}... | collective-permute-start | bytes 393224 | tf_op jit(solution)/shard_map/ppermute | solution.py:249
  48.2 7.0 %collective-permute-start.12 = (bf16[8,64,128]{2,1,0:T(8,128)(2,1)S(1)}, bf16[8,64,128]{2,1,0:T(8,128)(2,1)S(1)}, u32[]{:S(2)}, u32[]{:S(2)}) collective-permute-start(bf16[8,64,128]{2,1,0:T(8,128)(2,1)S(1)} %level.25.rest_1_.rest_0_.own_ref), channel_id=1, source_target_pairs={{0,64},{32,96},{64,0},{96,32},{1,65},{33,97},{65,1},{97,33},{2,66}... | collective-permute-start | bytes 393224 | tf_op jit(solution)/shard_map/ppermute | solution.py:249
  56.2 24.4 %copy-start.1 = (s32[128]{0:T(128)S(1)}, s32[128]{0:T(128)}, u32[]{:S(2)}) copy-start(s32[128]{0:T(128)} %slot_ref.1) | copy-start | bytes 1540

commit v4 on v3

--- a/solution.py
+++ b/solution.py
@@ -1,5 +1,4 @@
 import functools
-import itertools
 
 import jax
 import jax.numpy as jnp
@@ -12,10 +11,14 @@
 AXES = ("gx", "gy", "gz")
 PACK = 8
 CHUNKS = (8, 8)
-LOADS = {0: 2, 1: 1, 2: 1, 3: 2, 6: 1}
+EARLY = 1
+LOADS = {0: 1, 1: 1, 2: 1, 3: 2, 6: 1}
 PIECES = 4
 ORDER = (1, 2, 3, 0, 4)
 SPLIT = (2, 2, 4, 2, 4)
+CORE_STEP = ("gx", 0)
+CORE_PARTS = 2
+EVALUATE_COST = pl.CostEstimate(flops=10**9, bytes_accessed=0, transcendentals=0)
 MIB = 2**20
 FREE = pl.CostEstimate(flops=0, bytes_accessed=0, transcendentals=0)
 VMEM_LIMIT = 16 * MIB
@@ -107,46 +110,54 @@
         copy.wait()
 
 
-def load_call(levels, tables, whole, after):
+def load_call(levels, tables, whole, after, passes=False):
     outs = [jax.ShapeDtypeStruct(tables.shape[1:], tables.dtype)] * len(levels)
     outs += [jax.ShapeDtypeStruct(array.shape, array.dtype) for array in whole]
+    count = len(outs)
+    specs = [pl.BlockSpec(memory_space=pltpu.VMEM)] * count
+    if passes:
+        outs.append(jax.ShapeDtypeStruct(after.shape, after.dtype))
+        specs.append(pl.BlockSpec(memory_space=pl.ANY))
     return pl.pallas_call(
         functools.partial(load_body, levels, len(whole)),
         in_specs=[pl.BlockSpec(memory_space=pl.ANY)] * (2 + len(whole)),
-        out_specs=[pl.BlockSpec(memory_space=pltpu.VMEM)] * len(outs),
+        out_specs=specs,
         out_shape=outs,
-        scratch_shapes=[pltpu.SemaphoreType.DMA((len(outs),))],
+        input_output_aliases={1 + len(whole): count} if passes else {},
+        scratch_shapes=[pltpu.SemaphoreType.DMA((count,))],
         compiler_params=pltpu.CompilerParams(vmem_limit_bytes=LOAD_LIMIT),
         cost_estimate=FREE,
         name="load",
     )(tables, *whole, after)
 
 
-def level_body(first, table_ref, own_ref, far_ref, *rest):
+def level_body(first, parts, table_ref, own_ref, *rest):
     out_ref = rest[-1]
+    far_refs = rest[:parts]
     _, rank, both = table_ref.shape
     groups, _, lanes = own_ref.shape
     for grp in range(groups):
         at = (first + grp) * PACK
         block = table_ref[at : at + PACK].reshape(PACK * rank, both)
-        pair = jnp.concatenate([own_ref[grp], far_ref[grp]], axis=0)
+        per = groups // parts
+        pair = jnp.concatenate([own_ref[grp], far_refs[grp // per][grp % per]], axis=0)
         wide = jnp.dot(block, pair, preferred_element_type=jnp.float32)
         out_ref[grp] = pick(wide, rank, lanes // PACK).astype(jnp.bfloat16)
 
 
-def level_call(first, table, own, far, *after):
+def level_call(first, table, own, fars, *after):
     groups, rank, lanes = own.shape
     both = table.shape[2]
     return pl.pallas_call(
-        functools.partial(level_body, first),
-        in_specs=[pl.BlockSpec(memory_space=pltpu.VMEM)] * 3
+        functools.partial(level_body, first, len(fars)),
+        in_specs=[pl.BlockSpec(memory_space=pltpu.VMEM)] * (2 + len(fars))
         + [pl.BlockSpec(memory_space=pl.ANY)] * len(after),
         out_specs=pl.BlockSpec(memory_space=pltpu.VMEM),
         out_shape=jax.ShapeDtypeStruct(own.shape, jnp.bfloat16),
         compiler_params=pltpu.CompilerParams(vmem_limit_bytes=VMEM_LIMIT),
         cost_estimate=FREE,
         name="level",
-    )(table, own, far, *after)
+    )(table, own, *fars, *after)
 
 
 def eval_body(first, place_of, coeffs_ref, eval_ref, *rest):
@@ -180,7 +191,7 @@
         out_shape=jax.ShapeDtypeStruct((boxes, rhs, span), jnp.bfloat16),
         input_output_aliases={2: 0} if before else {},
         compiler_params=pltpu.CompilerParams(vmem_limit_bytes=VMEM_LIMIT),
-        cost_estimate=FREE,
+        cost_estimate=EVALUATE_COST,
         name="evaluate",
     )(coeffs, evaluate, *before)
 
@@ -249,18 +260,28 @@
     return lax.ppermute(value, axis, pairs)
 
 
+def kernel_order(steps, chunks):
+    order, at = [], 0
+    while at < len(steps):
+        width = 2 if at + 1 < len(steps) and steps[at + 1] == CORE_STEP else 1
+        for i in range(chunks):
+            order += [(level, i) for level in range(at, at + width)]
+        at += width
+    return order
+
+
 def local(sources, in_slot, interp, translate, evaluate, owner_slot):
     firsts = [sum(CHUNKS[:i]) for i in range(len(CHUNKS))]
     coeffs = list(interp_call(firsts, in_slot, sources, interp))
-    held = []
     steps = [
         (axis, bit_pos)
         for axis in ("gz", "gy", "gx")
         for bit_pos in range(lax.axis_size(axis).bit_length() - 1)
     ]
     tables = {}
+    *held, coeffs[-1] = load_call(range(EARLY), translate, [], coeffs[-1], True)
     last = coeffs[-1]
-    for level, i in itertools.product(range(len(steps)), range(len(firsts))):
+    for level, i in kernel_order(steps, len(firsts)):
         axis, bit_pos = steps[level]
         if i == 0:
             more = ()
@@ -272,9 +293,11 @@
                 if final:
                     evaluate = more[-1]
             tables[level] = more[:1]
-        far = from_partner(coeffs[i], axis, bit_pos)
+        parts = CORE_PARTS if steps[level] == CORE_STEP else 1
+        pieces = jnp.split(coeffs[i], parts) if parts > 1 else [coeffs[i]]
+        fars = [from_partner(piece, axis, bit_pos) for piece in pieces]
         last = coeffs[i] = level_call(
-            firsts[i], held[level], coeffs[i], far, last, *tables[level]
+            firsts[i], held[level], coeffs[i], fars, last, *tables[level]
         )
     devices = np.arange(int(np.prod(SPLIT))).reshape(SPLIT).transpose(ORDER).reshape(-1)
     group = [int(device) for device in devices]

time: 82.5 us -> 82.2 us (level)
  waiting for transfers between devices: 9.28 us -> 8.13 us
  Pallas kernels: 21.1 us -> 22.1 us
    ppermute x14 -> x16, waiting for transfers between devices: 9.28 us -> 8.13 us  [from_partner(): return lax.ppermute(value, axis, pairs)]
    pallas_call x5 -> x6, Pallas kernels: 9.28 us -> 10.2 us  [load_call(): pl.pallas_call(functools.partial(load_body, levels, len(whole)), in_specs...]
    ppermute x14 -> x16, starting transfers between devices: 26.6 us -> 25.8 us  [from_partner(): return lax.ppermute(value, axis, pairs)]
  transfers between devices with their start and end apart: 14 -> 16, of which waited for: 7 -> 8; matrix products, arithmetic and copies ran while one was open for 0% -> 0% of each run, Pallas kernels for 18% -> 20%
where the time goes in v4:
time: 82.2 us; the launch traced here: 81.9 us
  starting transfers between devices  25.8 us (31%)
  blocking collectives  25 us (30%)
  Pallas kernels  22.1 us (27%)
  waiting for transfers between devices  8.13 us (10%)
    ppermute x16, starting transfers between devices, from_partner(): return lax.ppermute(value, axis, pairs)  25.8 us
    all_to_all x1, blocking collectives, local(): lax.all_to_all(values[0], AXES, split_axis=0, concat_axis=0, axis_index_g...  25 us
    pallas_call x6, Pallas kernels, load_call(): pl.pallas_call(functools.partial(load_body, levels, len(whole)), in_specs...  10.2 us
    ppermute x16, waiting for transfers between devices, from_partner(): return lax.ppermute(value, axis, pairs)  8.13 us
    pallas_call x14, Pallas kernels, level_call(): pl.pallas_call(functools.partial(level_body, first, len(fars)), in_specs=...  5.85 us
    pallas_call x1, Pallas kernels, interp_call(): pl.pallas_call(functools.partial(interp_body, firsts), in_specs=[pl.Block...  3.38 us
  transfers between devices with their start and end apart: 16, of which 8 were waited for; matrix products, arithmetic and copies ran while one was open for 0% of the time, Pallas kernels for 20%

profile of v4, /device:TPU:1, one launch (start us, length us, event | category | flops | bytes accessed | tf_op | source)
XLA Modules:
  0.0 81.9 jit_solution(17863416659385669115)
XLA Ops:
  0.0 0.7 copy-done.2
  0.7 3.4 %interp.1 = (bf16[8,64,128]{2,1,0:T(8,128)(2,1)S(1)}, bf16[8,64,128]{2,1,0:T(8,128)(2,1)S(1)}) custom-call(s32[128]{0:T(128)S(1)} %copy-done.2, bf16[16,32768]{1,0:T(8,128)(2,1)} %src_hbm.1, bf16[128,64,256]{2,1,0:T(8,128)(2,1)} %interp_hbm.1), custom_call_target="tpu_custom_call" | custom-call | tf_op jit(solution)/shard_map/interp/pallas_call | solution.py:80
  4.0 2.5 %collective-permute-start.1 = (bf16[8,64,128]{2,1,0:T(8,128)(2,1)S(1)}, bf16[8,64,128]{2,1,0:T(8,128)(2,1)S(1)}, u32[]{:S(2)}, u32[]{:S(2)}) collective-permute-start(bf16[8,64,128]{2,1,0:T(8,128)(2,1)S(1)} %get-tuple-element.16.own_ref), channel_id=1, source_target_pairs={{0,1},{1,0},{2,3},{3,2},{4,5},{5,4},{6,7},{7,6},{8,9},{9,8},{10,11... | collective-permute-start | bytes 393224 | tf_op jit(solution)/shard_map/ppermute | solution.py:260
  6.6 1.6 %load.6 = (bf16[128,64,128]{2,1,0:T(8,128)(2,1)S(1)}, bf16[8,64,128]{2,1,0:T(8,128)(2,1)S(1)}) custom-call(bf16[7,128,64,128]{3,2,1,0:T(8,128)(2,1)} %table_hbm.11, bf16[8,64,128]{2,1,0:T(8,128)(2,1)S(1)} %get-tuple-element.13.rest_0_), custom_call_target="tpu_custom_call", output_to_operand_aliasing={{1}: (1, {})} | custom-call | tf_op jit(solution)/shard_map/load/pallas_call | solution.py:121
  8.2 0.1 collective-permute-start
  8.3 1.6 %load.7.rest_2_.table_ref = bf16[128,64,128]{2,1,0:T(8,128)(2,1)S(1)} custom-call(bf16[7,128,64,128]{3,2,1,0:T(8,128)(2,1)} %table_hbm.11, bf16[8,64,128]{2,1,0:T(8,128)(2,1)S(1)} %get-tuple-element.15.rest_0_.rest_1_.own_ref), custom_call_target="tpu_custom_call" | custom-call | tf_op jit(solution)/shard_map/load/pallas_call | solution.py:121
  9.9 0.4 level.14.rest_1_.own_ref
  10.3 3.5 %collective-permute-start.3 = (bf16[8,64,128]{2,1,0:T(8,128)(2,1)S(1)}, bf16[8,64,128]{2,1,0:T(8,128)(2,1)S(1)}, u32[]{:S(2)}, u32[]{:S(2)}) collective-permute-start(bf16[8,64,128]{2,1,0:T(8,128)(2,1)S(1)} %level.14.rest_1_.own_ref), channel_id=1, source_target_pairs={{0,2},{1,3},{2,0},{3,1},{4,6},{5,7},{6,4},{7,5},{8,10},{9,11},{10,... | collective-permute-start | bytes 393224 | tf_op jit(solution)/shard_map/ppermute | solution.py:260
  13.8 0.4 level.15.rest_0_.rest_1_.own_ref
  14.3 1.7 %collective-permute-start.2 = (bf16[8,64,128]{2,1,0:T(8,128)(2,1)S(1)}, bf16[8,64,128]{2,1,0:T(8,128)(2,1)S(1)}, u32[]{:S(2)}, u32[]{:S(2)}) collective-permute-start(bf16[8,64,128]{2,1,0:T(8,128)(2,1)S(1)} %level.15.rest_0_.rest_1_.own_ref), channel_id=1, source_target_pairs={{0,2},{1,3},{2,0},{3,1},{4,6},{5,7},{6,4},{7,5},{8,10},{9,11},{10,... | collective-permute-start | bytes 393224 | tf_op jit(solution)/shard_map/ppermute | solution.py:260
  15.9 1.6 %load.8.rest_2_.table_ref = bf16[128,64,128]{2,1,0:T(8,128)(2,1)S(1)} custom-call(bf16[7,128,64,128]{3,2,1,0:T(8,128)(2,1)} %table_hbm.11, bf16[8,64,128]{2,1,0:T(8,128)(2,1)S(1)} %level.15.rest_0_.rest_1_.own_ref), custom_call_target="tpu_custom_call" | custom-call | tf_op jit(solution)/shard_map/load/pallas_call | solution.py:121
  17.5 1.0 %collective-permute-done.3.rest_0_ = bf16[8,64,128]{2,1,0:T(8,128)(2,1)S(1)} collective-permute-done((bf16[8,64,128]{2,1,0:T(8,128)(2,1)S(1)}, bf16[8,64,128]{2,1,0:T(8,128)(2,1)S(1)}, u32[]{:S(2)}, u32[]{:S(2)}) %collective-permute-start.3) | collective-permute-done | bytes 131104 | tf_op jit(solution)/shard_map/ppermute | solution.py:260
  18.5 0.4 level.16.rest_1_.own_ref
  18.9 2.8 %collective-permute-start.5 = (bf16[8,64,128]{2,1,0:T(8,128)(2,1)S(1)}, bf16[8,64,128]{2,1,0:T(8,128)(2,1)S(1)}, u32[]{:S(2)}, u32[]{:S(2)}) collective-permute-start(bf16[8,64,128]{2,1,0:T(8,128)(2,1)S(1)} %level.16.rest_1_.own_ref), channel_id=1, source_target_pairs={{0,4},{1,5},{2,6},{3,7},{4,0},{5,1},{6,2},{7,3},{8,12},{9,13},{10,... | collective-permute-start | bytes 393224 | tf_op jit(solution)/shard_map/ppermute | solution.py:260
  21.8 0.4 level.17.rest_0_.rest_1_.own_ref
  22.2 2.3 %collective-permute-start.4 = (bf16[8,64,128]{2,1,0:T(8,128)(2,1)S(1)}, bf16[8,64,128]{2,1,0:T(8,128)(2,1)S(1)}, u32[]{:S(2)}, u32[]{:S(2)}) collective-permute-start(bf16[8,64,128]{2,1,0:T(8,128)(2,1)S(1)} %level.17.rest_0_.rest_1_.own_ref), channel_id=1, source_target_pairs={{0,4},{1,5},{2,6},{3,7},{4,0},{5,1},{6,2},{7,3},{8,12},{9,13},{10,... | collective-permute-start | bytes 393224 | tf_op jit(solution)/shard_map/ppermute | solution.py:260
  24.5 1.6 %load.9.rest_2_.table_ref = bf16[128,64,128]{2,1,0:T(8,128)(2,1)S(1)} custom-call(bf16[7,128,64,128]{3,2,1,0:T(8,128)(2,1)} %table_hbm.11, bf16[8,64,128]{2,1,0:T(8,128)(2,1)S(1)} %level.17.rest_0_.rest_1_.own_ref), custom_call_target="tpu_custom_call" | custom-call | tf_op jit(solution)/shard_map/load/pallas_call | solution.py:121
  26.1 0.4 level.18.rest_1_.own_ref
  26.5 1.4 %collective-permute-start.7 = (bf16[8,64,128]{2,1,0:T(8,128)(2,1)S(1)}, bf16[8,64,128]{2,1,0:T(8,128)(2,1)S(1)}, u32[]{:S(2)}, u32[]{:S(2)}) collective-permute-start(bf16[8,64,128]{2,1,0:T(8,128)(2,1)S(1)} %level.18.rest_1_.own_ref), channel_id=1, source_target_pairs={{0,8},{8,0},{16,24},{24,16},{1,9},{9,1},{17,25},{25,17},{2,10},{10... | collective-permute-start | bytes 393224 | tf_op jit(solution)/shard_map/ppermute | solution.py:260
  27.9 0.7 collective-permute-done.4.rest_0_
  28.6 0.4 level.19.rest_0_.rest_1_.own_ref
  29.0 1.4 %collective-permute-start.6 = (bf16[8,64,128]{2,1,0:T(8,128)(2,1)S(1)}, bf16[8,64,128]{2,1,0:T(8,128)(2,1)S(1)}, u32[]{:S(2)}, u32[]{:S(2)}) collective-permute-start(bf16[8,64,128]{2,1,0:T(8,128)(2,1)S(1)} %level.19.rest_0_.rest_1_.own_ref), channel_id=1, source_target_pairs={{0,8},{8,0},{16,24},{24,16},{1,9},{9,1},{17,25},{25,17},{2,10},{10... | collective-permute-start | bytes 393224 | tf_op jit(solution)/shard_map/ppermute | solution.py:260
  30.4 2.2 %load.10 = (bf16[128,64,128]{2,1,0:T(8,128)(2,1)S(1)}, bf16[128,64,128]{2,1,0:T(8,128)(2,1)S(1)}) custom-call(bf16[7,128,64,128]{3,2,1,0:T(8,128)(2,1)} %table_hbm.11, bf16[8,64,128]{2,1,0:T(8,128)(2,1)S(1)} %level.19.rest_0_.rest_1_.own_ref), custom_call_target="tpu_custom_call" | custom-call | tf_op jit(solution)/shard_map/load/pallas_call | solution.py:121
  32.6 0.4 level.20.rest_1_.own_ref
  33.1 2.7 %collective-permute-start.9 = (bf16[8,64,128]{2,1,0:T(8,128)(2,1)S(1)}, bf16[8,64,128]{2,1,0:T(8,128)(2,1)S(1)}, u32[]{:S(2)}, u32[]{:S(2)}) collective-permute-start(bf16[8,64,128]{2,1,0:T(8,128)(2,1)S(1)} %level.20.rest_1_.own_ref), channel_id=1, source_target_pairs={{0,16},{8,24},{16,0},{24,8},{1,17},{9,25},{17,1},{25,9},{2,18},{10... | collective-permute-start | bytes 393224 | tf_op jit(solution)/shard_map/ppermute | solution.py:260
  35.8 0.4 level.21.rest_1_.own_ref
  36.2 1.0 %collective-permute-start.8 = (bf16[8,64,128]{2,1,0:T(8,128)(2,1)S(1)}, bf16[8,64,128]{2,1,0:T(8,128)(2,1)S(1)}, u32[]{:S(2)}, u32[]{:S(2)}) collective-permute-start(bf16[8,64,128]{2,1,0:T(8,128)(2,1)S(1)} %level.21.rest_1_.own_ref), channel_id=1, source_target_pairs={{0,16},{8,24},{16,0},{24,8},{1,17},{9,25},{17,1},{25,9},{2,18},{10... | collective-permute-start | bytes 393224 | tf_op jit(solution)/shard_map/ppermute | solution.py:260
  37.2 2.5 %collective-permute-done.9.rest_0_ = bf16[8,64,128]{2,1,0:T(8,128)(2,1)S(1)} collective-permute-done((bf16[8,64,128]{2,1,0:T(8,128)(2,1)S(1)}, bf16[8,64,128]{2,1,0:T(8,128)(2,1)S(1)}, u32[]{:S(2)}, u32[]{:S(2)}) %collective-permute-start.9) | collective-permute-done | bytes 131104 | tf_op jit(solution)/shard_map/ppermute | solution.py:260
  39.7 0.4 level.22.own_ref.rest_2_
  40.2 4.1 %collective-permute-start.11 = (bf16[4,64,128]{2,1,0:T(8,128)(2,1)S(1)}, bf16[4,64,128]{2,1,0:T(8,128)(2,1)S(1)}, u32[]{:S(2)}, u32[]{:S(2)}) collective-permute-start(bf16[4,64,128]{2,1,0:T(8,128)(2,1)S(1)} %get-tuple-element.23), channel_id=1, source_target_pairs={{0,32},{32,0},{64,96},{96,64},{1,33},{33,1},{65,97},{97,65},{2,34}... | collective-permute-start | bytes 196616 | tf_op jit(solution)/shard_map/ppermute | solution.py:260
  44.3 0.8 collective-permute-done.11.rest_1_
  45.1 0.4 collective-permute-done.10.rest_0_
  45.5 0.4 level.23.rest_1_.own_ref
  45.9 0.8 collective-permute-start.15
  46.6 0.4 level.24.own_ref.rest_2_
  47.1 0.5 collective-permute-start.13
  47.7 0.8 collective-permute-done.13.rest_1_
  48.5 0.4 collective-permute-done.12.rest_0_
  48.9 0.4 level.25.rest_1_.own_ref
  49.3 0.9 %collective-permute-start.14 = (bf16[8,64,128]{2,1,0:T(8,128)(2,1)S(1)}, bf16[8,64,128]{2,1,0:T(8,128)(2,1)S(1)}, u32[]{:S(2)}, u32[]{:S(2)}) collective-permute-start(bf16[8,64,128]{2,1,0:T(8,128)(2,1)S(1)} %level.25.rest_1_.own_ref), channel_id=1, source_target_pairs={{0,64},{32,96},{64,0},{96,32},{1,65},{33,97},{65,1},{97,33},{2,66}... | collective-permute-start | bytes 393224 | tf_op jit(solution)/shard_map/ppermute | solution.py:260
  50.2 1.6 %load.11 = (bf16[128,64,128]{2,1,0:T(8,128)(2,1)S(1)}, bf16[128,64,256]{2,1,0:T(8,128)(2,1)S(1)}) custom-call(bf16[7,128,64,128]{3,2,1,0:T(8,128)(2,1)} %table_hbm.11, bf16[128,64,256]{2,1,0:T(8,128)(2,1)S(1)} %copy-done, bf16[8,64,128]{2,1,0:T(8,128)(2,1)S(1)} %level.25.rest_1_.own_ref), custom_call_target="tpu_custom_call" | custom-call | tf_op jit(solution)/shard_map/load/pallas_call | solution.py:121
  51.8 0.4 level.26.rest_1_.coeffs_ref
  52.2 0.5 evaluate.2.rest_0_
  52.7 1.6 %collective-permute-done.14.rest_0_ = bf16[8,64,128]{2,1,0:T(8,128)(2,1)S(1)} collective-permute-done((bf16[8,64,128]{2,1,0:T(8,128)(2,1)S(1)}, bf16[8,64,128]{2,1,0:T(8,128)(2,1)S(1)}, u32[]{:S(2)}, u32[]{:S(2)}) %collective-permute-start.14) | collective-permute-done | bytes 131104 | tf_op jit(solution)/shard_map/ppermute | solution.py:260
  54.3 0.4 level.27.coeffs_ref
  54.7 0.5 evaluate.3
  55.3 25.0 %all_to_all.5.got_ref = bf16[128,16,256]{2,1,0:T(8,128)(2,1)S(1)} all-to-all(bf16[128,16,256]{2,1,0:T(8,128)(2,1)S(1)} %evaluate.3), channel_id=1, replica_groups={{0,1,2,3,64,65,66,67,4,5,6,7,68,69,70,71,8,9,10,11,72,73,74,75,12,13,14..., dimensions={0} | all-to-all | bytes 2097152 | tf_op jit(solution)/shard_map/all_to_all | solution.py:308
  80.3 1.6 %place.1 = bf16[16,32768]{1,0:T(8,128)(2,1)} custom-call(s32[128]{0:T(128)S(1)} %copy-done.1, bf16[128,16,256]{2,1,0:T(8,128)(2,1)S(1)} %all_to_all.5.got_ref), custom_call_target="tpu_custom_call" | custom-call | tf_op jit(solution)/shard_map/place/pallas_call | solution.py:239
  (17 shorter events, 0.2 us)
Async XLA Ops:
  0.0 0.7 copy-start.2
  4.0 5.9 %collective-permute-start.1 = (bf16[8,64,128]{2,1,0:T(8,128)(2,1)S(1)}, bf16[8,64,128]{2,1,0:T(8,128)(2,1)S(1)}, u32[]{:S(2)}, u32[]{:S(2)}) collective-permute-start(bf16[8,64,128]{2,1,0:T(8,128)(2,1)S(1)} %get-tuple-element.16.own_ref), channel_id=1, source_target_pairs={{0,1},{1,0},{2,3},{3,2},{4,5},{5,4},{6,7},{7,6},{8,9},{9,8},{10,11... | collective-permute-start | bytes 393224 | tf_op jit(solution)/shard_map/ppermute | solution.py:260
  8.2 5.6 %collective-permute-start = (bf16[8,64,128]{2,1,0:T(8,128)(2,1)S(1)}, bf16[8,64,128]{2,1,0:T(8,128)(2,1)S(1)}, u32[]{:S(2)}, u32[]{:S(2)}) collective-permute-start(bf16[8,64,128]{2,1,0:T(8,128)(2,1)S(1)} %get-tuple-element.15.rest_0_.rest_1_.own_ref), channel_id=1, source_target_pairs={{0,1},{1,0},{2,3},{3,2},{4,5},{5,4},{6,7},{7,6},{8,9},{9,8},{10,11... | collective-permute-start | bytes 393224 | tf_op jit(solution)/shard_map/ppermute | solution.py:260
  10.3 8.2 %collective-permute-start.3 = (bf16[8,64,128]{2,1,0:T(8,128)(2,1)S(1)}, bf16[8,64,128]{2,1,0:T(8,128)(2,1)S(1)}, u32[]{:S(2)}, u32[]{:S(2)}) collective-permute-start(bf16[8,64,128]{2,1,0:T(8,128)(2,1)S(1)} %level.14.rest_1_.own_ref), channel_id=1, source_target_pairs={{0,2},{1,3},{2,0},{3,1},{4,6},{5,7},{6,4},{7,5},{8,10},{9,11},{10,... | collective-permute-start | bytes 393224 | tf_op jit(solution)/shard_map/ppermute | solution.py:260
  14.3 7.5 %collective-permute-start.2 = (bf16[8,64,128]{2,1,0:T(8,128)(2,1)S(1)}, bf16[8,64,128]{2,1,0:T(8,128)(2,1)S(1)}, u32[]{:S(2)}, u32[]{:S(2)}) collective-permute-start(bf16[8,64,128]{2,1,0:T(8,128)(2,1)S(1)} %level.15.rest_0_.rest_1_.own_ref), channel_id=1, source_target_pairs={{0,2},{1,3},{2,0},{3,1},{4,6},{5,7},{6,4},{7,5},{8,10},{9,11},{10,... | collective-permute-start | bytes 393224 | tf_op jit(solution)/shard_map/ppermute | solution.py:260
  18.9 7.2 %collective-permute-start.5 = (bf16[8,64,128]{2,1,0:T(8,128)(2,1)S(1)}, bf16[8,64,128]{2,1,0:T(8,128)(2,1)S(1)}, u32[]{:S(2)}, u32[]{:S(2)}) collective-permute-start(bf16[8,64,128]{2,1,0:T(8,128)(2,1)S(1)} %level.16.rest_1_.own_ref), channel_id=1, source_target_pairs={{0,4},{1,5},{2,6},{3,7},{4,0},{5,1},{6,2},{7,3},{8,12},{9,13},{10,... | collective-permute-start | bytes 393224 | tf_op jit(solution)/shard_map/ppermute | solution.py:260
  22.2 6.4 %collective-permute-start.4 = (bf16[8,64,128]{2,1,0:T(8,128)(2,1)S(1)}, bf16[8,64,128]{2,1,0:T(8,128)(2,1)S(1)}, u32[]{:S(2)}, u32[]{:S(2)}) collective-permute-start(bf16[8,64,128]{2,1,0:T(8,128)(2,1)S(1)} %level.17.rest_0_.rest_1_.own_ref), channel_id=1, source_target_pairs={{0,4},{1,5},{2,6},{3,7},{4,0},{5,1},{6,2},{7,3},{8,12},{9,13},{10,... | collective-permute-start | bytes 393224 | tf_op jit(solution)/shard_map/ppermute | solution.py:260
  26.5 6.1 %collective-permute-start.7 = (bf16[8,64,128]{2,1,0:T(8,128)(2,1)S(1)}, bf16[8,64,128]{2,1,0:T(8,128)(2,1)S(1)}, u32[]{:S(2)}, u32[]{:S(2)}) collective-permute-start(bf16[8,64,128]{2,1,0:T(8,128)(2,1)S(1)} %level.18.rest_1_.own_ref), channel_id=1, source_target_pairs={{0,8},{8,0},{16,24},{24,16},{1,9},{9,1},{17,25},{25,17},{2,10},{10... | collective-permute-start | bytes 393224 | tf_op jit(solution)/shard_map/ppermute | solution.py:260
  29.0 6.8 %collective-permute-start.6 = (bf16[8,64,128]{2,1,0:T(8,128)(2,1)S(1)}, bf16[8,64,128]{2,1,0:T(8,128)(2,1)S(1)}, u32[]{:S(2)}, u32[]{:S(2)}) collective-permute-start(bf16[8,64,128]{2,1,0:T(8,128)(2,1)S(1)} %level.19.rest_0_.rest_1_.own_ref), channel_id=1, source_target_pairs={{0,8},{8,0},{16,24},{24,16},{1,9},{9,1},{17,25},{25,17},{2,10},{10... | collective-permute-start | bytes 393224 | tf_op jit(solution)/shard_map/ppermute | solution.py:260
  33.1 6.6 %collective-permute-start.9 = (bf16[8,64,128]{2,1,0:T(8,128)(2,1)S(1)}, bf16[8,64,128]{2,1,0:T(8,128)(2,1)S(1)}, u32[]{:S(2)}, u32[]{:S(2)}) collective-permute-start(bf16[8,64,128]{2,1,0:T(8,128)(2,1)S(1)} %level.20.rest_1_.own_ref), channel_id=1, source_target_pairs={{0,16},{8,24},{16,0},{24,8},{1,17},{9,25},{17,1},{25,9},{2,18},{10... | collective-permute-start | bytes 393224 | tf_op jit(solution)/shard_map/ppermute | solution.py:260
  36.2 10.5 %collective-permute-start.8 = (bf16[8,64,128]{2,1,0:T(8,128)(2,1)S(1)}, bf16[8,64,128]{2,1,0:T(8,128)(2,1)S(1)}, u32[]{:S(2)}, u32[]{:S(2)}) collective-permute-start(bf16[8,64,128]{2,1,0:T(8,128)(2,1)S(1)} %level.21.rest_1_.own_ref), channel_id=1, source_target_pairs={{0,16},{8,24},{16,0},{24,8},{1,17},{9,25},{17,1},{25,9},{2,18},{10... | collective-permute-start | bytes 393224 | tf_op jit(solution)/shard_map/ppermute | solution.py:260
  40.2 5.0 %collective-permute-start.11 = (bf16[4,64,128]{2,1,0:T(8,128)(2,1)S(1)}, bf16[4,64,128]{2,1,0:T(8,128)(2,1)S(1)}, u32[]{:S(2)}, u32[]{:S(2)}) collective-permute-start(bf16[4,64,128]{2,1,0:T(8,128)(2,1)S(1)} %get-tuple-element.23), channel_id=1, source_target_pairs={{0,32},{32,0},{64,96},{96,64},{1,33},{33,1},{65,97},{97,65},{2,34}... | collective-permute-start | bytes 196616 | tf_op jit(solution)/shard_map/ppermute | solution.py:260
  44.2 1.3 %collective-permute-start.10 = (bf16[4,64,128]{2,1,0:T(8,128)(2,1)S(1)}, bf16[4,64,128]{2,1,0:T(8,128)(2,1)S(1)}, u32[]{:S(2)}, u32[]{:S(2)}) collective-permute-start(bf16[4,64,128]{2,1,0:T(8,128)(2,1)S(1)} %get-tuple-element.24), channel_id=1, source_target_pairs={{0,32},{32,0},{64,96},{96,64},{1,33},{33,1},{65,97},{97,65},{2,34}... | collective-permute-start | bytes 196616 | tf_op jit(solution)/shard_map/ppermute | solution.py:260
  45.9 5.9 %collective-permute-start.15 = (bf16[8,64,128]{2,1,0:T(8,128)(2,1)S(1)}, bf16[8,64,128]{2,1,0:T(8,128)(2,1)S(1)}, u32[]{:S(2)}, u32[]{:S(2)}) collective-permute-start(bf16[8,64,128]{2,1,0:T(8,128)(2,1)S(1)} %level.23.rest_1_.own_ref), channel_id=1, source_target_pairs={{0,64},{32,96},{64,0},{96,32},{1,65},{33,97},{65,1},{97,33},{2,66}... | collective-permute-start | bytes 393224 | tf_op jit(solution)/shard_map/ppermute | solution.py:260
  46.6 3.5 %copy-start = (bf16[128,64,256]{2,1,0:T(8,128)(2,1)S(1)}, bf16[128,64,256]{2,1,0:T(8,128)(2,1)}, u32[]{:S(2)}) copy-start(bf16[128,64,256]{2,1,0:T(8,128)(2,1)} %rest_0_.1) | copy-start | bytes 12582916
  47.1 1.4 %collective-permute-start.13 = (bf16[4,64,128]{2,1,0:T(8,128)(2,1)S(1)}, bf16[4,64,128]{2,1,0:T(8,128)(2,1)S(1)}, u32[]{:S(2)}, u32[]{:S(2)}) collective-permute-start(bf16[4,64,128]{2,1,0:T(8,128)(2,1)S(1)} %get-tuple-element.21), channel_id=1, source_target_pairs={{0,32},{32,0},{64,96},{96,64},{1,33},{33,1},{65,97},{97,65},{2,34}... | collective-permute-start | bytes 196616 | tf_op jit(solution)/shard_map/ppermute | solution.py:260
  47.6 1.3 %collective-permute-start.12 = (bf16[4,64,128]{2,1,0:T(8,128)(2,1)S(1)}, bf16[4,64,128]{2,1,0:T(8,128)(2,1)S(1)}, u32[]{:S(2)}, u32[]{:S(2)}) collective-permute-start(bf16[4,64,128]{2,1,0:T(8,128)(2,1)S(1)} %get-tuple-element.22), channel_id=1, source_target_pairs={{0,32},{32,0},{64,96},{96,64},{1,33},{33,1},{65,97},{97,65},{2,34}... | collective-permute-start | bytes 196616 | tf_op jit(solution)/shard_map/ppermute | solution.py:260
  49.3 5.0 %collective-permute-start.14 = (bf16[8,64,128]{2,1,0:T(8,128)(2,1)S(1)}, bf16[8,64,128]{2,1,0:T(8,128)(2,1)S(1)}, u32[]{:S(2)}, u32[]{:S(2)}) collective-permute-start(bf16[8,64,128]{2,1,0:T(8,128)(2,1)S(1)} %level.25.rest_1_.own_ref), channel_id=1, source_target_pairs={{0,64},{32,96},{64,0},{96,32},{1,65},{33,97},{65,1},{97,33},{2,66}... | collective-permute-start | bytes 393224 | tf_op jit(solution)/shard_map/ppermute | solution.py:260
  55.2 25.0 %copy-start.1 = (s32[128]{0:T(128)S(1)}, s32[128]{0:T(128)}, u32[]{:S(2)}) copy-start(s32[128]{0:T(128)} %slot_ref.1) | copy-start | bytes 1540

commit v5 on v4

--- a/solution.py
+++ b/solution.py
@@ -160,40 +160,43 @@
     )(table, own, *fars, *after)
 
 
-def eval_body(first, place_of, coeffs_ref, eval_ref, *rest):
+def last_body(first, place_of, table_ref, own_ref, far_ref, eval_ref, *rest):
     out_ref = rest[-1]
-    _, rank, span = eval_ref.shape
-    groups, _, lanes = coeffs_ref.shape
+    _, rank, both = table_ref.shape
+    span = eval_ref.shape[2]
+    groups, _, lanes = own_ref.shape
     rhs = lanes // PACK
     for grp in range(groups):
-        mine = coeffs_ref[grp].astype(jnp.float32)
+        at = (first + grp) * PACK
+        block = table_ref[at : at + PACK].reshape(PACK * rank, both)
+        pair = jnp.concatenate([own_ref[grp], far_ref[grp]], axis=0)
+        wide = jnp.dot(block, pair, preferred_element_type=jnp.float32)
+        mine = pick(wide, rank, rhs).astype(jnp.bfloat16).astype(jnp.float32)
         twice = jnp.concatenate([mine, mine], axis=0).T.astype(jnp.bfloat16)
         left = jnp.concatenate([twice] * (PACK // 2), axis=1)
         row_box = lax.broadcasted_iota(jnp.int32, left.shape, 0) // rhs
         col_box = lax.broadcasted_iota(jnp.int32, left.shape, 1) // rank
         left = jnp.where(row_box == col_box, left, jnp.zeros_like(left))
-        at = (first + grp) * PACK
         block = eval_ref[at : at + PACK].reshape(PACK * rank, span)
         vals = jnp.dot(left, block, preferred_element_type=jnp.float32)
         for box in range(PACK):
-            mine = vals[box * rhs : (box + 1) * rhs]
-            out_ref[place_of[at + box]] = mine.astype(jnp.bfloat16)
-
-
-def eval_call(first, place_of, coeffs, evaluate, *before):
-    groups, rank, lanes = coeffs.shape
+            own = vals[box * rhs : (box + 1) * rhs]
+            out_ref[place_of[at + box]] = own.astype(jnp.bfloat16)
+
+
+def last_call(first, place_of, table, own, far, evaluate, *before):
     boxes, _, span = evaluate.shape
-    rhs = lanes // PACK
-    return pl.pallas_call(
-        functools.partial(eval_body, first, place_of),
-        in_specs=[pl.BlockSpec(memory_space=pltpu.VMEM)] * (2 + len(before)),
+    rhs = own.shape[2] // PACK
+    return pl.pallas_call(
+        functools.partial(last_body, first, place_of),
+        in_specs=[pl.BlockSpec(memory_space=pltpu.VMEM)] * (4 + len(before)),
         out_specs=pl.BlockSpec(memory_space=pltpu.VMEM),
         out_shape=jax.ShapeDtypeStruct((boxes, rhs, span), jnp.bfloat16),
-        input_output_aliases={2: 0} if before else {},
+        input_output_aliases={4: 0} if before else {},
         compiler_params=pltpu.CompilerParams(vmem_limit_bytes=VMEM_LIMIT),
         cost_estimate=EVALUATE_COST,
-        name="evaluate",
-    )(coeffs, evaluate, *before)
+        name="last",
+    )(table, own, far, evaluate, *before)
 
 
 def bits_by_shift():
@@ -233,7 +236,7 @@
 
 
 def place_call(slot, got):
-    pieces = 4
+    pieces = 8
     boxes, rhs, span = got.shape
     shape = (rhs, boxes * span)
     return pl.pallas_call(
@@ -278,6 +281,10 @@
         for axis in ("gz", "gy", "gx")
         for bit_pos in range(lax.axis_size(axis).bit_length() - 1)
     ]
+    devices = np.arange(int(np.prod(SPLIT))).reshape(SPLIT).transpose(ORDER).reshape(-1)
+    group = [int(device) for device in devices]
+    place_of = [int(at) for at in np.argsort(devices)]
+    values = ()
     tables = {}
     *held, coeffs[-1] = load_call(range(EARLY), translate, [], coeffs[-1], True)
     last = coeffs[-1]
@@ -296,15 +303,14 @@
         parts = CORE_PARTS if steps[level] == CORE_STEP else 1
         pieces = jnp.split(coeffs[i], parts) if parts > 1 else [coeffs[i]]
         fars = [from_partner(piece, axis, bit_pos) for piece in pieces]
+        if level == len(steps) - 1:
+            values = (
+                last_call(firsts[i], place_of, held[level], coeffs[i], fars[0], evaluate, *values),
+            )
+            continue
         last = coeffs[i] = level_call(
             firsts[i], held[level], coeffs[i], fars, last, *tables[level]
         )
-    devices = np.arange(int(np.prod(SPLIT))).reshape(SPLIT).transpose(ORDER).reshape(-1)
-    group = [int(device) for device in devices]
-    place_of = [int(at) for at in np.argsort(devices)]
-    values = ()
-    for i, first in enumerate(firsts):
-        values = (eval_call(first, place_of, coeffs[i], evaluate, *values),)
     moved = lax.all_to_all(
         values[0], AXES, split_axis=0, concat_axis=0, axis_index_groups=[group], tiled=True
     )

time: 82.2 us -> 82.2 us (level)
    pallas_call x2, Pallas kernels: 0.98 us -> 1.83 us  [last_call(): pl.pallas_call(functools.partial(last_body, first, place_of), in_specs=[p...]
    pallas_call x14 -> x12, Pallas kernels: 5.85 us -> 5.01 us  [level_call(): pl.pallas_call(functools.partial(level_body, first, len(fars)), in_specs=...]
where the time goes in v5:
time: 82.2 us; the launch traced here: 81.9 us
  starting transfers between devices  25.8 us (31%)
  blocking collectives  25 us (30%)
  Pallas kernels  22.1 us (27%)
  waiting for transfers between devices  8.08 us (10%)
    ppermute x16, starting transfers between devices, from_partner(): return lax.ppermute(value, axis, pairs)  25.8 us
    all_to_all x1, blocking collectives, local(): lax.all_to_all(values[0], AXES, split_axis=0, concat_axis=0, axis_index_g...  25 us
    pallas_call x6, Pallas kernels, load_call(): pl.pallas_call(functools.partial(load_body, levels, len(whole)), in_specs...  10.2 us
    ppermute x16, waiting for transfers between devices, from_partner(): return lax.ppermute(value, axis, pairs)  8.08 us
    pallas_call x12, Pallas kernels, level_call(): pl.pallas_call(functools.partial(level_body, first, len(fars)), in_specs=...  5.01 us
    pallas_call x1, Pallas kernels, interp_call(): pl.pallas_call(functools.partial(interp_body, firsts), in_specs=[pl.Block...  3.37 us
    pallas_call x2, Pallas kernels, last_call(): pl.pallas_call(functools.partial(last_body, first, place_of), in_specs=[p...  1.83 us
  transfers between devices with their start and end apart: 16, of which 8 were waited for; matrix products, arithmetic and copies ran while one was open for 0% of the time, Pallas kernels for 20%

profile of v5, /device:TPU:1, one launch (start us, length us, event | category | flops | bytes accessed | tf_op | source)
XLA Modules:
  0.0 81.9 jit_solution(9033904644740572974)
XLA Ops:
  0.0 0.7 copy-done.2
  0.7 3.4 %interp.1 = (bf16[8,64,128]{2,1,0:T(8,128)(2,1)S(1)}, bf16[8,64,128]{2,1,0:T(8,128)(2,1)S(1)}) custom-call(s32[128]{0:T(128)S(1)} %copy-done.2, bf16[16,32768]{1,0:T(8,128)(2,1)} %src_hbm.1, bf16[128,64,256]{2,1,0:T(8,128)(2,1)} %interp_hbm.1), custom_call_target="tpu_custom_call" | custom-call | tf_op jit(solution)/shard_map/interp/pallas_call | solution.py:80
  4.0 2.6 %collective-permute-start.1 = (bf16[8,64,128]{2,1,0:T(8,128)(2,1)S(1)}, bf16[8,64,128]{2,1,0:T(8,128)(2,1)S(1)}, u32[]{:S(2)}, u32[]{:S(2)}) collective-permute-start(bf16[8,64,128]{2,1,0:T(8,128)(2,1)S(1)} %get-tuple-element.16.own_ref), channel_id=1, source_target_pairs={{0,1},{1,0},{2,3},{3,2},{4,5},{5,4},{6,7},{7,6},{8,9},{9,8},{10,11... | collective-permute-start | bytes 393224 | tf_op jit(solution)/shard_map/ppermute | solution.py:263
  6.6 1.6 %load.6 = (bf16[128,64,128]{2,1,0:T(8,128)(2,1)S(1)}, bf16[8,64,128]{2,1,0:T(8,128)(2,1)S(1)}) custom-call(bf16[7,128,64,128]{3,2,1,0:T(8,128)(2,1)} %table_hbm.11, bf16[8,64,128]{2,1,0:T(8,128)(2,1)S(1)} %get-tuple-element.13.rest_0_), custom_call_target="tpu_custom_call", output_to_operand_aliasing={{1}: (1, {})} | custom-call | tf_op jit(solution)/shard_map/load/pallas_call | solution.py:121
  8.2 0.1 collective-permute-start
  8.3 1.6 %load.7.rest_2_.table_ref = bf16[128,64,128]{2,1,0:T(8,128)(2,1)S(1)} custom-call(bf16[7,128,64,128]{3,2,1,0:T(8,128)(2,1)} %table_hbm.11, bf16[8,64,128]{2,1,0:T(8,128)(2,1)S(1)} %get-tuple-element.15.rest_0_.rest_1_.own_ref), custom_call_target="tpu_custom_call" | custom-call | tf_op jit(solution)/shard_map/load/pallas_call | solution.py:121
  9.9 0.4 level.12.rest_1_.own_ref
  10.3 3.5 %collective-permute-start.3 = (bf16[8,64,128]{2,1,0:T(8,128)(2,1)S(1)}, bf16[8,64,128]{2,1,0:T(8,128)(2,1)S(1)}, u32[]{:S(2)}, u32[]{:S(2)}) collective-permute-start(bf16[8,64,128]{2,1,0:T(8,128)(2,1)S(1)} %level.12.rest_1_.own_ref), channel_id=1, source_target_pairs={{0,2},{1,3},{2,0},{3,1},{4,6},{5,7},{6,4},{7,5},{8,10},{9,11},{10,... | collective-permute-start | bytes 393224 | tf_op jit(solution)/shard_map/ppermute | solution.py:263
  13.8 0.4 level.13.rest_0_.rest_1_.own_ref
  14.3 1.6 %collective-permute-start.2 = (bf16[8,64,128]{2,1,0:T(8,128)(2,1)S(1)}, bf16[8,64,128]{2,1,0:T(8,128)(2,1)S(1)}, u32[]{:S(2)}, u32[]{:S(2)}) collective-permute-start(bf16[8,64,128]{2,1,0:T(8,128)(2,1)S(1)} %level.13.rest_0_.rest_1_.own_ref), channel_id=1, source_target_pairs={{0,2},{1,3},{2,0},{3,1},{4,6},{5,7},{6,4},{7,5},{8,10},{9,11},{10,... | collective-permute-start | bytes 393224 | tf_op jit(solution)/shard_map/ppermute | solution.py:263
  15.9 1.6 %load.8.rest_2_.table_ref = bf16[128,64,128]{2,1,0:T(8,128)(2,1)S(1)} custom-call(bf16[7,128,64,128]{3,2,1,0:T(8,128)(2,1)} %table_hbm.11, bf16[8,64,128]{2,1,0:T(8,128)(2,1)S(1)} %level.13.rest_0_.rest_1_.own_ref), custom_call_target="tpu_custom_call" | custom-call | tf_op jit(solution)/shard_map/load/pallas_call | solution.py:121
  17.5 1.0 %collective-permute-done.3.rest_0_ = bf16[8,64,128]{2,1,0:T(8,128)(2,1)S(1)} collective-permute-done((bf16[8,64,128]{2,1,0:T(8,128)(2,1)S(1)}, bf16[8,64,128]{2,1,0:T(8,128)(2,1)S(1)}, u32[]{:S(2)}, u32[]{:S(2)}) %collective-permute-start.3) | collective-permute-done | bytes 131104 | tf_op jit(solution)/shard_map/ppermute | solution.py:263
  18.5 0.4 level.14.rest_1_.own_ref
  18.9 2.8 %collective-permute-start.5 = (bf16[8,64,128]{2,1,0:T(8,128)(2,1)S(1)}, bf16[8,64,128]{2,1,0:T(8,128)(2,1)S(1)}, u32[]{:S(2)}, u32[]{:S(2)}) collective-permute-start(bf16[8,64,128]{2,1,0:T(8,128)(2,1)S(1)} %level.14.rest_1_.own_ref), channel_id=1, source_target_pairs={{0,4},{1,5},{2,6},{3,7},{4,0},{5,1},{6,2},{7,3},{8,12},{9,13},{10,... | collective-permute-start | bytes 393224 | tf_op jit(solution)/shard_map/ppermute | solution.py:263
  21.8 0.4 level.15.rest_0_.rest_1_.own_ref
  22.2 2.3 %collective-permute-start.4 = (bf16[8,64,128]{2,1,0:T(8,128)(2,1)S(1)}, bf16[8,64,128]{2,1,0:T(8,128)(2,1)S(1)}, u32[]{:S(2)}, u32[]{:S(2)}) collective-permute-start(bf16[8,64,128]{2,1,0:T(8,128)(2,1)S(1)} %level.15.rest_0_.rest_1_.own_ref), channel_id=1, source_target_pairs={{0,4},{1,5},{2,6},{3,7},{4,0},{5,1},{6,2},{7,3},{8,12},{9,13},{10,... | collective-permute-start | bytes 393224 | tf_op jit(solution)/shard_map/ppermute | solution.py:263
  24.5 1.6 %load.9.rest_2_.table_ref = bf16[128,64,128]{2,1,0:T(8,128)(2,1)S(1)} custom-call(bf16[7,128,64,128]{3,2,1,0:T(8,128)(2,1)} %table_hbm.11, bf16[8,64,128]{2,1,0:T(8,128)(2,1)S(1)} %level.15.rest_0_.rest_1_.own_ref), custom_call_target="tpu_custom_call" | custom-call | tf_op jit(solution)/shard_map/load/pallas_call | solution.py:121
  26.1 0.4 level.16.rest_1_.own_ref
  26.5 1.4 %collective-permute-start.7 = (bf16[8,64,128]{2,1,0:T(8,128)(2,1)S(1)}, bf16[8,64,128]{2,1,0:T(8,128)(2,1)S(1)}, u32[]{:S(2)}, u32[]{:S(2)}) collective-permute-start(bf16[8,64,128]{2,1,0:T(8,128)(2,1)S(1)} %level.16.rest_1_.own_ref), channel_id=1, source_target_pairs={{0,8},{8,0},{16,24},{24,16},{1,9},{9,1},{17,25},{25,17},{2,10},{10... | collective-permute-start | bytes 393224 | tf_op jit(solution)/shard_map/ppermute | solution.py:263
  27.9 0.7 collective-permute-done.4.rest_0_
  28.6 0.4 level.17.rest_0_.rest_1_.own_ref
  29.0 1.4 %collective-permute-start.6 = (bf16[8,64,128]{2,1,0:T(8,128)(2,1)S(1)}, bf16[8,64,128]{2,1,0:T(8,128)(2,1)S(1)}, u32[]{:S(2)}, u32[]{:S(2)}) collective-permute-start(bf16[8,64,128]{2,1,0:T(8,128)(2,1)S(1)} %level.17.rest_0_.rest_1_.own_ref), channel_id=1, source_target_pairs={{0,8},{8,0},{16,24},{24,16},{1,9},{9,1},{17,25},{25,17},{2,10},{10... | collective-permute-start | bytes 393224 | tf_op jit(solution)/shard_map/ppermute | solution.py:263
  30.4 2.2 %load.10 = (bf16[128,64,128]{2,1,0:T(8,128)(2,1)S(1)}, bf16[128,64,128]{2,1,0:T(8,128)(2,1)S(1)}) custom-call(bf16[7,128,64,128]{3,2,1,0:T(8,128)(2,1)} %table_hbm.11, bf16[8,64,128]{2,1,0:T(8,128)(2,1)S(1)} %level.17.rest_0_.rest_1_.own_ref), custom_call_target="tpu_custom_call" | custom-call | tf_op jit(solution)/shard_map/load/pallas_call | solution.py:121
  32.6 0.4 level.18.rest_1_.own_ref
  33.1 2.7 %collective-permute-start.9 = (bf16[8,64,128]{2,1,0:T(8,128)(2,1)S(1)}, bf16[8,64,128]{2,1,0:T(8,128)(2,1)S(1)}, u32[]{:S(2)}, u32[]{:S(2)}) collective-permute-start(bf16[8,64,128]{2,1,0:T(8,128)(2,1)S(1)} %level.18.rest_1_.own_ref), channel_id=1, source_target_pairs={{0,16},{8,24},{16,0},{24,8},{1,17},{9,25},{17,1},{25,9},{2,18},{10... | collective-permute-start | bytes 393224 | tf_op jit(solution)/shard_map/ppermute | solution.py:263
  35.8 0.4 level.19.rest_1_.own_ref
  36.2 1.0 %collective-permute-start.8 = (bf16[8,64,128]{2,1,0:T(8,128)(2,1)S(1)}, bf16[8,64,128]{2,1,0:T(8,128)(2,1)S(1)}, u32[]{:S(2)}, u32[]{:S(2)}) collective-permute-start(bf16[8,64,128]{2,1,0:T(8,128)(2,1)S(1)} %level.19.rest_1_.own_ref), channel_id=1, source_target_pairs={{0,16},{8,24},{16,0},{24,8},{1,17},{9,25},{17,1},{25,9},{2,18},{10... | collective-permute-start | bytes 393224 | tf_op jit(solution)/shard_map/ppermute | solution.py:263
  37.2 2.5 %collective-permute-done.9.rest_0_ = bf16[8,64,128]{2,1,0:T(8,128)(2,1)S(1)} collective-permute-done((bf16[8,64,128]{2,1,0:T(8,128)(2,1)S(1)}, bf16[8,64,128]{2,1,0:T(8,128)(2,1)S(1)}, u32[]{:S(2)}, u32[]{:S(2)}) %collective-permute-start.9) | collective-permute-done | bytes 131104 | tf_op jit(solution)/shard_map/ppermute | solution.py:263
  39.7 0.4 level.20.own_ref.rest_2_
  40.1 4.1 %collective-permute-start.11 = (bf16[4,64,128]{2,1,0:T(8,128)(2,1)S(1)}, bf16[4,64,128]{2,1,0:T(8,128)(2,1)S(1)}, u32[]{:S(2)}, u32[]{:S(2)}) collective-permute-start(bf16[4,64,128]{2,1,0:T(8,128)(2,1)S(1)} %get-tuple-element.23), channel_id=1, source_target_pairs={{0,32},{32,0},{64,96},{96,64},{1,33},{33,1},{65,97},{97,65},{2,34}... | collective-permute-start | bytes 196616 | tf_op jit(solution)/shard_map/ppermute | solution.py:263
  44.2 0.1 collective-permute-start.10
  44.3 0.8 collective-permute-done.11.rest_1_
  45.1 0.4 collective-permute-done.10.rest_0_
  45.5 0.4 level.21.rest_1_.own_ref
  45.9 0.8 collective-permute-start.15
  46.7 0.4 level.22.own_ref.rest_2_
  47.1 0.5 collective-permute-start.13
  47.6 0.1 collective-permute-start.12
  47.7 0.8 collective-permute-done.13.rest_1_
  48.5 0.4 collective-permute-done.12.rest_0_
  48.9 0.4 level.23.rest_1_.own_ref
  49.3 0.9 %collective-permute-start.14 = (bf16[8,64,128]{2,1,0:T(8,128)(2,1)S(1)}, bf16[8,64,128]{2,1,0:T(8,128)(2,1)S(1)}, u32[]{:S(2)}, u32[]{:S(2)}) collective-permute-start(bf16[8,64,128]{2,1,0:T(8,128)(2,1)S(1)} %level.23.rest_1_.own_ref), channel_id=1, source_target_pairs={{0,64},{32,96},{64,0},{96,32},{1,65},{33,97},{65,1},{97,33},{2,66}... | collective-permute-start | bytes 393224 | tf_op jit(solution)/shard_map/ppermute | solution.py:263
  50.2 1.6 %load.11 = (bf16[128,64,128]{2,1,0:T(8,128)(2,1)S(1)}, bf16[128,64,256]{2,1,0:T(8,128)(2,1)S(1)}) custom-call(bf16[7,128,64,128]{3,2,1,0:T(8,128)(2,1)} %table_hbm.11, bf16[128,64,256]{2,1,0:T(8,128)(2,1)S(1)} %copy-done, bf16[8,64,128]{2,1,0:T(8,128)(2,1)S(1)} %level.23.rest_1_.own_ref), custom_call_target="tpu_custom_call" | custom-call | tf_op jit(solution)/shard_map/load/pallas_call | solution.py:121
  51.8 0.9 %last.2.rest_0_ = bf16[128,16,256]{2,1,0:T(8,128)(2,1)S(1)} custom-call(bf16[128,64,128]{2,1,0:T(8,128)(2,1)S(1)} %get-tuple-element.19.table_ref, bf16[8,64,128]{2,1,0:T(8,128)(2,1)S(1)} %level.21.rest_1_.own_ref, bf16[8,64,128]{2,1,0:T(8,128)(2,1)S(1)} %collective-permute-done.15.far_ref, bf16[128,64,256]{2,1,0:T(8,128)(2,1)S(1)} %get-tuple-element.20.eval_ref), custom_call_target="tpu_custom_call" | custom-call | flops 1000000000 | tf_op jit(solution)/shard_map/last/pallas_call | solution.py:190
  52.7 1.6 %collective-permute-done.14.far_ref = bf16[8,64,128]{2,1,0:T(8,128)(2,1)S(1)} collective-permute-done((bf16[8,64,128]{2,1,0:T(8,128)(2,1)S(1)}, bf16[8,64,128]{2,1,0:T(8,128)(2,1)S(1)}, u32[]{:S(2)}, u32[]{:S(2)}) %collective-permute-start.14) | collective-permute-done | bytes 131104 | tf_op jit(solution)/shard_map/ppermute | solution.py:263
  54.3 0.9 %last.3 = bf16[128,16,256]{2,1,0:T(8,128)(2,1)S(1)} custom-call(bf16[128,64,128]{2,1,0:T(8,128)(2,1)S(1)} %get-tuple-element.19.table_ref, bf16[8,64,128]{2,1,0:T(8,128)(2,1)S(1)} %level.23.rest_1_.own_ref, bf16[8,64,128]{2,1,0:T(8,128)(2,1)S(1)} %collective-permute-done.14.far_ref, ...), custom_call_target="tpu_custom_call", output_to_operand_aliasing={{}: (4, {})} | custom-call | flops 1000000000 | tf_op jit(solution)/shard_map/last/pallas_call | solution.py:190
  55.3 25.0 %all_to_all.5.got_ref = bf16[128,16,256]{2,1,0:T(8,128)(2,1)S(1)} all-to-all(bf16[128,16,256]{2,1,0:T(8,128)(2,1)S(1)} %last.3), channel_id=1, replica_groups={{0,1,2,3,64,65,66,67,4,5,6,7,68,69,70,71,8,9,10,11,72,73,74,75,12,13,14..., dimensions={0} | all-to-all | bytes 2097152 | tf_op jit(solution)/shard_map/all_to_all | solution.py:314
  80.3 1.6 %place.1 = bf16[16,32768]{1,0:T(8,128)(2,1)} custom-call(s32[128]{0:T(128)S(1)} %copy-done.1, bf16[128,16,256]{2,1,0:T(8,128)(2,1)S(1)} %all_to_all.5.got_ref), custom_call_target="tpu_custom_call" | custom-call | tf_op jit(solution)/shard_map/place/pallas_call | solution.py:242
  (15 shorter events, 0.1 us)
Async XLA Ops:
  0.0 0.7 copy-start.2
  4.0 5.9 %collective-permute-start.1 = (bf16[8,64,128]{2,1,0:T(8,128)(2,1)S(1)}, bf16[8,64,128]{2,1,0:T(8,128)(2,1)S(1)}, u32[]{:S(2)}, u32[]{:S(2)}) collective-permute-start(bf16[8,64,128]{2,1,0:T(8,128)(2,1)S(1)} %get-tuple-element.16.own_ref), channel_id=1, source_target_pairs={{0,1},{1,0},{2,3},{3,2},{4,5},{5,4},{6,7},{7,6},{8,9},{9,8},{10,11... | collective-permute-start | bytes 393224 | tf_op jit(solution)/shard_map/ppermute | solution.py:263
  8.2 5.6 %collective-permute-start = (bf16[8,64,128]{2,1,0:T(8,128)(2,1)S(1)}, bf16[8,64,128]{2,1,0:T(8,128)(2,1)S(1)}, u32[]{:S(2)}, u32[]{:S(2)}) collective-permute-start(bf16[8,64,128]{2,1,0:T(8,128)(2,1)S(1)} %get-tuple-element.15.rest_0_.rest_1_.own_ref), channel_id=1, source_target_pairs={{0,1},{1,0},{2,3},{3,2},{4,5},{5,4},{6,7},{7,6},{8,9},{9,8},{10,11... | collective-permute-start | bytes 393224 | tf_op jit(solution)/shard_map/ppermute | solution.py:263
  10.3 8.2 %collective-permute-start.3 = (bf16[8,64,128]{2,1,0:T(8,128)(2,1)S(1)}, bf16[8,64,128]{2,1,0:T(8,128)(2,1)S(1)}, u32[]{:S(2)}, u32[]{:S(2)}) collective-permute-start(bf16[8,64,128]{2,1,0:T(8,128)(2,1)S(1)} %level.12.rest_1_.own_ref), channel_id=1, source_target_pairs={{0,2},{1,3},{2,0},{3,1},{4,6},{5,7},{6,4},{7,5},{8,10},{9,11},{10,... | collective-permute-start | bytes 393224 | tf_op jit(solution)/shard_map/ppermute | solution.py:263
  14.3 7.5 %collective-permute-start.2 = (bf16[8,64,128]{2,1,0:T(8,128)(2,1)S(1)}, bf16[8,64,128]{2,1,0:T(8,128)(2,1)S(1)}, u32[]{:S(2)}, u32[]{:S(2)}) collective-permute-start(bf16[8,64,128]{2,1,0:T(8,128)(2,1)S(1)} %level.13.rest_0_.rest_1_.own_ref), channel_id=1, source_target_pairs={{0,2},{1,3},{2,0},{3,1},{4,6},{5,7},{6,4},{7,5},{8,10},{9,11},{10,... | collective-permute-start | bytes 393224 | tf_op jit(solution)/shard_map/ppermute | solution.py:263
  18.9 7.2 %collective-permute-start.5 = (bf16[8,64,128]{2,1,0:T(8,128)(2,1)S(1)}, bf16[8,64,128]{2,1,0:T(8,128)(2,1)S(1)}, u32[]{:S(2)}, u32[]{:S(2)}) collective-permute-start(bf16[8,64,128]{2,1,0:T(8,128)(2,1)S(1)} %level.14.rest_1_.own_ref), channel_id=1, source_target_pairs={{0,4},{1,5},{2,6},{3,7},{4,0},{5,1},{6,2},{7,3},{8,12},{9,13},{10,... | collective-permute-start | bytes 393224 | tf_op jit(solution)/shard_map/ppermute | solution.py:263
  22.2 6.4 %collective-permute-start.4 = (bf16[8,64,128]{2,1,0:T(8,128)(2,1)S(1)}, bf16[8,64,128]{2,1,0:T(8,128)(2,1)S(1)}, u32[]{:S(2)}, u32[]{:S(2)}) collective-permute-start(bf16[8,64,128]{2,1,0:T(8,128)(2,1)S(1)} %level.15.rest_0_.rest_1_.own_ref), channel_id=1, source_target_pairs={{0,4},{1,5},{2,6},{3,7},{4,0},{5,1},{6,2},{7,3},{8,12},{9,13},{10,... | collective-permute-start | bytes 393224 | tf_op jit(solution)/shard_map/ppermute | solution.py:263
  26.5 6.1 %collective-permute-start.7 = (bf16[8,64,128]{2,1,0:T(8,128)(2,1)S(1)}, bf16[8,64,128]{2,1,0:T(8,128)(2,1)S(1)}, u32[]{:S(2)}, u32[]{:S(2)}) collective-permute-start(bf16[8,64,128]{2,1,0:T(8,128)(2,1)S(1)} %level.16.rest_1_.own_ref), channel_id=1, source_target_pairs={{0,8},{8,0},{16,24},{24,16},{1,9},{9,1},{17,25},{25,17},{2,10},{10... | collective-permute-start | bytes 393224 | tf_op jit(solution)/shard_map/ppermute | solution.py:263
  29.0 6.8 %collective-permute-start.6 = (bf16[8,64,128]{2,1,0:T(8,128)(2,1)S(1)}, bf16[8,64,128]{2,1,0:T(8,128)(2,1)S(1)}, u32[]{:S(2)}, u32[]{:S(2)}) collective-permute-start(bf16[8,64,128]{2,1,0:T(8,128)(2,1)S(1)} %level.17.rest_0_.rest_1_.own_ref), channel_id=1, source_target_pairs={{0,8},{8,0},{16,24},{24,16},{1,9},{9,1},{17,25},{25,17},{2,10},{10... | collective-permute-start | bytes 393224 | tf_op jit(solution)/shard_map/ppermute | solution.py:263
  33.1 6.6 %collective-permute-start.9 = (bf16[8,64,128]{2,1,0:T(8,128)(2,1)S(1)}, bf16[8,64,128]{2,1,0:T(8,128)(2,1)S(1)}, u32[]{:S(2)}, u32[]{:S(2)}) collective-permute-start(bf16[8,64,128]{2,1,0:T(8,128)(2,1)S(1)} %level.18.rest_1_.own_ref), channel_id=1, source_target_pairs={{0,16},{8,24},{16,0},{24,8},{1,17},{9,25},{17,1},{25,9},{2,18},{10... | collective-permute-start | bytes 393224 | tf_op jit(solution)/shard_map/ppermute | solution.py:263
  36.2 10.5 %collective-permute-start.8 = (bf16[8,64,128]{2,1,0:T(8,128)(2,1)S(1)}, bf16[8,64,128]{2,1,0:T(8,128)(2,1)S(1)}, u32[]{:S(2)}, u32[]{:S(2)}) collective-permute-start(bf16[8,64,128]{2,1,0:T(8,128)(2,1)S(1)} %level.19.rest_1_.own_ref), channel_id=1, source_target_pairs={{0,16},{8,24},{16,0},{24,8},{1,17},{9,25},{17,1},{25,9},{2,18},{10... | collective-permute-start | bytes 393224 | tf_op jit(solution)/shard_map/ppermute | solution.py:263
  40.1 5.0 %collective-permute-start.11 = (bf16[4,64,128]{2,1,0:T(8,128)(2,1)S(1)}, bf16[4,64,128]{2,1,0:T(8,128)(2,1)S(1)}, u32[]{:S(2)}, u32[]{:S(2)}) collective-permute-start(bf16[4,64,128]{2,1,0:T(8,128)(2,1)S(1)} %get-tuple-element.23), channel_id=1, source_target_pairs={{0,32},{32,0},{64,96},{96,64},{1,33},{33,1},{65,97},{97,65},{2,34}... | collective-permute-start | bytes 196616 | tf_op jit(solution)/shard_map/ppermute | solution.py:263
  44.2 1.3 %collective-permute-start.10 = (bf16[4,64,128]{2,1,0:T(8,128)(2,1)S(1)}, bf16[4,64,128]{2,1,0:T(8,128)(2,1)S(1)}, u32[]{:S(2)}, u32[]{:S(2)}) collective-permute-start(bf16[4,64,128]{2,1,0:T(8,128)(2,1)S(1)} %get-tuple-element.24), channel_id=1, source_target_pairs={{0,32},{32,0},{64,96},{96,64},{1,33},{33,1},{65,97},{97,65},{2,34}... | collective-permute-start | bytes 196616 | tf_op jit(solution)/shard_map/ppermute | solution.py:263
  45.9 5.9 %collective-permute-start.15 = (bf16[8,64,128]{2,1,0:T(8,128)(2,1)S(1)}, bf16[8,64,128]{2,1,0:T(8,128)(2,1)S(1)}, u32[]{:S(2)}, u32[]{:S(2)}) collective-permute-start(bf16[8,64,128]{2,1,0:T(8,128)(2,1)S(1)} %level.21.rest_1_.own_ref), channel_id=1, source_target_pairs={{0,64},{32,96},{64,0},{96,32},{1,65},{33,97},{65,1},{97,33},{2,66}... | collective-permute-start | bytes 393224 | tf_op jit(solution)/shard_map/ppermute | solution.py:263
  46.7 3.5 %copy-start = (bf16[128,64,256]{2,1,0:T(8,128)(2,1)S(1)}, bf16[128,64,256]{2,1,0:T(8,128)(2,1)}, u32[]{:S(2)}) copy-start(bf16[128,64,256]{2,1,0:T(8,128)(2,1)} %rest_0_.1) | copy-start | bytes 12582916
  47.1 1.4 %collective-permute-start.13 = (bf16[4,64,128]{2,1,0:T(8,128)(2,1)S(1)}, bf16[4,64,128]{2,1,0:T(8,128)(2,1)S(1)}, u32[]{:S(2)}, u32[]{:S(2)}) collective-permute-start(bf16[4,64,128]{2,1,0:T(8,128)(2,1)S(1)} %get-tuple-element.21), channel_id=1, source_target_pairs={{0,32},{32,0},{64,96},{96,64},{1,33},{33,1},{65,97},{97,65},{2,34}... | collective-permute-start | bytes 196616 | tf_op jit(solution)/shard_map/ppermute | solution.py:263
  47.6 1.3 %collective-permute-start.12 = (bf16[4,64,128]{2,1,0:T(8,128)(2,1)S(1)}, bf16[4,64,128]{2,1,0:T(8,128)(2,1)S(1)}, u32[]{:S(2)}, u32[]{:S(2)}) collective-permute-start(bf16[4,64,128]{2,1,0:T(8,128)(2,1)S(1)} %get-tuple-element.22), channel_id=1, source_target_pairs={{0,32},{32,0},{64,96},{96,64},{1,33},{33,1},{65,97},{97,65},{2,34}... | collective-permute-start | bytes 196616 | tf_op jit(solution)/shard_map/ppermute | solution.py:263
  49.3 5.0 %collective-permute-start.14 = (bf16[8,64,128]{2,1,0:T(8,128)(2,1)S(1)}, bf16[8,64,128]{2,1,0:T(8,128)(2,1)S(1)}, u32[]{:S(2)}, u32[]{:S(2)}) collective-permute-start(bf16[8,64,128]{2,1,0:T(8,128)(2,1)S(1)} %level.23.rest_1_.own_ref), channel_id=1, source_target_pairs={{0,64},{32,96},{64,0},{96,32},{1,65},{33,97},{65,1},{97,33},{2,66}... | collective-permute-start | bytes 393224 | tf_op jit(solution)/shard_map/ppermute | solution.py:263
  55.3 25.0 %copy-start.1 = (s32[128]{0:T(128)S(1)}, s32[128]{0:T(128)}, u32[]{:S(2)}) copy-start(s32[128]{0:T(128)} %slot_ref.1) | copy-start | bytes 1540

commit v6 on v5

--- a/solution.py
+++ b/solution.py
@@ -294,11 +294,8 @@
             more = ()
             if level in LOADS:
                 levels = range(len(held), len(held) + LOADS[level])
-                final = level == len(steps) - 1
-                more = load_call(levels, translate, [evaluate] * final, coeffs[-1])
+                more = load_call(levels, translate, [], coeffs[-1])
                 held += more[: len(levels)]
-                if final:
-                    evaluate = more[-1]
             tables[level] = more[:1]
         parts = CORE_PARTS if steps[level] == CORE_STEP else 1
         pieces = jnp.split(coeffs[i], parts) if parts > 1 else [coeffs[i]]

time: 82.2 us -> 83.7 us (1.018)
  waiting for transfers between devices: 8.08 us -> 5.15 us
  starting transfers between devices: 25.8 us -> 28.5 us
  local copies, waits for them, and re-layouts: 0.69 us -> 1.73 us
    ppermute x16, waiting for transfers between devices: 8.08 us -> 5.15 us  [from_partner(): return lax.ppermute(value, axis, pairs)]
    ppermute x16, starting transfers between devices: 25.8 us -> 28.5 us  [from_partner(): return lax.ppermute(value, axis, pairs)]
    unnamed x6, local copies, waits for them, and re-layouts: 0.66 us -> 1.71 us
where the time goes in v6:
time: 83.7 us; the launch traced here: 83.5 us
  starting transfers between devices  28.5 us (34%)
  blocking collectives  25.6 us (31%)
  Pallas kernels  22.2 us (27%)
  waiting for transfers between devices  5.15 us (6%)
  local copies, waits for them, and re-layouts  1.73 us (2%)
    ppermute x16, starting transfers between devices, from_partner(): return lax.ppermute(value, axis, pairs)  28.5 us
    all_to_all x1, blocking collectives, local(): lax.all_to_all(values[0], AXES, split_axis=0, concat_axis=0, axis_index_g...  25.6 us
    pallas_call x6, Pallas kernels, load_call(): pl.pallas_call(functools.partial(load_body, levels, len(whole)), in_specs...  10.4 us
    ppermute x16, waiting for transfers between devices, from_partner(): return lax.ppermute(value, axis, pairs)  5.15 us
    pallas_call x12, Pallas kernels, level_call(): pl.pallas_call(functools.partial(level_body, first, len(fars)), in_specs=...  5.01 us
    pallas_call x1, Pallas kernels, interp_call(): pl.pallas_call(functools.partial(interp_body, firsts), in_specs=[pl.Block...  3.38 us
    pallas_call x2, Pallas kernels, last_call(): pl.pallas_call(functools.partial(last_body, first, place_of), in_specs=[p...  1.83 us
    unnamed x6, local copies, waits for them, and re-layouts  1.71 us
  transfers between devices with their start and end apart: 16, of which 8 were waited for; matrix products, arithmetic and copies ran while one was open for 0% of the time, Pallas kernels for 20%

profile of v6, /device:TPU:1, one launch (start us, length us, event | category | flops | bytes accessed | tf_op | source)
XLA Modules:
  0.0 83.5 jit_solution(10759119652854598014)
XLA Ops:
  0.0 0.7 copy-done.2
  0.7 3.4 %interp.1 = (bf16[8,64,128]{2,1,0:T(8,128)(2,1)S(1)}, bf16[8,64,128]{2,1,0:T(8,128)(2,1)S(1)}) custom-call(s32[128]{0:T(128)S(1)} %copy-done.2, bf16[16,32768]{1,0:T(8,128)(2,1)} %src_hbm.1, bf16[128,64,256]{2,1,0:T(8,128)(2,1)} %interp_hbm.1), custom_call_target="tpu_custom_call" | custom-call | tf_op jit(solution)/shard_map/interp/pallas_call | solution.py:80
  4.0 2.5 %collective-permute-start.1 = (bf16[8,64,128]{2,1,0:T(8,128)(2,1)S(1)}, bf16[8,64,128]{2,1,0:T(8,128)(2,1)S(1)}, u32[]{:S(2)}, u32[]{:S(2)}) collective-permute-start(bf16[8,64,128]{2,1,0:T(8,128)(2,1)S(1)} %get-tuple-element.14.own_ref), channel_id=1, source_target_pairs={{0,1},{1,0},{2,3},{3,2},{4,5},{5,4},{6,7},{7,6},{8,9},{9,8},{10,11... | collective-permute-start | bytes 393224 | tf_op jit(solution)/shard_map/ppermute | solution.py:263
  6.6 1.6 %load.6 = (bf16[128,64,128]{2,1,0:T(8,128)(2,1)S(1)}, bf16[8,64,128]{2,1,0:T(8,128)(2,1)S(1)}) custom-call(bf16[7,128,64,128]{3,2,1,0:T(8,128)(2,1)} %table_hbm.11, bf16[8,64,128]{2,1,0:T(8,128)(2,1)S(1)} %get-tuple-element.11.rest_0_), custom_call_target="tpu_custom_call", output_to_operand_aliasing={{1}: (1, {})} | custom-call | tf_op jit(solution)/shard_map/load/pallas_call | solution.py:121
  8.2 0.1 collective-permute-start
  8.3 1.6 %load.7.rest_2_.table_ref = bf16[128,64,128]{2,1,0:T(8,128)(2,1)S(1)} custom-call(bf16[7,128,64,128]{3,2,1,0:T(8,128)(2,1)} %table_hbm.11, bf16[8,64,128]{2,1,0:T(8,128)(2,1)S(1)} %get-tuple-element.13.rest_0_.rest_1_.own_ref), custom_call_target="tpu_custom_call" | custom-call | tf_op jit(solution)/shard_map/load/pallas_call | solution.py:121
  9.9 0.4 level.12.rest_1_.own_ref
  10.3 3.5 %collective-permute-start.3 = (bf16[8,64,128]{2,1,0:T(8,128)(2,1)S(1)}, bf16[8,64,128]{2,1,0:T(8,128)(2,1)S(1)}, u32[]{:S(2)}, u32[]{:S(2)}) collective-permute-start(bf16[8,64,128]{2,1,0:T(8,128)(2,1)S(1)} %level.12.rest_1_.own_ref), channel_id=1, source_target_pairs={{0,2},{1,3},{2,0},{3,1},{4,6},{5,7},{6,4},{7,5},{8,10},{9,11},{10,... | collective-permute-start | bytes 393224 | tf_op jit(solution)/shard_map/ppermute | solution.py:263
  13.8 0.4 level.13.rest_0_.rest_1_.own_ref
  14.3 1.6 %collective-permute-start.2 = (bf16[8,64,128]{2,1,0:T(8,128)(2,1)S(1)}, bf16[8,64,128]{2,1,0:T(8,128)(2,1)S(1)}, u32[]{:S(2)}, u32[]{:S(2)}) collective-permute-start(bf16[8,64,128]{2,1,0:T(8,128)(2,1)S(1)} %level.13.rest_0_.rest_1_.own_ref), channel_id=1, source_target_pairs={{0,2},{1,3},{2,0},{3,1},{4,6},{5,7},{6,4},{7,5},{8,10},{9,11},{10,... | collective-permute-start | bytes 393224 | tf_op jit(solution)/shard_map/ppermute | solution.py:263
  15.9 1.6 %load.8.rest_2_.table_ref = bf16[128,64,128]{2,1,0:T(8,128)(2,1)S(1)} custom-call(bf16[7,128,64,128]{3,2,1,0:T(8,128)(2,1)} %table_hbm.11, bf16[8,64,128]{2,1,0:T(8,128)(2,1)S(1)} %level.13.rest_0_.rest_1_.own_ref), custom_call_target="tpu_custom_call" | custom-call | tf_op jit(solution)/shard_map/load/pallas_call | solution.py:121
  17.5 1.0 %collective-permute-done.3.rest_0_ = bf16[8,64,128]{2,1,0:T(8,128)(2,1)S(1)} collective-permute-done((bf16[8,64,128]{2,1,0:T(8,128)(2,1)S(1)}, bf16[8,64,128]{2,1,0:T(8,128)(2,1)S(1)}, u32[]{:S(2)}, u32[]{:S(2)}) %collective-permute-start.3) | collective-permute-done | bytes 131104 | tf_op jit(solution)/shard_map/ppermute | solution.py:263
  18.5 0.4 level.14.rest_1_.own_ref
  18.9 2.8 %collective-permute-start.5 = (bf16[8,64,128]{2,1,0:T(8,128)(2,1)S(1)}, bf16[8,64,128]{2,1,0:T(8,128)(2,1)S(1)}, u32[]{:S(2)}, u32[]{:S(2)}) collective-permute-start(bf16[8,64,128]{2,1,0:T(8,128)(2,1)S(1)} %level.14.rest_1_.own_ref), channel_id=1, source_target_pairs={{0,4},{1,5},{2,6},{3,7},{4,0},{5,1},{6,2},{7,3},{8,12},{9,13},{10,... | collective-permute-start | bytes 393224 | tf_op jit(solution)/shard_map/ppermute | solution.py:263
  21.8 0.4 level.15.rest_0_.rest_1_.own_ref
  22.2 2.3 %collective-permute-start.4 = (bf16[8,64,128]{2,1,0:T(8,128)(2,1)S(1)}, bf16[8,64,128]{2,1,0:T(8,128)(2,1)S(1)}, u32[]{:S(2)}, u32[]{:S(2)}) collective-permute-start(bf16[8,64,128]{2,1,0:T(8,128)(2,1)S(1)} %level.15.rest_0_.rest_1_.own_ref), channel_id=1, source_target_pairs={{0,4},{1,5},{2,6},{3,7},{4,0},{5,1},{6,2},{7,3},{8,12},{9,13},{10,... | collective-permute-start | bytes 393224 | tf_op jit(solution)/shard_map/ppermute | solution.py:263
  24.5 1.6 %load.9.rest_2_.table_ref = bf16[128,64,128]{2,1,0:T(8,128)(2,1)S(1)} custom-call(bf16[7,128,64,128]{3,2,1,0:T(8,128)(2,1)} %table_hbm.11, bf16[8,64,128]{2,1,0:T(8,128)(2,1)S(1)} %level.15.rest_0_.rest_1_.own_ref), custom_call_target="tpu_custom_call" | custom-call | tf_op jit(solution)/shard_map/load/pallas_call | solution.py:121
  26.1 0.4 level.16.rest_1_.own_ref
  26.5 1.4 %collective-permute-start.7 = (bf16[8,64,128]{2,1,0:T(8,128)(2,1)S(1)}, bf16[8,64,128]{2,1,0:T(8,128)(2,1)S(1)}, u32[]{:S(2)}, u32[]{:S(2)}) collective-permute-start(bf16[8,64,128]{2,1,0:T(8,128)(2,1)S(1)} %level.16.rest_1_.own_ref), channel_id=1, source_target_pairs={{0,8},{8,0},{16,24},{24,16},{1,9},{9,1},{17,25},{25,17},{2,10},{10... | collective-permute-start | bytes 393224 | tf_op jit(solution)/shard_map/ppermute | solution.py:263
  27.9 0.7 collective-permute-done.4.rest_0_
  28.6 0.4 level.17.rest_0_.rest_1_.own_ref
  29.0 2.2 %load.10 = (bf16[128,64,128]{2,1,0:T(8,128)(2,1)S(1)}, bf16[128,64,128]{2,1,0:T(8,128)(2,1)S(1)}) custom-call(bf16[7,128,64,128]{3,2,1,0:T(8,128)(2,1)} %table_hbm.11, bf16[8,64,128]{2,1,0:T(8,128)(2,1)S(1)} %level.17.rest_0_.rest_1_.own_ref), custom_call_target="tpu_custom_call" | custom-call | tf_op jit(solution)/shard_map/load/pallas_call | solution.py:121
  31.3 1.4 %collective-permute-start.6 = (bf16[8,64,128]{2,1,0:T(8,128)(2,1)S(1)}, bf16[8,64,128]{2,1,0:T(8,128)(2,1)S(1)}, u32[]{:S(2)}, u32[]{:S(2)}) collective-permute-start(bf16[8,64,128]{2,1,0:T(8,128)(2,1)S(1)} %level.17.rest_0_.rest_1_.own_ref), channel_id=1, source_target_pairs={{0,8},{8,0},{16,24},{24,16},{1,9},{9,1},{17,25},{25,17},{2,10},{10... | collective-permute-start | bytes 393224 | tf_op jit(solution)/shard_map/ppermute | solution.py:263
  32.6 0.4 level.18.rest_1_.own_ref
  33.1 2.7 %collective-permute-start.9 = (bf16[8,64,128]{2,1,0:T(8,128)(2,1)S(1)}, bf16[8,64,128]{2,1,0:T(8,128)(2,1)S(1)}, u32[]{:S(2)}, u32[]{:S(2)}) collective-permute-start(bf16[8,64,128]{2,1,0:T(8,128)(2,1)S(1)} %level.18.rest_1_.own_ref), channel_id=1, source_target_pairs={{0,16},{8,24},{16,0},{24,8},{1,17},{9,25},{17,1},{25,9},{2,18},{10... | collective-permute-start | bytes 393224 | tf_op jit(solution)/shard_map/ppermute | solution.py:263
  35.8 0.4 level.19.rest_1_.own_ref
  36.2 2.4 %collective-permute-start.8 = (bf16[8,64,128]{2,1,0:T(8,128)(2,1)S(1)}, bf16[8,64,128]{2,1,0:T(8,128)(2,1)S(1)}, u32[]{:S(2)}, u32[]{:S(2)}) collective-permute-start(bf16[8,64,128]{2,1,0:T(8,128)(2,1)S(1)} %level.19.rest_1_.own_ref), channel_id=1, source_target_pairs={{0,16},{8,24},{16,0},{24,8},{1,17},{9,25},{17,1},{25,9},{2,18},{10... | collective-permute-start | bytes 393224 | tf_op jit(solution)/shard_map/ppermute | solution.py:263
  38.6 0.4 collective-permute-done.9.rest_0_
  39.0 0.4 level.20.own_ref.rest_2_
  39.5 5.4 %collective-permute-start.10 = (bf16[4,64,128]{2,1,0:T(8,128)(2,1)S(1)}, bf16[4,64,128]{2,1,0:T(8,128)(2,1)S(1)}, u32[]{:S(2)}, u32[]{:S(2)}) collective-permute-start(bf16[4,64,128]{2,1,0:T(8,128)(2,1)S(1)} %get-tuple-element.20), channel_id=1, source_target_pairs={{0,32},{32,0},{64,96},{96,64},{1,33},{33,1},{65,97},{97,65},{2,34}... | collective-permute-start | bytes 196616 | tf_op jit(solution)/shard_map/ppermute | solution.py:263
  44.9 0.1 collective-permute-start.11
  45.0 0.8 collective-permute-done.10.rest_0_
  45.8 0.4 collective-permute-done.11.rest_1_
  46.2 0.4 level.21.rest_1_.own_ref
  46.6 1.0 %collective-permute-start.15 = (bf16[8,64,128]{2,1,0:T(8,128)(2,1)S(1)}, bf16[8,64,128]{2,1,0:T(8,128)(2,1)S(1)}, u32[]{:S(2)}, u32[]{:S(2)}) collective-permute-start(bf16[8,64,128]{2,1,0:T(8,128)(2,1)S(1)} %level.21.rest_1_.own_ref), channel_id=1, source_target_pairs={{0,64},{32,96},{64,0},{96,32},{1,65},{33,97},{65,1},{97,33},{2,66}... | collective-permute-start | bytes 393224 | tf_op jit(solution)/shard_map/ppermute | solution.py:263
  47.6 0.4 level.22.own_ref.rest_2_
  48.0 0.5 collective-permute-start.12
  48.7 0.8 collective-permute-done.12.rest_0_
  49.5 0.4 collective-permute-done.13.rest_1_
  49.8 0.4 level.23.rest_0_.own_ref
  50.2 0.6 collective-permute-start.14
  50.8 1.7 %load.11.table_ref = bf16[128,64,128]{2,1,0:T(8,128)(2,1)S(1)} custom-call(bf16[7,128,64,128]{3,2,1,0:T(8,128)(2,1)} %table_hbm.11, bf16[8,64,128]{2,1,0:T(8,128)(2,1)S(1)} %level.23.rest_0_.own_ref), custom_call_target="tpu_custom_call" | custom-call | tf_op jit(solution)/shard_map/load/pallas_call | solution.py:121
  52.6 1.0 %copy-done = bf16[128,64,256]{2,1,0:T(8,128)(2,1)S(1)} copy-done((bf16[128,64,256]{2,1,0:T(8,128)(2,1)S(1)}, bf16[128,64,256]{2,1,0:T(8,128)(2,1)}, u32[]{:S(2)}) %copy-start) | copy-done | bytes 4194328
  53.7 0.9 %last.2.rest_0_ = bf16[128,16,256]{2,1,0:T(8,128)(2,1)S(1)} custom-call(bf16[128,64,128]{2,1,0:T(8,128)(2,1)S(1)} %load.11.table_ref, bf16[8,64,128]{2,1,0:T(8,128)(2,1)S(1)} %level.21.rest_1_.own_ref, bf16[8,64,128]{2,1,0:T(8,128)(2,1)S(1)} %collective-permute-done.15.far_ref, bf16[128,64,256]{2,1,0:T(8,128)(2,1)S(1)} %copy-done), custom_call_target="tpu_custom_call" | custom-call | flops 1000000000 | tf_op jit(solution)/shard_map/last/pallas_call | solution.py:190
  54.6 0.7 collective-permute-done.14.far_ref
  55.3 0.9 %last.3 = bf16[128,16,256]{2,1,0:T(8,128)(2,1)S(1)} custom-call(bf16[128,64,128]{2,1,0:T(8,128)(2,1)S(1)} %load.11.table_ref, bf16[8,64,128]{2,1,0:T(8,128)(2,1)S(1)} %level.23.rest_0_.own_ref, bf16[8,64,128]{2,1,0:T(8,128)(2,1)S(1)} %collective-permute-done.14.far_ref, bf16[128,64,256]{2,1,0:T(8,128)(2,1)S(1)} %copy-done, ...), custom_call_target="tpu_custom_call", output_to_operand_aliasing={{}: (4, {})} | custom-call | flops 1000000000 | tf_op jit(solution)/shard_map/last/pallas_call | solution.py:190
  56.2 25.6 %all_to_all.5.got_ref = bf16[128,16,256]{2,1,0:T(8,128)(2,1)S(1)} all-to-all(bf16[128,16,256]{2,1,0:T(8,128)(2,1)S(1)} %last.3), channel_id=1, replica_groups={{0,1,2,3,64,65,66,67,4,5,6,7,68,69,70,71,8,9,10,11,72,73,74,75,12,13,14..., dimensions={0} | all-to-all | bytes 2097152 | tf_op jit(solution)/shard_map/all_to_all | solution.py:311
  81.9 1.6 %place.1 = bf16[16,32768]{1,0:T(8,128)(2,1)} custom-call(s32[128]{0:T(128)S(1)} %copy-done.1, bf16[128,16,256]{2,1,0:T(8,128)(2,1)S(1)} %all_to_all.5.got_ref), custom_call_target="tpu_custom_call" | custom-call | tf_op jit(solution)/shard_map/place/pallas_call | solution.py:242
  (15 shorter events, 0.1 us)
Async XLA Ops:
  0.0 0.7 copy-start.2
  4.0 5.9 %collective-permute-start.1 = (bf16[8,64,128]{2,1,0:T(8,128)(2,1)S(1)}, bf16[8,64,128]{2,1,0:T(8,128)(2,1)S(1)}, u32[]{:S(2)}, u32[]{:S(2)}) collective-permute-start(bf16[8,64,128]{2,1,0:T(8,128)(2,1)S(1)} %get-tuple-element.14.own_ref), channel_id=1, source_target_pairs={{0,1},{1,0},{2,3},{3,2},{4,5},{5,4},{6,7},{7,6},{8,9},{9,8},{10,11... | collective-permute-start | bytes 393224 | tf_op jit(solution)/shard_map/ppermute | solution.py:263
  8.2 5.6 %collective-permute-start = (bf16[8,64,128]{2,1,0:T(8,128)(2,1)S(1)}, bf16[8,64,128]{2,1,0:T(8,128)(2,1)S(1)}, u32[]{:S(2)}, u32[]{:S(2)}) collective-permute-start(bf16[8,64,128]{2,1,0:T(8,128)(2,1)S(1)} %get-tuple-element.13.rest_0_.rest_1_.own_ref), channel_id=1, source_target_pairs={{0,1},{1,0},{2,3},{3,2},{4,5},{5,4},{6,7},{7,6},{8,9},{9,8},{10,11... | collective-permute-start | bytes 393224 | tf_op jit(solution)/shard_map/ppermute | solution.py:263
  10.3 8.2 %collective-permute-start.3 = (bf16[8,64,128]{2,1,0:T(8,128)(2,1)S(1)}, bf16[8,64,128]{2,1,0:T(8,128)(2,1)S(1)}, u32[]{:S(2)}, u32[]{:S(2)}) collective-permute-start(bf16[8,64,128]{2,1,0:T(8,128)(2,1)S(1)} %level.12.rest_1_.own_ref), channel_id=1, source_target_pairs={{0,2},{1,3},{2,0},{3,1},{4,6},{5,7},{6,4},{7,5},{8,10},{9,11},{10,... | collective-permute-start | bytes 393224 | tf_op jit(solution)/shard_map/ppermute | solution.py:263
  14.3 7.5 %collective-permute-start.2 = (bf16[8,64,128]{2,1,0:T(8,128)(2,1)S(1)}, bf16[8,64,128]{2,1,0:T(8,128)(2,1)S(1)}, u32[]{:S(2)}, u32[]{:S(2)}) collective-permute-start(bf16[8,64,128]{2,1,0:T(8,128)(2,1)S(1)} %level.13.rest_0_.rest_1_.own_ref), channel_id=1, source_target_pairs={{0,2},{1,3},{2,0},{3,1},{4,6},{5,7},{6,4},{7,5},{8,10},{9,11},{10,... | collective-permute-start | bytes 393224 | tf_op jit(solution)/shard_map/ppermute | solution.py:263
  18.9 7.2 %collective-permute-start.5 = (bf16[8,64,128]{2,1,0:T(8,128)(2,1)S(1)}, bf16[8,64,128]{2,1,0:T(8,128)(2,1)S(1)}, u32[]{:S(2)}, u32[]{:S(2)}) collective-permute-start(bf16[8,64,128]{2,1,0:T(8,128)(2,1)S(1)} %level.14.rest_1_.own_ref), channel_id=1, source_target_pairs={{0,4},{1,5},{2,6},{3,7},{4,0},{5,1},{6,2},{7,3},{8,12},{9,13},{10,... | collective-permute-start | bytes 393224 | tf_op jit(solution)/shard_map/ppermute | solution.py:263
  22.2 6.4 %collective-permute-start.4 = (bf16[8,64,128]{2,1,0:T(8,128)(2,1)S(1)}, bf16[8,64,128]{2,1,0:T(8,128)(2,1)S(1)}, u32[]{:S(2)}, u32[]{:S(2)}) collective-permute-start(bf16[8,64,128]{2,1,0:T(8,128)(2,1)S(1)} %level.15.rest_0_.rest_1_.own_ref), channel_id=1, source_target_pairs={{0,4},{1,5},{2,6},{3,7},{4,0},{5,1},{6,2},{7,3},{8,12},{9,13},{10,... | collective-permute-start | bytes 393224 | tf_op jit(solution)/shard_map/ppermute | solution.py:263
  26.5 6.1 %collective-permute-start.7 = (bf16[8,64,128]{2,1,0:T(8,128)(2,1)S(1)}, bf16[8,64,128]{2,1,0:T(8,128)(2,1)S(1)}, u32[]{:S(2)}, u32[]{:S(2)}) collective-permute-start(bf16[8,64,128]{2,1,0:T(8,128)(2,1)S(1)} %level.16.rest_1_.own_ref), channel_id=1, source_target_pairs={{0,8},{8,0},{16,24},{24,16},{1,9},{9,1},{17,25},{25,17},{2,10},{10... | collective-permute-start | bytes 393224 | tf_op jit(solution)/shard_map/ppermute | solution.py:263
  31.3 4.5 %collective-permute-start.6 = (bf16[8,64,128]{2,1,0:T(8,128)(2,1)S(1)}, bf16[8,64,128]{2,1,0:T(8,128)(2,1)S(1)}, u32[]{:S(2)}, u32[]{:S(2)}) collective-permute-start(bf16[8,64,128]{2,1,0:T(8,128)(2,1)S(1)} %level.17.rest_0_.rest_1_.own_ref), channel_id=1, source_target_pairs={{0,8},{8,0},{16,24},{24,16},{1,9},{9,1},{17,25},{25,17},{2,10},{10... | collective-permute-start | bytes 393224 | tf_op jit(solution)/shard_map/ppermute | solution.py:263
  33.1 5.9 %collective-permute-start.9 = (bf16[8,64,128]{2,1,0:T(8,128)(2,1)S(1)}, bf16[8,64,128]{2,1,0:T(8,128)(2,1)S(1)}, u32[]{:S(2)}, u32[]{:S(2)}) collective-permute-start(bf16[8,64,128]{2,1,0:T(8,128)(2,1)S(1)} %level.18.rest_1_.own_ref), channel_id=1, source_target_pairs={{0,16},{8,24},{16,0},{24,8},{1,17},{9,25},{17,1},{25,9},{2,18},{10... | collective-permute-start | bytes 393224 | tf_op jit(solution)/shard_map/ppermute | solution.py:263
  36.2 11.4 %collective-permute-start.8 = (bf16[8,64,128]{2,1,0:T(8,128)(2,1)S(1)}, bf16[8,64,128]{2,1,0:T(8,128)(2,1)S(1)}, u32[]{:S(2)}, u32[]{:S(2)}) collective-permute-start(bf16[8,64,128]{2,1,0:T(8,128)(2,1)S(1)} %level.19.rest_1_.own_ref), channel_id=1, source_target_pairs={{0,16},{8,24},{16,0},{24,8},{1,17},{9,25},{17,1},{25,9},{2,18},{10... | collective-permute-start | bytes 393224 | tf_op jit(solution)/shard_map/ppermute | solution.py:263
  39.5 6.3 %collective-permute-start.10 = (bf16[4,64,128]{2,1,0:T(8,128)(2,1)S(1)}, bf16[4,64,128]{2,1,0:T(8,128)(2,1)S(1)}, u32[]{:S(2)}, u32[]{:S(2)}) collective-permute-start(bf16[4,64,128]{2,1,0:T(8,128)(2,1)S(1)} %get-tuple-element.20), channel_id=1, source_target_pairs={{0,32},{32,0},{64,96},{96,64},{1,33},{33,1},{65,97},{97,65},{2,34}... | collective-permute-start | bytes 196616 | tf_op jit(solution)/shard_map/ppermute | solution.py:263
  44.9 1.3 %collective-permute-start.11 = (bf16[4,64,128]{2,1,0:T(8,128)(2,1)S(1)}, bf16[4,64,128]{2,1,0:T(8,128)(2,1)S(1)}, u32[]{:S(2)}, u32[]{:S(2)}) collective-permute-start(bf16[4,64,128]{2,1,0:T(8,128)(2,1)S(1)} %get-tuple-element.19), channel_id=1, source_target_pairs={{0,32},{32,0},{64,96},{96,64},{1,33},{33,1},{65,97},{97,65},{2,34}... | collective-permute-start | bytes 196616 | tf_op jit(solution)/shard_map/ppermute | solution.py:263
  46.6 6.0 %collective-permute-start.15 = (bf16[8,64,128]{2,1,0:T(8,128)(2,1)S(1)}, bf16[8,64,128]{2,1,0:T(8,128)(2,1)S(1)}, u32[]{:S(2)}, u32[]{:S(2)}) collective-permute-start(bf16[8,64,128]{2,1,0:T(8,128)(2,1)S(1)} %level.21.rest_1_.own_ref), channel_id=1, source_target_pairs={{0,64},{32,96},{64,0},{96,32},{1,65},{33,97},{65,1},{97,33},{2,66}... | collective-permute-start | bytes 393224 | tf_op jit(solution)/shard_map/ppermute | solution.py:263
  48.0 1.4 %collective-permute-start.12 = (bf16[4,64,128]{2,1,0:T(8,128)(2,1)S(1)}, bf16[4,64,128]{2,1,0:T(8,128)(2,1)S(1)}, u32[]{:S(2)}, u32[]{:S(2)}) collective-permute-start(bf16[4,64,128]{2,1,0:T(8,128)(2,1)S(1)} %get-tuple-element.18), channel_id=1, source_target_pairs={{0,32},{32,0},{64,96},{96,64},{1,33},{33,1},{65,97},{97,65},{2,34}... | collective-permute-start | bytes 196616 | tf_op jit(solution)/shard_map/ppermute | solution.py:263
  48.6 1.3 %collective-permute-start.13 = (bf16[4,64,128]{2,1,0:T(8,128)(2,1)S(1)}, bf16[4,64,128]{2,1,0:T(8,128)(2,1)S(1)}, u32[]{:S(2)}, u32[]{:S(2)}) collective-permute-start(bf16[4,64,128]{2,1,0:T(8,128)(2,1)S(1)} %get-tuple-element.17), channel_id=1, source_target_pairs={{0,32},{32,0},{64,96},{96,64},{1,33},{33,1},{65,97},{97,65},{2,34}... | collective-permute-start | bytes 196616 | tf_op jit(solution)/shard_map/ppermute | solution.py:263
  50.2 5.0 %collective-permute-start.14 = (bf16[8,64,128]{2,1,0:T(8,128)(2,1)S(1)}, bf16[8,64,128]{2,1,0:T(8,128)(2,1)S(1)}, u32[]{:S(2)}, u32[]{:S(2)}) collective-permute-start(bf16[8,64,128]{2,1,0:T(8,128)(2,1)S(1)} %level.23.rest_0_.own_ref), channel_id=1, source_target_pairs={{0,64},{32,96},{64,0},{96,32},{1,65},{33,97},{65,1},{97,33},{2,66}... | collective-permute-start | bytes 393224 | tf_op jit(solution)/shard_map/ppermute | solution.py:263
  50.8 2.8 %copy-start = (bf16[128,64,256]{2,1,0:T(8,128)(2,1)S(1)}, bf16[128,64,256]{2,1,0:T(8,128)(2,1)}, u32[]{:S(2)}) copy-start(bf16[128,64,256]{2,1,0:T(8,128)(2,1)} %eval_ref.3) | copy-start | bytes 12582916
  56.2 25.7 %copy-start.1 = (s32[128]{0:T(128)S(1)}, s32[128]{0:T(128)}, u32[]{:S(2)}) copy-start(s32[128]{0:T(128)} %slot_ref.1) | copy-start | bytes 1540
